TPU v7x, 128 devices: a whole 4x4x4 slice. The times are simulated.
128 devices in a mesh: lat: 8 (over x, core), lon: 16 (over z, y).
Axes of the slice: x: 4, y: 4, z: 4, core: 2. Of those that a mesh axis runs over, the one named last changes fastest.
Arguments:
- field: bfloat16 [720, 1440, 128], P('lat', 'lon'), may hold values from -6 to 6
- legendre: bfloat16 [720, 720, 720], P('lon', None, 'lat'), may hold values from -0.21875 to 0.21875
- quadrature: float32 [720], P('lat'), may hold values from 0.5 to 2
- mix_real: bfloat16 [720, 128, 128], P('lat'), may hold values from -0.375 to 0.375
- mix_imag: bfloat16 [720, 128, 128], P('lat'), may hold values from -0.375 to 0.375
Outputs:
- output: bfloat16 [720, 1440, 128], P('lat', 'lon')
All inputs are finite; a program needn't handle non-finite values.
Results may differ from a plain program's by a relative error of at most 0.015.
Values may be sent and summed in bfloat16 or wider, within the bound.
No kernel may reach another device: no remote copies, remote signals or barrier semaphores. Data moves between devices by JAX's collectives and lax.ppermute only.
A program may use at most 128 MiB of HBM per device.

v0:
```python
import jax
import jax.numpy as jnp
from jax import lax
from jax.sharding import PartitionSpec as P


def per_device(field, legendre, quadrature, mix_real, mix_imag):
    lon_devices = lax.axis_size("lon")
    lon_cols = field.shape[1]
    orders_dev = legendre.shape[0]
    degrees = legendre.shape[1]
    full_lon = lon_cols * lon_devices
    orders = orders_dev * lon_devices
    col_pos = jnp.arange(full_lon, dtype=jnp.int32)
    ord_pos = jnp.arange(orders, dtype=jnp.int32)
    phase = (col_pos[:, None] * ord_pos[None, :] % full_lon).astype(jnp.float32) * (
        2.0 * jnp.pi / full_lon
    )
    cosine = jnp.cos(phase)
    sine = jnp.sin(phase)
    forward_table = (
        jnp.stack([cosine, -sine], 1) * (1.0 / jnp.sqrt(jnp.float32(full_lon)))
    ).astype(jnp.bfloat16)
    inverse_table = (
        jnp.stack([cosine.T, -sine.T], 0) * jnp.sqrt(jnp.float32(2.0 / full_lon))
    ).astype(jnp.bfloat16)
    spectrum = jnp.einsum(
        "anc,nrm->armc",
        lax.all_to_all(field, "lon", split_axis=2, concat_axis=1, tiled=True),
        forward_table,
        preferred_element_type=jnp.float32,
    ).astype(jnp.bfloat16)
    fourier = lax.all_to_all(spectrum, "lon", split_axis=2, concat_axis=3, tiled=True)
    weighted = (quadrature[:, None, None, None] * fourier.astype(jnp.float32)).astype(jnp.bfloat16)
    lowest_order = lax.axis_index("lon") * orders_dev
    order_glob = lowest_order + jnp.arange(orders_dev, dtype=jnp.int32)
    degree_pos = jnp.arange(degrees, dtype=jnp.int32)
    masked = jnp.where(
        degree_pos[None, :, None] >= order_glob[:, None, None],
        legendre,
        jnp.zeros((), jnp.bfloat16),
    )
    coefficients = lax.psum_scatter(
        jnp.einsum("mla,armc->lrmc", masked, weighted, preferred_element_type=jnp.float32).astype(
            jnp.bfloat16
        ),
        "lat",
        scatter_dimension=0,
        tiled=True,
    )
    real_part = coefficients[:, 0]
    imag_part = coefficients[:, 1]

    def apply_mix(values, weights):
        return jnp.einsum("lmc,lcd->lmd", values, weights, preferred_element_type=jnp.float32)

    mixed = jnp.stack(
        [
            apply_mix(real_part, mix_real) - apply_mix(imag_part, mix_imag),
            apply_mix(real_part, mix_imag) + apply_mix(imag_part, mix_real),
        ],
        1,
    ).astype(jnp.bfloat16)
    every_degree = lax.all_gather(mixed, "lat", axis=0, tiled=True)
    grid_values = jnp.einsum(
        "mla,lrmc->armc", masked, every_degree, preferred_element_type=jnp.float32
    )
    grid_spectrum = grid_values.astype(jnp.bfloat16)
    samples = jnp.einsum(
        "armc,rmn->anc",
        lax.all_to_all(grid_spectrum, "lon", split_axis=3, concat_axis=2, tiled=True),
        inverse_table,
        preferred_element_type=jnp.float32,
    ).astype(jnp.bfloat16)
    synthesis = lax.all_to_all(samples, "lon", split_axis=1, concat_axis=2, tiled=True)
    return (field.astype(jnp.float32) + synthesis.astype(jnp.float32)).astype(jnp.bfloat16)


def solution(mesh):
    placed = (
        P("lat", "lon", None),
        P("lon", None, "lat"),
        P("lat"),
        P("lat", None, None),
        P("lat", None, None),
    )
    return jax.shard_map(
        per_device, mesh=mesh, in_specs=placed, out_specs=P("lat", "lon", None), check_vma=False
    )
```

profile of v0, /device:TPU:0, one launch (start us, length us, event | category | flops | bytes accessed | tf_op | source)
XLA Modules:
  0.0 658.2 jit_solution(100758692703265444)
XLA Ops:
  6.5 4.9 copy.54
  11.4 8.2 %all-to-all-start = ((bf16[90,90,128]{1,0,2:T(8,128)(2,1)}), bf16[90,90,128]{1,0,2:T(8,128)(2,1)}, u32[]{:S(2)}, u32[]{:S(2)}) async-start(bf16[90,90,128]{1,0,2:T(8,128)(2,1)} %copy.54), calls=%async_computation | async-start | bytes 6291456 | tf_op jit(solution)/shard_map/all_to_all | solution.py:29
  19.6 19.7 %sine_negate_fusion = (f32[1440,1,720]{2,0,1:T(8,128)}, f32[1440,1,720]{2,0,1:T(8,128)}) fusion(), kind=kLoop, calls=%fused_computation.27 | loop fusion | flops 10368000 | bytes 8294400 | tf_op jit(solution)/shard_map/neg | solution.py:22
  39.3 27.9 %all-to-all-done = bf16[90,90,128]{1,0,2:T(8,128)(2,1)} async-done(((bf16[90,90,128]{1,0,2:T(8,128)(2,1)}), bf16[90,90,128]{1,0,2:T(8,128)(2,1)}, u32[]{:S(2)}, u32[]{:S(2)}) %all-to-all-start) | async-done | bytes 2073632 | tf_op jit(solution)/shard_map/all_to_all | solution.py:29
  67.2 5.4 copy.79
  72.6 5.7 reshape.152
  78.3 9.7 %convert_bitcast_fusion.2 = bf16[90,2,720,8]{2,0,3,1:T(8,128)(2,1)} fusion(bf16[90,1440,8,1]{1,0,2,3:T(8,128)(2,1)} %reshape.152, f32[1440,1,720]{2,0,1:T(8,128)} %get-tuple-element.7, f32[1440,1,720]{2,0,1:T(8,128)} %get-tuple-element.8), kind=kOutput, calls=%fused_computation.46 | convolution fusion | flops 2993241600 | bytes 12441600 | tf_op jit(solution)/shard_map/anc,nrm->armc/dot_general | solution.py:27
  87.9 5.0 copy.58
  92.9 4.5 all-to-all-start.1
  97.9 41.4 %all-to-all-done.1 = bf16[90,2,720,8]{0,3,1,2:T(8,128)(2,1)} async-done(((bf16[90,2,720,8]{0,3,1,2:T(8,128)(2,1)}), bf16[90,2,720,8]{0,3,1,2:T(8,128)(2,1)}, u32[]{:S(2)}, u32[]{:S(2)}) %all-to-all-start.1) | async-done | bytes 2073632 | tf_op jit(solution)/shard_map/all_to_all | solution.py:33
  139.3 3.9 copy.59
  143.2 10.5 %convert_bitcast_fusion = bf16[720,2,45,128]{3,0,1,2:T(8,128)(2,1)} fusion(bf16[45,720,90]{1,2,0:T(8,128)(2,1)} %param.6, pred[45,720]{1,0:T(8,128)(4,1)S(1)} %iota_compare_fusion, f32[90]{0:T(128)S(1)} %copy-done.5, bf16[90,2,16,45,8]{0,4,3,2,1:T(8,128)(2,1)} %bitcast.88), kind=kOutput, calls=%fused_computation.2 | convolution fusion | flops 1507312768 | bytes 24527160 | tf_op jit(solution)/shard_map/mla,armc->lrmc/dot_general | solution.py:44
  153.8 57.4 %copy.62 = bf16[720,2,45,128]{3,1,2,0:T(2,128)(2,1)} copy(bf16[720,2,45,128]{3,0,1,2:T(8,128)(2,1)} %convert_bitcast_fusion) | data formatting | bytes 33177600 | tf_op jit(solution)/shard_map/convert_element_type | solution.py:44
  213.1 176.4 %all-reduce.3.cloned.1.call-done = bf16[720,2,45,128]{3,1,2,0:T(2,128)(2,1)} async-done(((bf16[720,2,45,128]{3,1,2,0:T(2,128)(2,1)}), bf16[720,2,45,128]{3,1,2,0:T(2,128)(2,1)}) %all-reduce.3.cloned.1.call-update) | async-done | bytes 16588816
  389.5 5.7 constant_dynamic-slice_fusion.1
  397.1 1.0 fusion.42
  399.1 1.6 pad_maximum_fusion
  400.7 89.6 %all-gather.2.cloned.1.call-done = bf16[720,2,45,128]{3,2,0,1:T(8,128)(2,1)} async-done(((bf16[90,2,45,128]{3,2,0,1:T(8,128)(2,1)}), bf16[720,2,45,128]{3,2,0,1:T(8,128)(2,1)}) %all-gather.2.cloned.1.call-update) | async-done | bytes 16588816 | tf_op jit(solution)/shard_map/all_gather | solution.py:64
  490.3 16.1 %convert_bitcast_fusion.3 = bf16[90,2,45,128]{3,0,1,2:T(8,128)(2,1)S(1)} fusion(bf16[45,720,90]{1,2,0:T(8,128)(2,1)} %param.6, pred[45,720]{1,0:T(8,128)(4,1)S(1)} %iota_compare_fusion, bf16[720,2,45,128]{3,2,0,1:T(8,128)(2,1)} %all-gather.2.cloned.1.call-done), kind=kOutput, calls=%fused_computation.48 | convolution fusion | flops 1496944768 | bytes 24526800 | tf_op jit(solution)/shard_map/mla,lrmc->armc/dot_general | solution.py:65
  506.4 5.0 copy.66
  511.4 7.0 %all-to-all-start.2 = ((bf16[90,2,45,128]{0,1,2,3:T(2,128)(2,1)}), bf16[90,2,45,128]{0,1,2,3:T(2,128)(2,1)S(1)}, u32[]{:S(2)}, u32[]{:S(2)}) async-start(bf16[90,2,45,128]{0,1,2,3:T(2,128)(2,1)} %copy.66), calls=%async_computation.2 | async-start | bytes 5898240 | tf_op jit(solution)/shard_map/all_to_all | solution.py:71
  518.4 19.8 %sine_negate_fusion.1 = (f32[1,720,1440]{2,1,0:T(8,128)}, f32[1,720,1440]{2,1,0:T(8,128)}) fusion(), kind=kLoop, calls=%fused_computation.33 | loop fusion | flops 10368000 | bytes 8294400 | tf_op jit(solution)/shard_map/neg | solution.py:25
  538.2 25.9 %all-to-all-done.2 = bf16[90,2,45,128]{0,1,2,3:T(2,128)(2,1)S(1)} async-done(((bf16[90,2,45,128]{0,1,2,3:T(2,128)(2,1)}), bf16[90,2,45,128]{0,1,2,3:T(2,128)(2,1)S(1)}, u32[]{:S(2)}, u32[]{:S(2)}) %all-to-all-start.2) | async-done | bytes 2073632 | tf_op jit(solution)/shard_map/all_to_all | solution.py:71
  566.4 1.5 copy-done.3
  567.9 5.6 fusion.31
  573.5 4.8 copy.70
  578.4 41.6 %all_to_all.54 = bf16[90,1440,8]{0,2,1:T(8,128)(2,1)S(1)} all-to-all(bf16[90,1440,8]{0,2,1:T(8,128)(2,1)} %copy.70), channel_id=1, replica_groups=mesh['lat'=8,'lon'=16] {'lon'}, dimensions={1} | all-to-all | bytes 4147200 | tf_op jit(solution)/shard_map/all_to_all | solution.py:75
  620.0 4.0 copy.71
  624.0 7.9 %reshape.150 = f32[90,16,90,8]{2,1,3,0:T(8,128)} reshape(bf16[90,1440,8]{1,2,0:T(8,128)(2,1)} %copy.71) | data formatting | bytes 6220800 | tf_op jit(solution)/shard_map/convert_element_type | solution.py:76
  632.0 8.0 %copy.103 = f32[90,90,16,8]{1,3,2,0:T(8,128)} copy(f32[90,90,16,8]{1,2,3,0:T(8,128)} %bitcast.87) | data formatting | bytes 8294400 | tf_op jit(solution)/shard_map/convert_element_type | solution.py:76
  640.0 6.2 copy.73
  646.2 5.0 add_convert_fusion
  (25 shorter events, 6.8 us)
Async XLA Ops:
  6.5 389.6 %copy-start = (bf16[90,128,128]{2,1,0:T(8,128)(2,1)S(1)}, bf16[90,128,128]{2,1,0:T(8,128)(2,1)}, u32[]{:S(2)}) copy-start(bf16[90,128,128]{2,1,0:T(8,128)(2,1)} %param.9) | copy-start | bytes 8847364
  11.4 55.7 %all-to-all-start = ((bf16[90,90,128]{1,0,2:T(8,128)(2,1)}), bf16[90,90,128]{1,0,2:T(8,128)(2,1)}, u32[]{:S(2)}, u32[]{:S(2)}) async-start(bf16[90,90,128]{1,0,2:T(8,128)(2,1)} %copy.54), calls=%async_computation | async-start | bytes 6291456 | tf_op jit(solution)/shard_map/all_to_all | solution.py:29
  92.9 46.4 %all-to-all-start.1 = ((bf16[90,2,720,8]{0,3,1,2:T(8,128)(2,1)}), bf16[90,2,720,8]{0,3,1,2:T(8,128)(2,1)}, u32[]{:S(2)}, u32[]{:S(2)}) async-start(bf16[90,2,720,8]{0,3,1,2:T(8,128)(2,1)} %copy.58), calls=%async_computation.1 | async-start | bytes 5898240 | tf_op jit(solution)/shard_map/all_to_all | solution.py:33
  97.4 292.1 %all-reduce.3.cloned.1.call-start = ((), (), s32[]{:S(2)}) async-start(), calls=%async_computation.5 | async-start | bytes 33177600
  97.9 45.4 %copy-start.5 = (f32[90]{0:T(128)S(1)}, f32[90]{0:T(128)}, u32[]{:S(2)}) copy-start(f32[90]{0:T(128)} %param.7) | copy-start | bytes 1084
  211.2 0.7 copy-start.6
  211.2 279.1 %all-gather.2.cloned.1.call-start = ((), (), s32[]{:S(2)}) async-start(), calls=%async_computation.4 | async-start | bytes 19906560 | tf_op jit(solution)/shard_map/all_gather | solution.py:64
  389.5 5.7 copy-start.2
  511.4 52.7 %all-to-all-start.2 = ((bf16[90,2,45,128]{0,1,2,3:T(2,128)(2,1)}), bf16[90,2,45,128]{0,1,2,3:T(2,128)(2,1)S(1)}, u32[]{:S(2)}, u32[]{:S(2)}) async-start(bf16[90,2,45,128]{0,1,2,3:T(2,128)(2,1)} %copy.66), calls=%async_computation.2 | async-start | bytes 5898240 | tf_op jit(solution)/shard_map/all_to_all | solution.py:71
  564.1 2.3 copy-start.4
  564.9 3.0 copy-start.3
  640.0 11.2 %copy-start.1 = (bf16[90,128,128]{2,1,0:T(8,128)(2,1)S(1)}, bf16[90,128,128]{2,1,0:T(8,128)(2,1)}, u32[]{:S(2)}) copy-start(bf16[90,128,128]{2,1,0:T(8,128)(2,1)} %param.9) | copy-start | bytes 8847364
Sparse Core Ops, SparseCore 0:
  211.3 178.1 all-reduce.2
  400.8 89.4 all-gather.1
where the time goes:
time: 666 us; the launch traced here: 658 us
  waiting for transfers between devices  361 us (54%)
  local copies, waits for them, and re-layouts  128 us (19%)
  other arithmetic  46.1 us (7%)
  matrix products  45.7 us (7%)
  blocking collectives  41.6 us (6%)
  starting transfers between devices  20.5 us (3%)
  between operations  14.4 us (2%)
    unnamed x3, waiting for transfers between devices  176 us
    all_gather x1, waiting for transfers between devices, per_device(): every_degree = lax.all_gather(mixed, 'lat', axis=0, tiled=True)  89.6 us
    convert_element_type x1, local copies, waits for them, and re-layouts, per_device(): jnp.einsum('mla,armc->lrmc', masked, weighted, preferred_element_type=jnp...  57.4 us
    all_to_all x1, blocking collectives, per_device(): lax.all_to_all(samples, 'lon', split_axis=1, concat_axis=2, tiled=True)  41.6 us
    all_to_all x1, waiting for transfers between devices, per_device(): lax.all_to_all(spectrum, 'lon', split_axis=2, concat_axis=3, tiled=True)  41.4 us
    all_to_all x1, waiting for transfers between devices, per_device(): lax.all_to_all(field, 'lon', split_axis=2, concat_axis=1, tiled=True)  27.9 us
    all_to_all x1, waiting for transfers between devices, per_device(): lax.all_to_all(grid_spectrum, 'lon', split_axis=3, concat_axis=2, tiled=T...  25.9 us
    convert_element_type x3, local copies, waits for them, and re-layouts, per_device(): synthesis.astype(jnp.float32)  22.2 us
  transfers between devices with their start and end apart: 5, of which 5 were waited for; matrix products, arithmetic and copies ran while one was open for 6% of the time, Pallas kernels for 0%

commit v1 on v0

v1 whole, which is shorter than its diff:
```python
import jax
import jax.numpy as jnp
import ml_dtypes
import numpy as np
from jax import lax
from jax.experimental import pallas as pl
from jax.experimental.pallas import tpu as pltpu
from jax.sharding import PartitionSpec as P

LAT = 8
LON = 16
ALL = LAT * LON
BAND = 90
PAD = 96
OWN = 6
RM = 2 * OWN
BLOCK = OWN * RM
SPEC = ALL * BLOCK
DEG = 720
DEGPAD = 768
COEF = DEG * RM
PART = BAND * RM
STEP = 15
SHIFTS = (0, 1, 7, 2, 6, 3, 5, 4)
GROUPS = ((4, 3, 5), (2, 6, 1, 7, 0))
SENDS = GROUPS[0] + GROUPS[1]
CH = 128
FULL = 1440
VMEM = 32 * 1024 * 1024
LEGENDRE_VMEM = 58 * 1024 * 1024


def order_of():
    p = np.arange(LAT)[None, :, None]
    q = np.arange(LON)[None, None, :]
    j = np.arange(OWN)[:, None, None]
    first = np.minimum(6 * p, 45 - OWN)
    order = 45 * q + first + j
    valid = np.broadcast_to(first + j >= 6 * p, order.shape)
    return order.reshape(-1), valid.reshape(-1)


def make_tables():
    order, valid = order_of()
    n = np.arange(FULL)
    phase = (n[:, None] * order[None, :] % FULL).astype(np.float32) * np.float32(2.0 * np.pi / FULL)
    cosine = np.cos(phase.astype(np.float64)).astype(np.float32)
    sine = np.sin(phase.astype(np.float64)).astype(np.float32)
    both = np.concatenate([cosine, -sine], 1) * np.concatenate([valid, valid])[None, :]
    both = both.reshape(LON, BAND, 2 * OWN * ALL)
    both = np.pad(both, ((0, 0), (0, PAD - BAND), (0, 0))).reshape(LON * PAD, RM * ALL)
    forward = both * np.float32(1.0 / np.sqrt(np.float32(FULL)))
    inverse = both * np.sqrt(np.float32(2.0 / FULL))
    return (
        np.ascontiguousarray(forward.T).astype(ml_dtypes.bfloat16),
        np.ascontiguousarray(inverse).astype(ml_dtypes.bfloat16),
    )


def widen(src, dst, rows):
    step = 576

    @pl.loop(0, rows // step)
    def _(i):
        part = pl.ds(pl.multiple_of(i * step, step), step)
        dst[part, :] = src[part, :].astype(dst.dtype)


def cut_kernel(scalars_ref, *refs):
    ins, outs = refs[: len(refs) // 2], refs[len(refs) // 2 :]
    count = ins[0].shape[0]
    degree = lax.broadcasted_iota(jnp.int32, (BAND, DEG), 1)
    for s, (in_ref, out_ref) in enumerate(zip(ins, outs)):
        first = scalars_ref[len(ins)] + (scalars_ref[s] + pl.program_id(0)) * count
        out_ref[...] = jnp.zeros(out_ref.shape, out_ref.dtype)
        for j in range(count):
            part = in_ref[j].astype(jnp.float32)
            part = jnp.where(degree >= first + j, part, 0.0)
            out_ref[j, :BAND, :DEG] = part.astype(out_ref.dtype)


def pass_kernel(in_ref, out_ref):
    for i in range(in_ref.shape[0]):
        out_ref[i] = in_ref[i]


def part_of(p):
    return pl.ds(pl.multiple_of(p * PART, 8), PART)


def dft_kernel(quad_ref, x_ref, t_ref, out_ref, s_ref):
    step = pl.program_id(0)
    x = jnp.concatenate(
        [x_ref[:, 0].reshape(LON * PAD, CH), x_ref[:, 1].reshape(LON * PAD, CH)], axis=1
    )
    rows = 768

    @pl.loop(0, RM * ALL // rows)
    def _(chunk):
        t = t_ref[pl.ds(pl.multiple_of(chunk * rows, rows), rows), :]
        y = jnp.dot(t, x, preferred_element_type=jnp.float32)
        for j in range(2):
            a = 2 * step + j
            scaled = y[:, j * CH : (j + 1) * CH] * quad_ref[a]
            for k in range(rows // ALL):
                s_ref[pl.ds(a * RM + chunk * (rows // ALL) + k, ALL, stride=BLOCK), :] = scaled[
                    k * ALL : (k + 1) * ALL
                ]

    @pl.when(step == pl.num_programs(0) - 1)
    def _():
        widen(s_ref, out_ref, SPEC)


def legendre_kernel(src_ref, dest_ref, w_ref, *refs):
    legs, outs, (s_in, s_out) = refs[:LAT], refs[LAT:-2], refs[-2:]
    m = pl.program_id(0)

    @pl.when(m == 0)
    def _():
        widen(w_ref, s_in, SPEC)

    parts = []
    for s in range(LAT):
        base = src_ref[s] * (PAD * RM) + m
        parts.append(
            jnp.concatenate(
                [s_in[pl.ds(base + r * OWN, PAD, stride=RM), :] for r in range(2)], axis=1
            ).astype(jnp.bfloat16)
        )
    w = jnp.concatenate(parts, axis=0)
    leg = jnp.concatenate([leg_ref[0] for leg_ref in legs], axis=0)
    y = lax.dot_general(leg, w, (((0,), (0,)), ((), ())), preferred_element_type=jnp.float32)
    for r in range(2):
        s_out[pl.ds(r * OWN + m, DEG, stride=RM), :] = y[:DEG, r * CH : (r + 1) * CH]

    @pl.when(m == pl.num_programs(0) - 1)
    def _():
        for s, out_ref in enumerate(outs):
            out_ref[...] = s_out[part_of(dest_ref[s]), :].astype(out_ref.dtype)


def mix_kernel(*refs):
    n = (len(refs) - 4) // 2
    xs, (wr_ref, wi_ref), outs = refs[:n], refs[n : n + 2], refs[n + 2 : -2]
    s_in, s_out = refs[-2:]
    step = pl.program_id(0)

    @pl.when(step == 0)
    def _():
        for s, x_ref in enumerate(xs):
            s_in[part_of(s), :] = x_ref[...].astype(s_in.dtype)

    count = wr_ref.shape[0]
    for d in range(count):
        base = (step * count + d) * RM
        x = jnp.concatenate(
            [
                jnp.concatenate(
                    [s_in[pl.ds(base + r * OWN + j, n, stride=PART), :] for j in range(OWN)],
                    axis=0,
                )
                for r in range(2)
            ],
            axis=1,
        ).astype(jnp.bfloat16)
        wr, wi = wr_ref[d], wi_ref[d]
        w = jnp.concatenate(
            [jnp.concatenate([wr, wi], axis=1), jnp.concatenate([-wi, wr], axis=1)], axis=0
        )
        y = jnp.dot(x, w, preferred_element_type=jnp.float32)
        for r in range(2):
            for j in range(OWN):
                s_out[pl.ds(base + r * OWN + j, n, stride=PART), :] = y[
                    j * n : (j + 1) * n, r * CH : (r + 1) * CH
                ]

    @pl.when(step == pl.num_programs(0) - 1)
    def _():
        for s, out_ref in enumerate(outs):
            out_ref[...] = s_out[part_of(s), :].astype(out_ref.dtype)


def inverse_legendre_kernel(src_ref, dest_ref, *refs):
    xs, legs, (out_ref, s_in, s_out) = refs[:LAT], refs[LAT:-3], refs[-3:]
    m = pl.program_id(0)

    @pl.when(m == 0)
    def _():
        for s, x_ref in enumerate(xs):
            s_in[part_of(dest_ref[s]), :] = x_ref[...].astype(s_in.dtype)

    x = jnp.concatenate(
        [s_in[pl.ds(r * OWN + m, DEG, stride=RM), :] for r in range(2)], axis=1
    ).astype(jnp.bfloat16)
    x = jnp.concatenate([x, jnp.zeros((DEGPAD - DEG, 2 * CH), jnp.bfloat16)], axis=0)
    leg = jnp.concatenate([leg_ref[0] for leg_ref in legs], axis=0)
    y = jnp.dot(leg, x, preferred_element_type=jnp.float32)
    for s in range(LAT):
        base = src_ref[s] * (PAD * RM) + m
        for r in range(2):
            s_out[pl.ds(base + r * OWN, PAD, stride=RM), :] = y[
                s * PAD : (s + 1) * PAD, r * CH : (r + 1) * CH
            ]

    @pl.when(m == pl.num_programs(0) - 1)
    def _():
        widen(s_out, out_ref, SPEC)


def inverse_dft_kernel(x_ref, t_ref, out_ref, s_in):
    step = pl.program_id(0)

    @pl.when(step == 0)
    def _():
        widen(x_ref, s_in, SPEC)

    x = jnp.concatenate(
        [
            jnp.concatenate(
                [s_in[pl.ds((2 * step + j) * RM + k, ALL, stride=BLOCK), :] for k in range(RM)],
                axis=0,
            )
            for j in range(2)
        ],
        axis=1,
    ).astype(jnp.bfloat16)
    blocks = 8
    rows = blocks * PAD

    @pl.loop(0, LON // blocks)
    def _(chunk):
        t = t_ref[pl.ds(pl.multiple_of(chunk * rows, rows), rows), :]
        y = jnp.dot(t, x, preferred_element_type=jnp.float32).astype(jnp.bfloat16)
        for j in range(2):
            out_ref[pl.ds(chunk * blocks, blocks), j] = y[:, j * CH : (j + 1) * CH].reshape(
                blocks, PAD, CH
            )


def params(limit=VMEM):
    return pltpu.CompilerParams(dimension_semantics=("arbitrary",), vmem_limit_bytes=limit)


def whole(shape):
    return pl.BlockSpec(shape, lambda *_: (0,) * len(shape))


def cut(table, scalars, n):
    count = 3
    return pl.pallas_call(
        cut_kernel,
        grid_spec=pltpu.PrefetchScalarGridSpec(
            num_scalar_prefetch=1,
            grid=(OWN // count,),
            in_specs=[
                pl.BlockSpec((count, BAND, DEG), lambda i, ref, s=s: (ref[s] + i, 0, 0))
                for s in range(n)
            ],
            out_specs=[pl.BlockSpec((count, PAD, DEGPAD), lambda i, ref: (i, 0, 0))] * n,
        ),
        out_shape=[jax.ShapeDtypeStruct((OWN, PAD, DEGPAD), jnp.bfloat16)] * n,
        compiler_params=params(LEGENDRE_VMEM),
        cost_estimate=pl.CostEstimate(
            flops=1_000_000 * n, bytes_accessed=1_700_000 * n, transcendentals=0
        ),
        name="cut",
    )(scalars, *[table] * n)


def in_order(token):
    return pl.pallas_call(
        pass_kernel,
        in_specs=[pl.BlockSpec(memory_space=pltpu.SMEM)],
        out_specs=pl.BlockSpec(memory_space=pltpu.SMEM),
        out_shape=jax.ShapeDtypeStruct(token.shape, token.dtype),
        cost_estimate=pl.CostEstimate(
            flops=60_000_000_000, bytes_accessed=200_000_000, transcendentals=0
        ),
        name="in_order",
    )(token)


def dft(quad, x, table):
    return pl.pallas_call(
        dft_kernel,
        grid=(OWN // 2,),
        in_specs=[
            pl.BlockSpec(memory_space=pltpu.SMEM),
            pl.BlockSpec((LON, 2, PAD, CH), lambda s: (0, s, 0, 0)),
            whole((RM * ALL, LON * PAD)),
        ],
        out_specs=whole((SPEC, CH)),
        out_shape=jax.ShapeDtypeStruct((SPEC, CH), jnp.bfloat16),
        scratch_shapes=[pltpu.VMEM((SPEC, CH), jnp.float32)],
        compiler_params=params(),
        cost_estimate=pl.CostEstimate(
            flops=1_000_000, bytes_accessed=100_000, transcendentals=0
        ),
        name="dft",
    )(quad, x, table)


def legendre_call(kernel, name, src, dest, xs, legs, rows_out, limit):
    rows_in = [x.shape[0] for x in xs]
    return pl.pallas_call(
        kernel,
        grid=(OWN,),
        in_specs=[pl.BlockSpec(memory_space=pltpu.SMEM)] * 2
        + [whole((rows, CH)) for rows in rows_in]
        + [pl.BlockSpec((1, PAD, DEGPAD), lambda m: (m, 0, 0))] * LAT,
        out_specs=[whole((rows, CH)) for rows in rows_out],
        out_shape=[jax.ShapeDtypeStruct((rows, CH), jnp.bfloat16) for rows in rows_out],
        scratch_shapes=[
            pltpu.VMEM((sum(rows_in), CH), jnp.float32),
            pltpu.VMEM((sum(rows_out), CH), jnp.float32),
        ],
        compiler_params=params(limit),
        cost_estimate=pl.CostEstimate(
            flops=2 * 6 * 768 * 768 * 256, bytes_accessed=12_000_000, transcendentals=0
        ),
        name=name,
    )(src, dest, *xs, *legs)


def mix(xs, wr, wi):
    n = len(xs)
    weight = pl.BlockSpec((STEP, CH, CH), lambda s: (s, 0, 0))
    return pl.pallas_call(
        mix_kernel,
        grid=(BAND // STEP,),
        in_specs=[whole((PART, CH))] * n + [weight, weight],
        out_specs=[whole((PART, CH))] * n,
        out_shape=[jax.ShapeDtypeStruct((PART, CH), jnp.bfloat16)] * n,
        scratch_shapes=[pltpu.VMEM((n * PART, CH), jnp.float32)] * 2,
        compiler_params=params(),
        cost_estimate=pl.CostEstimate(
            flops=2 * 90 * 48 * 256 * 256, bytes_accessed=10_000_000, transcendentals=0
        ),
        name="mix",
    )(*xs, wr, wi)


def inverse_dft(x, table):
    return pl.pallas_call(
        inverse_dft_kernel,
        grid=(OWN // 2,),
        in_specs=[whole((SPEC, CH)), whole((LON * PAD, RM * ALL))],
        out_specs=pl.BlockSpec((LON, 2, PAD, CH), lambda s: (0, s, 0, 0)),
        out_shape=jax.ShapeDtypeStruct((LON, OWN, PAD, CH), jnp.bfloat16),
        scratch_shapes=[pltpu.VMEM((SPEC, CH), jnp.float32)],
        compiler_params=params(),
        cost_estimate=pl.CostEstimate(
            flops=2 * 1536 * 1536 * 768, bytes_accessed=10_000_000, transcendentals=0
        ),
        name="inverse_dft",
    )(x, table)


def swap(x, axes):
    return lax.all_to_all(x, axes, split_axis=0, concat_axis=0, tiled=True)


def shifted(part, shift):
    if shift == 0:
        return part
    return lax.ppermute(part, "lat", [(i, (i + shift) % LAT) for i in range(LAT)])


def per_device(field, legendre, quadrature, mix_real, mix_imag):
    p = lax.axis_index("lat")
    q = lax.axis_index("lon")
    forward_table, inverse_table = make_tables()

    rows = swap(jnp.pad(field, ((0, PAD - BAND), (0, PAD - BAND), (0, 0))), "lon")

    orders = legendre.shape[0]
    table = jnp.transpose(legendre, (0, 2, 1))
    shifts = jnp.array(SHIFTS, jnp.int32)
    firsts = jnp.minimum(lax.rem(p + shifts, LAT) * (OWN // 3), (orders - OWN) // 3)
    src = lax.rem(p - shifts + LAT, LAT)
    dest = lax.rem(p + jnp.array(SENDS, jnp.int32), LAT)
    cuts = [None] * LAT
    for group in ((1, 2, 3, 4), (5, 6, 7, 0)):
        scalars = jnp.stack([firsts[i] for i in group] + [q * orders])
        parts = cut(table, scalars, len(group))
        table, *parts = lax.optimization_barrier((table, *parts))
        for i, part in zip(group, parts):
            cuts[i] = part
    quad = lax.dynamic_slice_in_dim(jnp.pad(quadrature, (0, PAD - BAND)), q * OWN, OWN, 0)

    legs = list(cuts)

    def end(value, places):
        parts = [shifted(cuts[i], SHIFTS[i]) for i in places]
        value, parts = lax.optimization_barrier((value, parts))
        for i, part in zip(places, parts):
            legs[i] = part
        return value

    dest = in_order(end(dest, (1, 2, 3, 4, 7)))
    cuts[5:7], rows, dest = lax.optimization_barrier((cuts[5:7], rows, dest))
    spectrum = dft(quad, rows.reshape(LON, OWN, PAD, CH), jnp.asarray(forward_table))
    dest = in_order(end(dest, (5, 6)))
    weighted = swap(spectrum, ("lat", "lon"))
    coefficients = legendre_call(
        legendre_kernel, "legendre", src, dest, [weighted], legs, [PART] * LAT, LEGENDRE_VMEM
    )
    mixed = []
    for group in GROUPS:
        parts = [shifted(coefficients[len(mixed) + i], shift) for i, shift in enumerate(group)]
        parts = mix(parts, mix_real, mix_imag)
        mixed += [shifted(part, (LAT - shift) % LAT) for part, shift in zip(parts, group)]
    (grid_spectrum,) = legendre_call(
        inverse_legendre_kernel, "inverse_legendre", src, dest, mixed, legs, [SPEC], VMEM
    )
    grid_spectrum = swap(grid_spectrum, ("lat", "lon"))
    samples = inverse_dft(grid_spectrum, jnp.asarray(inverse_table))
    synthesis = swap(samples.reshape(LON * OWN, PAD, CH), "lon")[:BAND, :BAND]
    return (field.astype(jnp.float32) + synthesis.astype(jnp.float32)).astype(jnp.bfloat16)


def solution(mesh):
    placed = (
        P("lat", "lon", None),
        P("lon", None, "lat"),
        P("lat"),
        P("lat", None, None),
        P("lat", None, None),
    )
    return jax.shard_map(
        per_device, mesh=mesh, in_specs=placed, out_specs=P("lat", "lon", None), check_vma=False
    )
```

time: 666 us -> 275 us (0.41); the launches traced: 658 us -> 274 us
  waiting for transfers between devices: 361 us -> 94.9 us
  local copies, waits for them, and re-layouts: 128 us -> 7.05 us
  matrix products: 45.7 us -> 0 us
  Pallas kernels: 0 us -> 44.8 us
  other arithmetic: 46.1 us -> 4.35 us
  blocking collectives: 41.6 us -> 72.2 us
  starting transfers between devices: 20.5 us -> 50.6 us
  between operations: 14.4 us -> 0.26 us
    unnamed x3 -> x0, waiting for transfers between devices: 176 us -> none
    convert_element_type x7 -> x0, local copies, waits for them, and re-layouts: 94.4 us -> none  [the longest x1 57.4 us: per_device(): jnp.einsum('mla,armc->lrmc', masked, weighted, preferred_element_type=jnp...]
    all_gather x1 -> x0, waiting for transfers between devices: 89.6 us -> none  [per_device(): every_degree = lax.all_gather(mixed, 'lat', axis=0, tiled=True)]
    all_to_all x3 -> x2, waiting for transfers between devices: 95.2 us -> 28.6 us  [swap(): return lax.all_to_all(x, axes, split_axis=0, concat_axis=0, tiled=True)]
    ppermute x0 -> x21, waiting for transfers between devices: none -> 66.3 us  [shifted(): lax.ppermute(part, 'lat', [(i, (i + shift) % LAT) for i in range(LAT)])]
    dot_general x8 -> x0, matrix products: 45.7 us -> none  [the longest x1 16.1 us: per_device(): jnp.einsum('mla,lrmc->armc', masked, every_degree, preferred_element_type...]
    pallas_call x0 -> x10, Pallas kernels: none -> 44.8 us  [the longest x2 15.6 us: legendre_call(): pl.pallas_call(kernel, grid=(OWN,), in_specs=[pl.BlockSpec(memory_space=p...]
    neg x2 -> x0, other arithmetic: 39.5 us -> none  [the longest x1 19.8 us: per_device(): -sine.T]
  transfers between devices with their start and end apart: 5 -> 23, of which waited for: 5 -> 16; matrix products, arithmetic and copies ran while one was open for 6% -> 1% of each run, Pallas kernels for 0% -> 7%
where the time goes in v1:
time: 275 us; the launch traced here: 274 us
  waiting for transfers between devices  94.9 us (35%)
  blocking collectives  72.2 us (26%)
  starting transfers between devices  50.6 us (18%)
  Pallas kernels  44.8 us (16%)
  local copies, waits for them, and re-layouts  7.05 us (3%)
  other arithmetic  4.35 us (2%)
    all_to_all x2, blocking collectives, swap(): return lax.all_to_all(x, axes, split_axis=0, concat_axis=0, tiled=True)  72.2 us
    ppermute x21, waiting for transfers between devices, shifted(): lax.ppermute(part, 'lat', [(i, (i + shift) % LAT) for i in range(LAT)])  66.3 us
    ppermute x21, starting transfers between devices, shifted(): lax.ppermute(part, 'lat', [(i, (i + shift) % LAT) for i in range(LAT)])  31.3 us
    all_to_all x2, waiting for transfers between devices, swap(): return lax.all_to_all(x, axes, split_axis=0, concat_axis=0, tiled=True)  28.6 us
    all_to_all x2, starting transfers between devices, swap(): return lax.all_to_all(x, axes, split_axis=0, concat_axis=0, tiled=True)  19.3 us
    pallas_call x2, Pallas kernels, legendre_call(): pl.pallas_call(kernel, grid=(OWN,), in_specs=[pl.BlockSpec(memory_space=p...  15.6 us
    pallas_call x2, Pallas kernels, cut(): pl.pallas_call(cut_kernel, grid_spec=pltpu.PrefetchScalarGridSpec(num_sca...  8.44 us
    pallas_call x2, Pallas kernels, mix(): pl.pallas_call(mix_kernel, grid=(BAND // STEP,), in_specs=[whole((PART, C...  6.49 us
  transfers between devices with their start and end apart: 23, of which 16 were waited for; matrix products, arithmetic and copies ran while one was open for 1% of the time, Pallas kernels for 7%

profile of v1, /device:TPU:0, one launch (start us, length us, event | category | flops | bytes accessed | tf_op | source)
XLA Modules:
  0.0 274.1 jit_solution(2085000405266180343)
XLA Ops:
  1.5 4.2 %cut.2 = (bf16[6,96,768]{2,1,0:T(8,128)(2,1)}, bf16[6,96,768]{2,1,0:T(8,128)(2,1)}, bf16[6,96,768]{2,1,0:T(8,128)(2,1)}, bf16[6,96,768]{2,1,0:T(8,128)(2,1)}) custom-call(s32[5]{0:T(128)} %get-tuple-element.97.scalars_ref, bf16[45,90,720]{2,1,0:T(8,128)(2,1)} %bitcast.16, bf16[45,90,720]{2,1,0:T(8,128)(2,1)} %bitcast.17, bf16[45,90,720]{2,1,0:T(8,128)(2,1)} %bitcast.18, ...), custom_call_target="tpu_custom_call" | custom-call | flops 4000000 | bytes 6800000 | tf_op jit(solution)/shard_map/cut/pallas_call | solution.py:251
  5.7 3.0 %collective-permute-start.1 = (bf16[6,96,768]{2,1,0:T(8,128)(2,1)}, bf16[6,96,768]{2,1,0:T(8,128)(2,1)}, u32[]{:S(2)}, u32[]{:S(2)}) collective-permute-start(bf16[6,96,768]{2,1,0:T(8,128)(2,1)} %get-tuple-element.63), channel_id=1, source_target_pairs={{0,112},{16,0},{32,16},{48,32},{64,48},{80,64},{96,80},{112,96},{1... | collective-permute-start | bytes 2654216 | tf_op jit(solution)/shard_map/ppermute | solution.py:367
  9.0 2.9 %collective-permute-start.3 = (bf16[6,96,768]{2,1,0:T(8,128)(2,1)}, bf16[6,96,768]{2,1,0:T(8,128)(2,1)}, u32[]{:S(2)}, u32[]{:S(2)}) collective-permute-start(bf16[6,96,768]{2,1,0:T(8,128)(2,1)} %get-tuple-element.65), channel_id=1, source_target_pairs={{0,96},{16,112},{32,0},{48,16},{64,32},{80,48},{96,64},{112,80},{1... | collective-permute-start | bytes 2654216 | tf_op jit(solution)/shard_map/ppermute | solution.py:367
  11.9 4.3 %cut.3 = (bf16[6,96,768]{2,1,0:T(8,128)(2,1)}, bf16[6,96,768]{2,1,0:T(8,128)(2,1)}, bf16[6,96,768]{2,1,0:T(8,128)(2,1)}, bf16[6,96,768]{2,1,0:T(8,128)(2,1)}) custom-call(s32[5]{0:T(128)} %get-tuple-element.98.scalars_ref, bf16[45,90,720]{2,1,0:T(8,128)(2,1)} %bitcast.20, bf16[45,90,720]{2,1,0:T(8,128)(2,1)} %bitcast.21, bf16[45,90,720]{2,1,0:T(8,128)(2,1)} %bitcast.22, ...), custom_call_target="tpu_custom_call" | custom-call | flops 4000000 | bytes 6800000 | tf_op jit(solution)/shard_map/cut/pallas_call | solution.py:251
  18.4 8.2 %all-to-all-start = ((bf16[96,96,128]{2,1,0:T(8,128)(2,1)}), bf16[96,96,128]{2,1,0:T(8,128)(2,1)S(1)}, u32[]{:S(2)}, u32[]{:S(2)}) async-start(bf16[96,96,128]{2,1,0:T(8,128)(2,1)} %pad.8), calls=%async_computation | async-start | bytes 4718592 | tf_op jit(solution)/shard_map/all_to_all | solution.py:361
  28.3 4.6 %collective-permute-done.2.refs_3_.refs_11_ = bf16[6,96,768]{2,1,0:T(8,128)(2,1)} collective-permute-done((bf16[6,96,768]{2,1,0:T(8,128)(2,1)}, bf16[6,96,768]{2,1,0:T(8,128)(2,1)}, u32[]{:S(2)}, u32[]{:S(2)}) %collective-permute-start.2) | collective-permute-done | bytes 884768 | tf_op jit(solution)/shard_map/ppermute | solution.py:367
  32.9 15.3 %collective-permute-done.3.refs_4_.refs_12_ = bf16[6,96,768]{2,1,0:T(8,128)(2,1)} collective-permute-done((bf16[6,96,768]{2,1,0:T(8,128)(2,1)}, bf16[6,96,768]{2,1,0:T(8,128)(2,1)}, u32[]{:S(2)}, u32[]{:S(2)}) %collective-permute-start.3) | collective-permute-done | bytes 884768 | tf_op jit(solution)/shard_map/ppermute | solution.py:367
  48.2 3.4 %collective-permute-done.4.refs_7_.refs_15_ = bf16[6,96,768]{2,1,0:T(8,128)(2,1)} collective-permute-done((bf16[6,96,768]{2,1,0:T(8,128)(2,1)}, bf16[6,96,768]{2,1,0:T(8,128)(2,1)}, u32[]{:S(2)}, u32[]{:S(2)}) %collective-permute-start.4) | collective-permute-done | bytes 884768 | tf_op jit(solution)/shard_map/ppermute | solution.py:367
  52.8 6.6 %all-to-all-done = bf16[96,96,128]{2,1,0:T(8,128)(2,1)S(1)} async-done(((bf16[96,96,128]{2,1,0:T(8,128)(2,1)}), bf16[96,96,128]{2,1,0:T(8,128)(2,1)S(1)}, u32[]{:S(2)}, u32[]{:S(2)}) %all-to-all-start) | async-done | bytes 2359328 | tf_op jit(solution)/shard_map/all_to_all | solution.py:361
  59.4 3.2 %collective-permute-start.6 = (bf16[6,96,768]{2,1,0:T(8,128)(2,1)}, bf16[6,96,768]{2,1,0:T(8,128)(2,1)}, u32[]{:S(2)}, u32[]{:S(2)}) collective-permute-start(bf16[6,96,768]{2,1,0:T(8,128)(2,1)} %get-tuple-element.70), channel_id=1, source_target_pairs={{0,80},{16,96},{32,112},{48,0},{64,16},{80,32},{96,48},{112,64},{1... | collective-permute-start | bytes 2654216 | tf_op jit(solution)/shard_map/ppermute | solution.py:367
  63.3 2.3 copy-done.3
  65.6 5.8 %dft.1 = bf16[9216,128]{1,0:T(8,128)(2,1)S(1)} custom-call(f32[6]{0:T(128)S(1)} %pad_dynamic-slice_fusion.quad_ref, bf16[16,6,96,128]{3,2,1,0:T(8,128)(2,1)S(1)} %bitcast.9, bf16[1536,1536]{1,0:T(8,128)(2,1)S(1)} %copy-done.3), custom_call_target="tpu_custom_call" | custom-call | flops 1000000 | bytes 100000 | tf_op jit(solution)/shard_map/dft/pallas_call | solution.py:285
  72.9 11.1 %all-to-all-start.1 = ((bf16[128,72,128]{2,1,0:T(8,128)(2,1)}), bf16[128,72,128]{2,1,0:T(8,128)(2,1)S(1)}, u32[]{:S(2)}, u32[]{:S(2)}) async-start(bf16[128,72,128]{2,1,0:T(8,128)(2,1)} %bitcast.11), calls=%async_computation.1 | async-start | bytes 4718592 | tf_op jit(solution)/shard_map/all_to_all | solution.py:361
  84.0 16.0 %collective-permute-done.6.refs_6_.refs_14_ = bf16[6,96,768]{2,1,0:T(8,128)(2,1)} collective-permute-done((bf16[6,96,768]{2,1,0:T(8,128)(2,1)}, bf16[6,96,768]{2,1,0:T(8,128)(2,1)}, u32[]{:S(2)}, u32[]{:S(2)}) %collective-permute-start.6) | collective-permute-done | bytes 884768 | tf_op jit(solution)/shard_map/ppermute | solution.py:367
  101.3 21.9 %all-to-all-done.1 = bf16[128,72,128]{2,1,0:T(8,128)(2,1)S(1)} async-done(((bf16[128,72,128]{2,1,0:T(8,128)(2,1)}), bf16[128,72,128]{2,1,0:T(8,128)(2,1)S(1)}, u32[]{:S(2)}, u32[]{:S(2)}) %all-to-all-start.1) | async-done | bytes 2359328 | tf_op jit(solution)/shard_map/all_to_all | solution.py:361
  124.6 9.3 %legendre.1 = (bf16[1080,128]{1,0:T(8,128)(2,1)}, bf16[1080,128]{1,0:T(8,128)(2,1)}, bf16[1080,128]{1,0:T(8,128)(2,1)}, bf16[1080,128]{1,0:T(8,128)(2,1)}, bf16[...) custom-call(s32[8]{0:T(128)} %compare_select_fusion.4.src_ref, ...), custom_call_target="tpu_custom_call" | custom-call | flops 1811939328 | bytes 12000000 | tf_op jit(solution)/shard_map/legendre/pallas_call | solution.py:306
  142.4 2.5 collective-permute-done.7.refs_0_
  144.9 3.3 %collective-permute-done.8.refs_1_ = bf16[1080,128]{1,0:T(8,128)(2,1)S(1)} collective-permute-done((bf16[1080,128]{1,0:T(8,128)(2,1)}, bf16[1080,128]{1,0:T(8,128)(2,1)S(1)}, u32[]{:S(2)}, u32[]{:S(2)}) %collective-permute-start.8) | collective-permute-done | bytes 276512 | tf_op jit(solution)/shard_map/ppermute | solution.py:367
  148.2 2.9 %collective-permute-start.16 = (bf16[1080,128]{1,0:T(8,128)(2,1)}, bf16[1080,128]{1,0:T(8,128)(2,1)S(1)}, u32[]{:S(2)}, u32[]{:S(2)}) collective-permute-start(bf16[1080,128]{1,0:T(8,128)(2,1)} %get-tuple-element.90), channel_id=1, source_target_pairs={{0,112},{16,0},{32,16},{48,32},{64,48},{80,64},{96,80},{112,96},{1... | collective-permute-start | bytes 829448 | tf_op jit(solution)/shard_map/ppermute | solution.py:367
  151.1 5.1 %collective-permute-done.9.refs_2_ = bf16[1080,128]{1,0:T(8,128)(2,1)S(1)} collective-permute-done((bf16[1080,128]{1,0:T(8,128)(2,1)}, bf16[1080,128]{1,0:T(8,128)(2,1)S(1)}, u32[]{:S(2)}, u32[]{:S(2)}) %collective-permute-start.9) | collective-permute-done | bytes 276512 | tf_op jit(solution)/shard_map/ppermute | solution.py:367
  156.2 3.1 %mix.2 = (bf16[1080,128]{1,0:T(8,128)(2,1)S(1)}, bf16[1080,128]{1,0:T(8,128)(2,1)S(1)}, bf16[1080,128]{1,0:T(8,128)(2,1)S(1)}) custom-call(bf16[1080,128]{1,0:T(8,128)(2,1)S(1)} %collective-permute-done.7.refs_0_, bf16[1080,128]{1,0:T(8,128)(2,1)S(1)} %collective-permute-done.8.refs_1_, bf16[1080,128]{1,0:T(8,128)(2,1)S(1)} %collective-permute-done.9.refs_2_, ...), custom_call_target="tpu_custom_call" | custom-call | flops 566231040 | bytes 10000000 | tf_op jit(solution)/shard_map/mix/pallas_call | solution.py:329
  159.3 2.4 collective-permute-start.10
  163.5 3.4 %mix.3 = (bf16[1080,128]{1,0:T(8,128)(2,1)S(1)}, bf16[1080,128]{1,0:T(8,128)(2,1)S(1)}, bf16[1080,128]{1,0:T(8,128)(2,1)S(1)}, bf16[1080,128]{1,0:T(8,128)(2,1)S(1)}, bf16[1080,128]{1,0:T(8,128)(2,1)S(1)}) custom-call(bf16[1080,128]{1,0:T(8,128)(2,1)S(1)} %collective-permute-done.13.refs_0_, bf16[1080,128]{1,0:T(8,128)(2,1)S(1)} %collective-permute-done.14.refs_1_, ...), custom_call_target="tpu_custom_call" | custom-call | flops 566231040 | bytes 10000000 | tf_op jit(solution)/shard_map/mix/pallas_call | solution.py:329
  166.9 3.0 %collective-permute-start.17 = (bf16[1080,128]{1,0:T(8,128)(2,1)S(1)}, bf16[1080,128]{1,0:T(8,128)(2,1)S(1)}, u32[]{:S(2)}, u32[]{:S(2)}) collective-permute-start(bf16[1080,128]{1,0:T(8,128)(2,1)S(1)} %get-tuple-element.92), channel_id=1, source_target_pairs={{0,96},{16,112},{32,0},{48,16},{64,32},{80,48},{96,64},{112,80},{1... | collective-permute-start | bytes 829448 | tf_op jit(solution)/shard_map/ppermute | solution.py:367
  171.7 3.0 %collective-permute-done.11.refs_1_ = bf16[1080,128]{1,0:T(8,128)(2,1)S(1)} collective-permute-done((bf16[1080,128]{1,0:T(8,128)(2,1)S(1)}, bf16[1080,128]{1,0:T(8,128)(2,1)S(1)}, u32[]{:S(2)}, u32[]{:S(2)}) %collective-permute-start.11) | collective-permute-done | bytes 276512 | tf_op jit(solution)/shard_map/ppermute | solution.py:367
  176.1 2.9 %collective-permute-done.12.refs_2_ = bf16[1080,128]{1,0:T(8,128)(2,1)S(1)} collective-permute-done((bf16[1080,128]{1,0:T(8,128)(2,1)S(1)}, bf16[1080,128]{1,0:T(8,128)(2,1)S(1)}, u32[]{:S(2)}, u32[]{:S(2)}) %collective-permute-start.12) | collective-permute-done | bytes 276512 | tf_op jit(solution)/shard_map/ppermute | solution.py:367
  178.9 3.4 %collective-permute-done.17.refs_3_ = bf16[1080,128]{1,0:T(8,128)(2,1)S(1)} collective-permute-done((bf16[1080,128]{1,0:T(8,128)(2,1)S(1)}, bf16[1080,128]{1,0:T(8,128)(2,1)S(1)}, u32[]{:S(2)}, u32[]{:S(2)}) %collective-permute-start.17) | collective-permute-done | bytes 276512 | tf_op jit(solution)/shard_map/ppermute | solution.py:367
  182.3 5.1 %collective-permute-done.18.refs_4_ = bf16[1080,128]{1,0:T(8,128)(2,1)S(1)} collective-permute-done((bf16[1080,128]{1,0:T(8,128)(2,1)S(1)}, bf16[1080,128]{1,0:T(8,128)(2,1)S(1)}, u32[]{:S(2)}, u32[]{:S(2)}) %collective-permute-start.18) | collective-permute-done | bytes 276512 | tf_op jit(solution)/shard_map/ppermute | solution.py:367
  187.6 6.3 %inverse_legendre.1 = bf16[9216,128]{1,0:T(8,128)(2,1)S(1)} custom-call(s32[8]{0:T(128)S(1)} %copy-done.10, s32[8]{0:T(128)S(1)} %copy-done.11, bf16[1080,128]{1,0:T(8,128)(2,1)S(1)} %collective-permute-done.10.refs_0_, bf16[1080,128]{1,0:T(8,128)(2,1)S(1)} %collective-permute-done.11.refs_1_, bf16[1080,128]{1,0:T(8,128)(2,1)S(1)} %collective-permute-done.12.refs_2_, ...), custom_call_target="tpu_custom_call" | custom-call | flops 1811939328 | bytes 12000000 | tf_op jit(solution)/shard_map/inverse_legendre/pallas_call | solution.py:306
  193.9 37.5 %all_to_all.32 = bf16[128,72,128]{2,1,0:T(8,128)(2,1)S(1)} all-to-all(bf16[128,72,128]{2,1,0:T(8,128)(2,1)S(1)} %bitcast.10), channel_id=1, replica_groups=mesh['lat'=8,'lon'=16] {'lat','lon'}, dimensions={0} | all-to-all | bytes 4718592 | tf_op jit(solution)/shard_map/all_to_all | solution.py:361
  231.4 6.0 %inverse_dft.1 = bf16[16,6,96,128]{3,2,1,0:T(8,128)(2,1)S(1)} custom-call(bf16[9216,128]{1,0:T(8,128)(2,1)S(1)} %bitcast.12, bf16[1536,1536]{1,0:T(8,128)(2,1)S(1)} %bitcast.15), custom_call_target="tpu_custom_call" | custom-call | flops 3623878656 | bytes 10000000 | tf_op jit(solution)/shard_map/inverse_dft/pallas_call | solution.py:345
  237.5 34.6 %all_to_all.33 = bf16[96,96,128]{2,1,0:T(8,128)(2,1)S(1)} all-to-all(bf16[96,96,128]{2,1,0:T(8,128)(2,1)S(1)} %bitcast.13), channel_id=1, replica_groups=mesh['lat'=8,'lon'=16] {'lon'}, dimensions={0} | all-to-all | bytes 4718592 | tf_op jit(solution)/shard_map/all_to_all | solution.py:361
  (76 shorter events, 27.2 us)
Async XLA Ops:
  5.7 21.5 %collective-permute-start = (bf16[6,96,768]{2,1,0:T(8,128)(2,1)}, bf16[6,96,768]{2,1,0:T(8,128)(2,1)S(1)}, u32[]{:S(2)}, u32[]{:S(2)}) collective-permute-start(bf16[6,96,768]{2,1,0:T(8,128)(2,1)} %get-tuple-element.62), channel_id=1, source_target_pairs={{0,16},{16,32},{32,48},{48,64},{64,80},{80,96},{96,112},{112,0},{1... | collective-permute-start | bytes 2654216 | tf_op jit(solution)/shard_map/ppermute | solution.py:367
  5.7 22.6 %collective-permute-start.1 = (bf16[6,96,768]{2,1,0:T(8,128)(2,1)}, bf16[6,96,768]{2,1,0:T(8,128)(2,1)}, u32[]{:S(2)}, u32[]{:S(2)}) collective-permute-start(bf16[6,96,768]{2,1,0:T(8,128)(2,1)} %get-tuple-element.63), channel_id=1, source_target_pairs={{0,112},{16,0},{32,16},{48,32},{64,48},{80,64},{96,80},{112,96},{1... | collective-permute-start | bytes 2654216 | tf_op jit(solution)/shard_map/ppermute | solution.py:367
  8.6 24.2 %collective-permute-start.2 = (bf16[6,96,768]{2,1,0:T(8,128)(2,1)}, bf16[6,96,768]{2,1,0:T(8,128)(2,1)}, u32[]{:S(2)}, u32[]{:S(2)}) collective-permute-start(bf16[6,96,768]{2,1,0:T(8,128)(2,1)} %get-tuple-element.64), channel_id=1, source_target_pairs={{0,32},{16,48},{32,64},{48,80},{64,96},{80,112},{96,0},{112,16},{1... | collective-permute-start | bytes 2654216 | tf_op jit(solution)/shard_map/ppermute | solution.py:367
  9.0 39.2 %collective-permute-start.3 = (bf16[6,96,768]{2,1,0:T(8,128)(2,1)}, bf16[6,96,768]{2,1,0:T(8,128)(2,1)}, u32[]{:S(2)}, u32[]{:S(2)}) collective-permute-start(bf16[6,96,768]{2,1,0:T(8,128)(2,1)} %get-tuple-element.65), channel_id=1, source_target_pairs={{0,96},{16,112},{32,0},{48,16},{64,32},{80,48},{96,64},{112,80},{1... | collective-permute-start | bytes 2654216 | tf_op jit(solution)/shard_map/ppermute | solution.py:367
  16.1 35.4 %collective-permute-start.4 = (bf16[6,96,768]{2,1,0:T(8,128)(2,1)}, bf16[6,96,768]{2,1,0:T(8,128)(2,1)}, u32[]{:S(2)}, u32[]{:S(2)}) collective-permute-start(bf16[6,96,768]{2,1,0:T(8,128)(2,1)} %get-tuple-element.66), channel_id=1, source_target_pairs={{0,64},{16,80},{32,96},{48,112},{64,0},{80,16},{96,32},{112,48},{1... | collective-permute-start | bytes 2654216 | tf_op jit(solution)/shard_map/ppermute | solution.py:367
  18.4 41.0 %all-to-all-start = ((bf16[96,96,128]{2,1,0:T(8,128)(2,1)}), bf16[96,96,128]{2,1,0:T(8,128)(2,1)S(1)}, u32[]{:S(2)}, u32[]{:S(2)}) async-start(bf16[96,96,128]{2,1,0:T(8,128)(2,1)} %pad.8), calls=%async_computation | async-start | bytes 4718592 | tf_op jit(solution)/shard_map/all_to_all | solution.py:361
  27.2 35.5 %copy-start.15 = (f32[90]{0:T(128)S(1)}, f32[90]{0:T(128)}, u32[]{:S(2)}) copy-start(f32[90]{0:T(128)} %param.11) | copy-start | bytes 1084
  27.2 35.6 %copy-start.16 = (s32[8]{0:T(128)S(1)}, s32[8]{0:T(128)}, u32[]{:S(2)}) copy-start(s32[8]{0:T(128)} %constant.55) | copy-start | bytes 100
  27.2 25.6 %copy-start.4 = (bf16[6,96,768]{2,1,0:T(8,128)(2,1)}, bf16[6,96,768]{2,1,0:T(8,128)(2,1)S(1)}, u32[]{:S(2)}) copy-start(bf16[6,96,768]{2,1,0:T(8,128)(2,1)S(1)} %collective-permute-done.refs_1_.refs_9_) | copy-start | bytes 2654212
  59.4 24.6 %collective-permute-start.5 = (bf16[6,96,768]{2,1,0:T(8,128)(2,1)}, bf16[6,96,768]{2,1,0:T(8,128)(2,1)S(1)}, u32[]{:S(2)}, u32[]{:S(2)}) collective-permute-start(bf16[6,96,768]{2,1,0:T(8,128)(2,1)} %get-tuple-element.69), channel_id=1, source_target_pairs={{0,48},{16,64},{32,80},{48,96},{64,112},{80,0},{96,16},{112,32},{1... | collective-permute-start | bytes 2654216 | tf_op jit(solution)/shard_map/ppermute | solution.py:367
  59.4 40.6 %collective-permute-start.6 = (bf16[6,96,768]{2,1,0:T(8,128)(2,1)}, bf16[6,96,768]{2,1,0:T(8,128)(2,1)}, u32[]{:S(2)}, u32[]{:S(2)}) collective-permute-start(bf16[6,96,768]{2,1,0:T(8,128)(2,1)} %get-tuple-element.70), channel_id=1, source_target_pairs={{0,80},{16,96},{32,112},{48,0},{64,16},{80,32},{96,48},{112,64},{1... | collective-permute-start | bytes 2654216 | tf_op jit(solution)/shard_map/ppermute | solution.py:367
  72.9 50.3 %all-to-all-start.1 = ((bf16[128,72,128]{2,1,0:T(8,128)(2,1)}), bf16[128,72,128]{2,1,0:T(8,128)(2,1)S(1)}, u32[]{:S(2)}, u32[]{:S(2)}) async-start(bf16[128,72,128]{2,1,0:T(8,128)(2,1)} %bitcast.11), calls=%async_computation.1 | async-start | bytes 4718592 | tf_op jit(solution)/shard_map/all_to_all | solution.py:361
  124.6 31.6 %copy-start = (bf16[90,128,128]{2,1,0:T(8,128)(2,1)S(1)}, bf16[90,128,128]{2,1,0:T(8,128)(2,1)}, u32[]{:S(2)}) copy-start(bf16[90,128,128]{2,1,0:T(8,128)(2,1)} %refs_5_.1) | copy-start | bytes 8847364
  124.6 31.6 %copy-start.1 = (bf16[90,128,128]{2,1,0:T(8,128)(2,1)S(1)}, bf16[90,128,128]{2,1,0:T(8,128)(2,1)}, u32[]{:S(2)}) copy-start(bf16[90,128,128]{2,1,0:T(8,128)(2,1)} %refs_6_.1) | copy-start | bytes 8847364
  133.9 11.0 %collective-permute-start.7 = (bf16[1080,128]{1,0:T(8,128)(2,1)}, bf16[1080,128]{1,0:T(8,128)(2,1)S(1)}, u32[]{:S(2)}, u32[]{:S(2)}) collective-permute-start(bf16[1080,128]{1,0:T(8,128)(2,1)} %get-tuple-element.81), channel_id=1, source_target_pairs={{0,64},{16,80},{32,96},{48,112},{64,0},{80,16},{96,32},{112,48},{1... | collective-permute-start | bytes 829448 | tf_op jit(solution)/shard_map/ppermute | solution.py:367
  135.9 12.3 %collective-permute-start.8 = (bf16[1080,128]{1,0:T(8,128)(2,1)}, bf16[1080,128]{1,0:T(8,128)(2,1)S(1)}, u32[]{:S(2)}, u32[]{:S(2)}) collective-permute-start(bf16[1080,128]{1,0:T(8,128)(2,1)} %get-tuple-element.82), channel_id=1, source_target_pairs={{0,48},{16,64},{32,80},{48,96},{64,112},{80,0},{96,16},{112,32},{1... | collective-permute-start | bytes 829448 | tf_op jit(solution)/shard_map/ppermute | solution.py:367
  137.1 19.0 %collective-permute-start.9 = (bf16[1080,128]{1,0:T(8,128)(2,1)}, bf16[1080,128]{1,0:T(8,128)(2,1)S(1)}, u32[]{:S(2)}, u32[]{:S(2)}) collective-permute-start(bf16[1080,128]{1,0:T(8,128)(2,1)} %get-tuple-element.83), channel_id=1, source_target_pairs={{0,80},{16,96},{32,112},{48,0},{64,16},{80,32},{96,48},{112,64},{1... | collective-permute-start | bytes 829448 | tf_op jit(solution)/shard_map/ppermute | solution.py:367
  139.2 22.5 %collective-permute-start.13 = (bf16[1080,128]{1,0:T(8,128)(2,1)}, bf16[1080,128]{1,0:T(8,128)(2,1)S(1)}, u32[]{:S(2)}, u32[]{:S(2)}) collective-permute-start(bf16[1080,128]{1,0:T(8,128)(2,1)} %get-tuple-element.87), channel_id=1, source_target_pairs={{0,32},{16,48},{32,64},{48,80},{64,96},{80,112},{96,0},{112,16},{1... | collective-permute-start | bytes 829448 | tf_op jit(solution)/shard_map/ppermute | solution.py:367
  140.3 22.3 %collective-permute-start.14 = (bf16[1080,128]{1,0:T(8,128)(2,1)}, bf16[1080,128]{1,0:T(8,128)(2,1)S(1)}, u32[]{:S(2)}, u32[]{:S(2)}) collective-permute-start(bf16[1080,128]{1,0:T(8,128)(2,1)} %get-tuple-element.88), channel_id=1, source_target_pairs={{0,96},{16,112},{32,0},{48,16},{64,32},{80,48},{96,64},{112,80},{1... | collective-permute-start | bytes 829448 | tf_op jit(solution)/shard_map/ppermute | solution.py:367
  144.9 18.5 %collective-permute-start.15 = (bf16[1080,128]{1,0:T(8,128)(2,1)}, bf16[1080,128]{1,0:T(8,128)(2,1)S(1)}, u32[]{:S(2)}, u32[]{:S(2)}) collective-permute-start(bf16[1080,128]{1,0:T(8,128)(2,1)} %get-tuple-element.89), channel_id=1, source_target_pairs={{0,16},{16,32},{32,48},{48,64},{64,80},{80,96},{96,112},{112,0},{1... | collective-permute-start | bytes 829448 | tf_op jit(solution)/shard_map/ppermute | solution.py:367
  148.2 15.2 %collective-permute-start.16 = (bf16[1080,128]{1,0:T(8,128)(2,1)}, bf16[1080,128]{1,0:T(8,128)(2,1)S(1)}, u32[]{:S(2)}, u32[]{:S(2)}) collective-permute-start(bf16[1080,128]{1,0:T(8,128)(2,1)} %get-tuple-element.90), channel_id=1, source_target_pairs={{0,112},{16,0},{32,16},{48,32},{64,48},{80,64},{96,80},{112,96},{1... | collective-permute-start | bytes 829448 | tf_op jit(solution)/shard_map/ppermute | solution.py:367
  159.3 11.1 %collective-permute-start.10 = (bf16[1080,128]{1,0:T(8,128)(2,1)S(1)}, bf16[1080,128]{1,0:T(8,128)(2,1)S(1)}, u32[]{:S(2)}, u32[]{:S(2)}) collective-permute-start(bf16[1080,128]{1,0:T(8,128)(2,1)S(1)} %get-tuple-element.84), channel_id=1, source_target_pairs={{0,64},{16,80},{32,96},{48,112},{64,0},{80,16},{96,32},{112,48},{1... | collective-permute-start | bytes 829448 | tf_op jit(solution)/shard_map/ppermute | solution.py:367
  161.6 13.0 %collective-permute-start.11 = (bf16[1080,128]{1,0:T(8,128)(2,1)S(1)}, bf16[1080,128]{1,0:T(8,128)(2,1)S(1)}, u32[]{:S(2)}, u32[]{:S(2)}) collective-permute-start(bf16[1080,128]{1,0:T(8,128)(2,1)S(1)} %get-tuple-element.85), channel_id=1, source_target_pairs={{0,80},{16,96},{32,112},{48,0},{64,16},{80,32},{96,48},{112,64},{1... | collective-permute-start | bytes 829448 | tf_op jit(solution)/shard_map/ppermute | solution.py:367
  162.6 16.4 %collective-permute-start.12 = (bf16[1080,128]{1,0:T(8,128)(2,1)S(1)}, bf16[1080,128]{1,0:T(8,128)(2,1)S(1)}, u32[]{:S(2)}, u32[]{:S(2)}) collective-permute-start(bf16[1080,128]{1,0:T(8,128)(2,1)S(1)} %get-tuple-element.86), channel_id=1, source_target_pairs={{0,48},{16,64},{32,80},{48,96},{64,112},{80,0},{96,16},{112,32},{1... | collective-permute-start | bytes 829448 | tf_op jit(solution)/shard_map/ppermute | solution.py:367
  163.4 24.1 %copy-start.5 = (bf16[6,96,768]{2,1,0:T(8,128)(2,1)S(1)}, bf16[6,96,768]{2,1,0:T(8,128)(2,1)}, u32[]{:S(2)}) copy-start(bf16[6,96,768]{2,1,0:T(8,128)(2,1)} %copy-done.4) | copy-start | bytes 2654212
  163.5 68.0 %slice-start = ((s8[4718592]{0:T(1024)(128)(4,1)}), s8[4194304]{0:T(1024)(128)(4,1)S(1)}, s32[]{:S(2)}) async-start(s8[4718592]{0:T(1024)(128)(4,1)} %bitcast.14), calls=%async_computation.4 | async-start | bytes 8388608
  166.9 15.5 %collective-permute-start.17 = (bf16[1080,128]{1,0:T(8,128)(2,1)S(1)}, bf16[1080,128]{1,0:T(8,128)(2,1)S(1)}, u32[]{:S(2)}, u32[]{:S(2)}) collective-permute-start(bf16[1080,128]{1,0:T(8,128)(2,1)S(1)} %get-tuple-element.92), channel_id=1, source_target_pairs={{0,96},{16,112},{32,0},{48,16},{64,32},{80,48},{96,64},{112,80},{1... | collective-permute-start | bytes 829448 | tf_op jit(solution)/shard_map/ppermute | solution.py:367
  169.9 17.6 %collective-permute-start.18 = (bf16[1080,128]{1,0:T(8,128)(2,1)S(1)}, bf16[1080,128]{1,0:T(8,128)(2,1)S(1)}, u32[]{:S(2)}, u32[]{:S(2)}) collective-permute-start(bf16[1080,128]{1,0:T(8,128)(2,1)S(1)} %get-tuple-element.93), channel_id=1, source_target_pairs={{0,32},{16,48},{32,64},{48,80},{64,96},{80,112},{96,0},{112,16},{1... | collective-permute-start | bytes 829448 | tf_op jit(solution)/shard_map/ppermute | solution.py:367
  170.4 17.0 %collective-permute-start.19 = (bf16[1080,128]{1,0:T(8,128)(2,1)S(1)}, bf16[1080,128]{1,0:T(8,128)(2,1)S(1)}, u32[]{:S(2)}, u32[]{:S(2)}) collective-permute-start(bf16[1080,128]{1,0:T(8,128)(2,1)S(1)} %get-tuple-element.94), channel_id=1, source_target_pairs={{0,112},{16,0},{32,16},{48,32},{64,48},{80,64},{96,80},{112,96},{1... | collective-permute-start | bytes 829448 | tf_op jit(solution)/shard_map/ppermute | solution.py:367
  174.7 12.9 %collective-permute-start.20 = (bf16[1080,128]{1,0:T(8,128)(2,1)S(1)}, bf16[1080,128]{1,0:T(8,128)(2,1)S(1)}, u32[]{:S(2)}, u32[]{:S(2)}) collective-permute-start(bf16[1080,128]{1,0:T(8,128)(2,1)S(1)} %get-tuple-element.95), channel_id=1, source_target_pairs={{0,16},{16,32},{32,48},{48,64},{64,80},{80,96},{96,112},{112,0},{1... | collective-permute-start | bytes 829448 | tf_op jit(solution)/shard_map/ppermute | solution.py:367
  187.6 43.9 %slice-start.1 = ((s8[4718592]{0:T(1024)(128)(4,1)}), s8[524288]{0:T(1024)(128)(4,1)S(1)}, s32[]{:S(2)}) async-start(s8[4718592]{0:T(1024)(128)(4,1)} %bitcast.14), calls=%async_computation.5 | async-start | bytes 1048576
  237.5 34.6 %copy-start.14 = (bf16[90,90,128]{2,1,0:T(8,128)(2,1)S(1)}, bf16[90,90,128]{2,1,0:T(8,128)(2,1)}, u32[]{:S(2)}) copy-start(bf16[90,90,128]{2,1,0:T(8,128)(2,1)} %param.9) | copy-start | bytes 6220804
  (11 other events, 147.2 us)

commit v2 on v1

--- a/solution.py
+++ b/solution.py
@@ -26,8 +26,8 @@
 SENDS = GROUPS[0] + GROUPS[1]
 CH = 128
 FULL = 1440
-VMEM = 32 * 1024 * 1024
-LEGENDRE_VMEM = 58 * 1024 * 1024
+VMEM = 24 * 1024 * 1024
+CUT_VMEM = 58 * 1024 * 1024
 
 
 def order_of():
@@ -260,7 +260,7 @@
             out_specs=[pl.BlockSpec((count, PAD, DEGPAD), lambda i, ref: (i, 0, 0))] * n,
         ),
         out_shape=[jax.ShapeDtypeStruct((OWN, PAD, DEGPAD), jnp.bfloat16)] * n,
-        compiler_params=params(LEGENDRE_VMEM),
+        compiler_params=params(CUT_VMEM),
         cost_estimate=pl.CostEstimate(
             flops=1_000_000 * n, bytes_accessed=1_700_000 * n, transcendentals=0
         ),
@@ -274,6 +274,7 @@
         in_specs=[pl.BlockSpec(memory_space=pltpu.SMEM)],
         out_specs=pl.BlockSpec(memory_space=pltpu.SMEM),
         out_shape=jax.ShapeDtypeStruct(token.shape, token.dtype),
+        compiler_params=pltpu.CompilerParams(vmem_limit_bytes=1024 * 1024),
         cost_estimate=pl.CostEstimate(
             flops=60_000_000_000, bytes_accessed=200_000_000, transcendentals=0
         ),
@@ -377,12 +378,13 @@
     orders = legendre.shape[0]
     table = jnp.transpose(legendre, (0, 2, 1))
     shifts = jnp.array(SHIFTS, jnp.int32)
-    firsts = jnp.minimum(lax.rem(p + shifts, LAT) * (OWN // 3), (orders - OWN) // 3)
     src = lax.rem(p - shifts + LAT, LAT)
     dest = lax.rem(p + jnp.array(SENDS, jnp.int32), LAT)
     cuts = [None] * LAT
     for group in ((1, 2, 3, 4), (5, 6, 7, 0)):
-        scalars = jnp.stack([firsts[i] for i in group] + [q * orders])
+        moves = jnp.array([SHIFTS[i] for i in group] + [0], jnp.int32)
+        firsts = jnp.minimum(lax.rem(p + moves, LAT) * (OWN // 3), (orders - OWN) // 3)
+        scalars = jnp.where(jnp.arange(len(group) + 1) == len(group), q * orders, firsts)
         parts = cut(table, scalars, len(group))
         table, *parts = lax.optimization_barrier((table, *parts))
         for i, part in zip(group, parts):
@@ -404,7 +406,7 @@
     dest = in_order(end(dest, (5, 6)))
     weighted = swap(spectrum, ("lat", "lon"))
     coefficients = legendre_call(
-        legendre_kernel, "legendre", src, dest, [weighted], legs, [PART] * LAT, LEGENDRE_VMEM
+        legendre_kernel, "legendre", src, dest, [weighted], legs, [PART] * LAT, VMEM
     )
     mixed = []
     for group in GROUPS:

time: 275 us -> 272 us (0.989)
  no operation moved by 1% of the time
where the time goes in v2:
time: 272 us; the launch traced here: 271 us
  waiting for transfers between devices  95.8 us (35%)
  blocking collectives  72.1 us (27%)
  starting transfers between devices  50.6 us (19%)
  Pallas kernels  42.4 us (16%)
  local copies, waits for them, and re-layouts  6.7 us (2%)
  other arithmetic  3.22 us (1%)
    all_to_all x2, blocking collectives, swap(): return lax.all_to_all(x, axes, split_axis=0, concat_axis=0, tiled=True)  72.1 us
    ppermute x21, waiting for transfers between devices, shifted(): lax.ppermute(part, 'lat', [(i, (i + shift) % LAT) for i in range(LAT)])  67.5 us
    ppermute x21, starting transfers between devices, shifted(): lax.ppermute(part, 'lat', [(i, (i + shift) % LAT) for i in range(LAT)])  31.4 us
    all_to_all x2, waiting for transfers between devices, swap(): return lax.all_to_all(x, axes, split_axis=0, concat_axis=0, tiled=True)  28.2 us
    all_to_all x2, starting transfers between devices, swap(): return lax.all_to_all(x, axes, split_axis=0, concat_axis=0, tiled=True)  19.2 us
    pallas_call x2, Pallas kernels, legendre_call(): pl.pallas_call(kernel, grid=(OWN,), in_specs=[pl.BlockSpec(memory_space=p...  13.3 us
    pallas_call x2, Pallas kernels, cut(): pl.pallas_call(cut_kernel, grid_spec=pltpu.PrefetchScalarGridSpec(num_sca...  8.47 us
    pallas_call x2, Pallas kernels, mix(): pl.pallas_call(mix_kernel, grid=(BAND // STEP,), in_specs=[whole((PART, C...  6.49 us
  transfers between devices with their start and end apart: 23, of which 16 were waited for; matrix products, arithmetic and copies ran while one was open for 1% of the time, Pallas kernels for 7%

profile of v2, /device:TPU:0, one launch (start us, length us, event | category | flops | bytes accessed | tf_op | source)
XLA Modules:
  0.0 271.0 jit_solution(8899933424743653192)
XLA Ops:
  1.3 4.2 %cut.2 = (bf16[6,96,768]{2,1,0:T(8,128)(2,1)}, bf16[6,96,768]{2,1,0:T(8,128)(2,1)}, bf16[6,96,768]{2,1,0:T(8,128)(2,1)}, bf16[6,96,768]{2,1,0:T(8,128)(2,1)}) custom-call(s32[5]{0:T(128)} %get-tuple-element.98.scalars_ref, bf16[45,90,720]{2,1,0:T(8,128)(2,1)} %bitcast.15, bf16[45,90,720]{2,1,0:T(8,128)(2,1)} %bitcast.16, bf16[45,90,720]{2,1,0:T(8,128)(2,1)} %bitcast.17, ...), custom_call_target="tpu_custom_call" | custom-call | flops 4000000 | bytes 6800000 | tf_op jit(solution)/shard_map/cut/pallas_call | solution.py:251
  5.5 3.0 %collective-permute-start.1 = (bf16[6,96,768]{2,1,0:T(8,128)(2,1)}, bf16[6,96,768]{2,1,0:T(8,128)(2,1)}, u32[]{:S(2)}, u32[]{:S(2)}) collective-permute-start(bf16[6,96,768]{2,1,0:T(8,128)(2,1)} %get-tuple-element.63), channel_id=1, source_target_pairs={{0,112},{16,0},{32,16},{48,32},{64,48},{80,64},{96,80},{112,96},{1... | collective-permute-start | bytes 2654216 | tf_op jit(solution)/shard_map/ppermute | solution.py:368
  8.8 2.9 %collective-permute-start.3 = (bf16[6,96,768]{2,1,0:T(8,128)(2,1)}, bf16[6,96,768]{2,1,0:T(8,128)(2,1)}, u32[]{:S(2)}, u32[]{:S(2)}) collective-permute-start(bf16[6,96,768]{2,1,0:T(8,128)(2,1)} %get-tuple-element.65), channel_id=1, source_target_pairs={{0,96},{16,112},{32,0},{48,16},{64,32},{80,48},{96,64},{112,80},{1... | collective-permute-start | bytes 2654216 | tf_op jit(solution)/shard_map/ppermute | solution.py:368
  11.7 4.3 %cut.3 = (bf16[6,96,768]{2,1,0:T(8,128)(2,1)}, bf16[6,96,768]{2,1,0:T(8,128)(2,1)}, bf16[6,96,768]{2,1,0:T(8,128)(2,1)}, bf16[6,96,768]{2,1,0:T(8,128)(2,1)}) custom-call(s32[5]{0:T(128)} %get-tuple-element.97.scalars_ref, bf16[45,90,720]{2,1,0:T(8,128)(2,1)} %bitcast.19, bf16[45,90,720]{2,1,0:T(8,128)(2,1)} %bitcast.20, bf16[45,90,720]{2,1,0:T(8,128)(2,1)} %bitcast.21, ...), custom_call_target="tpu_custom_call" | custom-call | flops 4000000 | bytes 6800000 | tf_op jit(solution)/shard_map/cut/pallas_call | solution.py:251
  18.3 8.2 %all-to-all-start = ((bf16[96,96,128]{2,1,0:T(8,128)(2,1)}), bf16[96,96,128]{2,1,0:T(8,128)(2,1)S(1)}, u32[]{:S(2)}, u32[]{:S(2)}) async-start(bf16[96,96,128]{2,1,0:T(8,128)(2,1)} %pad.8), calls=%async_computation | async-start | bytes 4718592 | tf_op jit(solution)/shard_map/all_to_all | solution.py:362
  28.1 4.6 %collective-permute-done.2.refs_3_.refs_11_ = bf16[6,96,768]{2,1,0:T(8,128)(2,1)} collective-permute-done((bf16[6,96,768]{2,1,0:T(8,128)(2,1)}, bf16[6,96,768]{2,1,0:T(8,128)(2,1)}, u32[]{:S(2)}, u32[]{:S(2)}) %collective-permute-start.2) | collective-permute-done | bytes 884768 | tf_op jit(solution)/shard_map/ppermute | solution.py:368
  32.7 15.3 %collective-permute-done.3.refs_4_.refs_12_ = bf16[6,96,768]{2,1,0:T(8,128)(2,1)} collective-permute-done((bf16[6,96,768]{2,1,0:T(8,128)(2,1)}, bf16[6,96,768]{2,1,0:T(8,128)(2,1)}, u32[]{:S(2)}, u32[]{:S(2)}) %collective-permute-start.3) | collective-permute-done | bytes 884768 | tf_op jit(solution)/shard_map/ppermute | solution.py:368
  48.0 3.4 %collective-permute-done.4.refs_7_.refs_15_ = bf16[6,96,768]{2,1,0:T(8,128)(2,1)} collective-permute-done((bf16[6,96,768]{2,1,0:T(8,128)(2,1)}, bf16[6,96,768]{2,1,0:T(8,128)(2,1)}, u32[]{:S(2)}, u32[]{:S(2)}) %collective-permute-start.4) | collective-permute-done | bytes 884768 | tf_op jit(solution)/shard_map/ppermute | solution.py:368
  52.5 6.8 %all-to-all-done = bf16[96,96,128]{2,1,0:T(8,128)(2,1)S(1)} async-done(((bf16[96,96,128]{2,1,0:T(8,128)(2,1)}), bf16[96,96,128]{2,1,0:T(8,128)(2,1)S(1)}, u32[]{:S(2)}, u32[]{:S(2)}) %all-to-all-start) | async-done | bytes 2359328 | tf_op jit(solution)/shard_map/all_to_all | solution.py:362
  59.3 3.2 %collective-permute-start.6 = (bf16[6,96,768]{2,1,0:T(8,128)(2,1)}, bf16[6,96,768]{2,1,0:T(8,128)(2,1)}, u32[]{:S(2)}, u32[]{:S(2)}) collective-permute-start(bf16[6,96,768]{2,1,0:T(8,128)(2,1)} %get-tuple-element.70), channel_id=1, source_target_pairs={{0,80},{16,96},{32,112},{48,0},{64,16},{80,32},{96,48},{112,64},{1... | collective-permute-start | bytes 2654216 | tf_op jit(solution)/shard_map/ppermute | solution.py:368
  62.6 2.3 copy-done.3
  64.9 5.8 %dft.1 = bf16[9216,128]{1,0:T(8,128)(2,1)S(1)} custom-call(f32[6]{0:T(128)S(1)} %pad_dynamic-slice_fusion.quad_ref, bf16[16,6,96,128]{3,2,1,0:T(8,128)(2,1)S(1)} %bitcast.8, bf16[1536,1536]{1,0:T(8,128)(2,1)S(1)} %copy-done.3), custom_call_target="tpu_custom_call" | custom-call | flops 1000000 | bytes 100000 | tf_op jit(solution)/shard_map/dft/pallas_call | solution.py:286
  72.2 11.0 %all-to-all-start.1 = ((bf16[128,72,128]{2,1,0:T(8,128)(2,1)}), bf16[128,72,128]{2,1,0:T(8,128)(2,1)S(1)}, u32[]{:S(2)}, u32[]{:S(2)}) async-start(bf16[128,72,128]{2,1,0:T(8,128)(2,1)} %bitcast.10), calls=%async_computation.1 | async-start | bytes 4718592 | tf_op jit(solution)/shard_map/all_to_all | solution.py:362
  83.2 17.1 %collective-permute-done.6.refs_6_.refs_14_ = bf16[6,96,768]{2,1,0:T(8,128)(2,1)} collective-permute-done((bf16[6,96,768]{2,1,0:T(8,128)(2,1)}, bf16[6,96,768]{2,1,0:T(8,128)(2,1)}, u32[]{:S(2)}, u32[]{:S(2)}) %collective-permute-start.6) | collective-permute-done | bytes 884768 | tf_op jit(solution)/shard_map/ppermute | solution.py:368
  101.5 21.5 %all-to-all-done.1 = bf16[128,72,128]{2,1,0:T(8,128)(2,1)S(1)} async-done(((bf16[128,72,128]{2,1,0:T(8,128)(2,1)}), bf16[128,72,128]{2,1,0:T(8,128)(2,1)S(1)}, u32[]{:S(2)}, u32[]{:S(2)}) %all-to-all-start.1) | async-done | bytes 2359328 | tf_op jit(solution)/shard_map/all_to_all | solution.py:362
  124.1 6.7 %legendre.1 = (bf16[1080,128]{1,0:T(8,128)(2,1)S(1)}, bf16[1080,128]{1,0:T(8,128)(2,1)S(1)}, bf16[1080,128]{1,0:T(8,128)(2,1)S(1)}, bf16[1080,128]{1,0:T(8,128)(...) custom-call(s32[8]{0:T(128)S(1)} %compare_select_fusion.6.src_ref, ...), custom_call_target="tpu_custom_call" | custom-call | flops 1811939328 | bytes 12000000 | tf_op jit(solution)/shard_map/legendre/pallas_call | solution.py:307
  139.3 2.4 collective-permute-done.7.refs_0_
  141.7 3.1 %collective-permute-done.8.refs_1_ = bf16[1080,128]{1,0:T(8,128)(2,1)S(1)} collective-permute-done((bf16[1080,128]{1,0:T(8,128)(2,1)S(1)}, bf16[1080,128]{1,0:T(8,128)(2,1)S(1)}, u32[]{:S(2)}, u32[]{:S(2)}) %collective-permute-start.8) | collective-permute-done | bytes 276512 | tf_op jit(solution)/shard_map/ppermute | solution.py:368
  144.8 3.1 %collective-permute-start.16 = (bf16[1080,128]{1,0:T(8,128)(2,1)S(1)}, bf16[1080,128]{1,0:T(8,128)(2,1)S(1)}, u32[]{:S(2)}, u32[]{:S(2)}) collective-permute-start(bf16[1080,128]{1,0:T(8,128)(2,1)S(1)} %get-tuple-element.90), channel_id=1, source_target_pairs={{0,112},{16,0},{32,16},{48,32},{64,48},{80,64},{96,80},{112,96},{1... | collective-permute-start | bytes 829448 | tf_op jit(solution)/shard_map/ppermute | solution.py:368
  147.9 5.0 %collective-permute-done.9.refs_2_ = bf16[1080,128]{1,0:T(8,128)(2,1)S(1)} collective-permute-done((bf16[1080,128]{1,0:T(8,128)(2,1)S(1)}, bf16[1080,128]{1,0:T(8,128)(2,1)S(1)}, u32[]{:S(2)}, u32[]{:S(2)}) %collective-permute-start.9) | collective-permute-done | bytes 276512 | tf_op jit(solution)/shard_map/ppermute | solution.py:368
  152.9 3.1 %mix.2 = (bf16[1080,128]{1,0:T(8,128)(2,1)S(1)}, bf16[1080,128]{1,0:T(8,128)(2,1)S(1)}, bf16[1080,128]{1,0:T(8,128)(2,1)S(1)}) custom-call(bf16[1080,128]{1,0:T(8,128)(2,1)S(1)} %collective-permute-done.7.refs_0_, bf16[1080,128]{1,0:T(8,128)(2,1)S(1)} %collective-permute-done.8.refs_1_, bf16[1080,128]{1,0:T(8,128)(2,1)S(1)} %collective-permute-done.9.refs_2_, ...), custom_call_target="tpu_custom_call" | custom-call | flops 566231040 | bytes 10000000 | tf_op jit(solution)/shard_map/mix/pallas_call | solution.py:330
  156.0 2.4 collective-permute-start.10
  160.1 3.4 %mix.3 = (bf16[1080,128]{1,0:T(8,128)(2,1)S(1)}, bf16[1080,128]{1,0:T(8,128)(2,1)S(1)}, bf16[1080,128]{1,0:T(8,128)(2,1)S(1)}, bf16[1080,128]{1,0:T(8,128)(2,1)S(1)}, bf16[1080,128]{1,0:T(8,128)(2,1)S(1)}) custom-call(bf16[1080,128]{1,0:T(8,128)(2,1)S(1)} %collective-permute-done.13.refs_0_, bf16[1080,128]{1,0:T(8,128)(2,1)S(1)} %collective-permute-done.14.refs_1_, ...), custom_call_target="tpu_custom_call" | custom-call | flops 566231040 | bytes 10000000 | tf_op jit(solution)/shard_map/mix/pallas_call | solution.py:330
  163.5 3.0 %collective-permute-start.17 = (bf16[1080,128]{1,0:T(8,128)(2,1)S(1)}, bf16[1080,128]{1,0:T(8,128)(2,1)S(1)}, u32[]{:S(2)}, u32[]{:S(2)}) collective-permute-start(bf16[1080,128]{1,0:T(8,128)(2,1)S(1)} %get-tuple-element.92), channel_id=1, source_target_pairs={{0,96},{16,112},{32,0},{48,16},{64,32},{80,48},{96,64},{112,80},{1... | collective-permute-start | bytes 829448 | tf_op jit(solution)/shard_map/ppermute | solution.py:368
  168.3 3.1 %collective-permute-done.11.refs_1_ = bf16[1080,128]{1,0:T(8,128)(2,1)S(1)} collective-permute-done((bf16[1080,128]{1,0:T(8,128)(2,1)S(1)}, bf16[1080,128]{1,0:T(8,128)(2,1)S(1)}, u32[]{:S(2)}, u32[]{:S(2)}) %collective-permute-start.11) | collective-permute-done | bytes 276512 | tf_op jit(solution)/shard_map/ppermute | solution.py:368
  172.7 2.9 %collective-permute-done.12.refs_2_ = bf16[1080,128]{1,0:T(8,128)(2,1)S(1)} collective-permute-done((bf16[1080,128]{1,0:T(8,128)(2,1)S(1)}, bf16[1080,128]{1,0:T(8,128)(2,1)S(1)}, u32[]{:S(2)}, u32[]{:S(2)}) %collective-permute-start.12) | collective-permute-done | bytes 276512 | tf_op jit(solution)/shard_map/ppermute | solution.py:368
  175.6 3.4 %collective-permute-done.17.refs_3_ = bf16[1080,128]{1,0:T(8,128)(2,1)S(1)} collective-permute-done((bf16[1080,128]{1,0:T(8,128)(2,1)S(1)}, bf16[1080,128]{1,0:T(8,128)(2,1)S(1)}, u32[]{:S(2)}, u32[]{:S(2)}) %collective-permute-start.17) | collective-permute-done | bytes 276512 | tf_op jit(solution)/shard_map/ppermute | solution.py:368
  179.1 5.2 %collective-permute-done.18.refs_4_ = bf16[1080,128]{1,0:T(8,128)(2,1)S(1)} collective-permute-done((bf16[1080,128]{1,0:T(8,128)(2,1)S(1)}, bf16[1080,128]{1,0:T(8,128)(2,1)S(1)}, u32[]{:S(2)}, u32[]{:S(2)}) %collective-permute-start.18) | collective-permute-done | bytes 276512 | tf_op jit(solution)/shard_map/ppermute | solution.py:368
  184.3 6.6 %inverse_legendre.1 = bf16[9216,128]{1,0:T(8,128)(2,1)S(1)} custom-call(s32[8]{0:T(128)S(1)} %compare_select_fusion.6.src_ref, s32[8]{0:T(128)S(1)} %in_order.3.dest_ref, bf16[1080,128]{1,0:T(8,128)(2,1)S(1)} %collective-permute-done.10.refs_0_, bf16[1080,128]{1,0:T(8,128)(2,1)S(1)} %collective-permute-done.11.refs_1_, ...), custom_call_target="tpu_custom_call" | custom-call | flops 1811939328 | bytes 12000000 | tf_op jit(solution)/shard_map/inverse_legendre/pallas_call | solution.py:307
  190.9 37.5 %all_to_all.32 = bf16[128,72,128]{2,1,0:T(8,128)(2,1)S(1)} all-to-all(bf16[128,72,128]{2,1,0:T(8,128)(2,1)S(1)} %bitcast.9), channel_id=1, replica_groups=mesh['lat'=8,'lon'=16] {'lat','lon'}, dimensions={0} | all-to-all | bytes 4718592 | tf_op jit(solution)/shard_map/all_to_all | solution.py:362
  228.3 6.0 %inverse_dft.1 = bf16[16,6,96,128]{3,2,1,0:T(8,128)(2,1)S(1)} custom-call(bf16[9216,128]{1,0:T(8,128)(2,1)S(1)} %bitcast.11, bf16[1536,1536]{1,0:T(8,128)(2,1)S(1)} %bitcast.14), custom_call_target="tpu_custom_call" | custom-call | flops 3623878656 | bytes 10000000 | tf_op jit(solution)/shard_map/inverse_dft/pallas_call | solution.py:346
  234.4 34.6 %all_to_all.33 = bf16[96,96,128]{2,1,0:T(8,128)(2,1)S(1)} all-to-all(bf16[96,96,128]{2,1,0:T(8,128)(2,1)S(1)} %bitcast.12), channel_id=1, replica_groups=mesh['lat'=8,'lon'=16] {'lon'}, dimensions={0} | all-to-all | bytes 4718592 | tf_op jit(solution)/shard_map/all_to_all | solution.py:362
  (59 shorter events, 26.0 us)
Async XLA Ops:
  5.5 21.0 %collective-permute-start = (bf16[6,96,768]{2,1,0:T(8,128)(2,1)}, bf16[6,96,768]{2,1,0:T(8,128)(2,1)S(1)}, u32[]{:S(2)}, u32[]{:S(2)}) collective-permute-start(bf16[6,96,768]{2,1,0:T(8,128)(2,1)} %get-tuple-element.62), channel_id=1, source_target_pairs={{0,16},{16,32},{32,48},{48,64},{64,80},{80,96},{96,112},{112,0},{1... | collective-permute-start | bytes 2654216 | tf_op jit(solution)/shard_map/ppermute | solution.py:368
  5.5 22.6 %collective-permute-start.1 = (bf16[6,96,768]{2,1,0:T(8,128)(2,1)}, bf16[6,96,768]{2,1,0:T(8,128)(2,1)}, u32[]{:S(2)}, u32[]{:S(2)}) collective-permute-start(bf16[6,96,768]{2,1,0:T(8,128)(2,1)} %get-tuple-element.63), channel_id=1, source_target_pairs={{0,112},{16,0},{32,16},{48,32},{64,48},{80,64},{96,80},{112,96},{1... | collective-permute-start | bytes 2654216 | tf_op jit(solution)/shard_map/ppermute | solution.py:368
  8.4 24.2 %collective-permute-start.2 = (bf16[6,96,768]{2,1,0:T(8,128)(2,1)}, bf16[6,96,768]{2,1,0:T(8,128)(2,1)}, u32[]{:S(2)}, u32[]{:S(2)}) collective-permute-start(bf16[6,96,768]{2,1,0:T(8,128)(2,1)} %get-tuple-element.64), channel_id=1, source_target_pairs={{0,32},{16,48},{32,64},{48,80},{64,96},{80,112},{96,0},{112,16},{1... | collective-permute-start | bytes 2654216 | tf_op jit(solution)/shard_map/ppermute | solution.py:368
  8.8 39.2 %collective-permute-start.3 = (bf16[6,96,768]{2,1,0:T(8,128)(2,1)}, bf16[6,96,768]{2,1,0:T(8,128)(2,1)}, u32[]{:S(2)}, u32[]{:S(2)}) collective-permute-start(bf16[6,96,768]{2,1,0:T(8,128)(2,1)} %get-tuple-element.65), channel_id=1, source_target_pairs={{0,96},{16,112},{32,0},{48,16},{64,32},{80,48},{96,64},{112,80},{1... | collective-permute-start | bytes 2654216 | tf_op jit(solution)/shard_map/ppermute | solution.py:368
  15.9 35.4 %collective-permute-start.4 = (bf16[6,96,768]{2,1,0:T(8,128)(2,1)}, bf16[6,96,768]{2,1,0:T(8,128)(2,1)}, u32[]{:S(2)}, u32[]{:S(2)}) collective-permute-start(bf16[6,96,768]{2,1,0:T(8,128)(2,1)} %get-tuple-element.66), channel_id=1, source_target_pairs={{0,64},{16,80},{32,96},{48,112},{64,0},{80,16},{96,32},{112,48},{1... | collective-permute-start | bytes 2654216 | tf_op jit(solution)/shard_map/ppermute | solution.py:368
  18.3 8.2 %copy-start.10 = (s32[8]{0:T(128)S(1)}, s32[8]{0:T(128)}, u32[]{:S(2)}) copy-start(s32[8]{0:T(128)} %constant.52.clone) | copy-start | bytes 100
  18.3 41.0 %all-to-all-start = ((bf16[96,96,128]{2,1,0:T(8,128)(2,1)}), bf16[96,96,128]{2,1,0:T(8,128)(2,1)S(1)}, u32[]{:S(2)}, u32[]{:S(2)}) async-start(bf16[96,96,128]{2,1,0:T(8,128)(2,1)} %pad.8), calls=%async_computation | async-start | bytes 4718592 | tf_op jit(solution)/shard_map/all_to_all | solution.py:362
  26.5 36.0 %copy-start.8 = (f32[90]{0:T(128)S(1)}, f32[90]{0:T(128)}, u32[]{:S(2)}) copy-start(f32[90]{0:T(128)} %param.13) | copy-start | bytes 1084
  26.5 36.1 %copy-start.9 = (s32[8]{0:T(128)S(1)}, s32[8]{0:T(128)}, u32[]{:S(2)}) copy-start(s32[8]{0:T(128)} %constant.66) | copy-start | bytes 100
  59.3 24.0 %collective-permute-start.5 = (bf16[6,96,768]{2,1,0:T(8,128)(2,1)}, bf16[6,96,768]{2,1,0:T(8,128)(2,1)}, u32[]{:S(2)}, u32[]{:S(2)}) collective-permute-start(bf16[6,96,768]{2,1,0:T(8,128)(2,1)} %get-tuple-element.69), channel_id=1, source_target_pairs={{0,48},{16,64},{32,80},{48,96},{64,112},{80,0},{96,16},{112,32},{1... | collective-permute-start | bytes 2654216 | tf_op jit(solution)/shard_map/ppermute | solution.py:368
  59.3 41.0 %collective-permute-start.6 = (bf16[6,96,768]{2,1,0:T(8,128)(2,1)}, bf16[6,96,768]{2,1,0:T(8,128)(2,1)}, u32[]{:S(2)}, u32[]{:S(2)}) collective-permute-start(bf16[6,96,768]{2,1,0:T(8,128)(2,1)} %get-tuple-element.70), channel_id=1, source_target_pairs={{0,80},{16,96},{32,112},{48,0},{64,16},{80,32},{96,48},{112,64},{1... | collective-permute-start | bytes 2654216 | tf_op jit(solution)/shard_map/ppermute | solution.py:368
  72.2 50.7 %all-to-all-start.1 = ((bf16[128,72,128]{2,1,0:T(8,128)(2,1)}), bf16[128,72,128]{2,1,0:T(8,128)(2,1)S(1)}, u32[]{:S(2)}, u32[]{:S(2)}) async-start(bf16[128,72,128]{2,1,0:T(8,128)(2,1)} %bitcast.10), calls=%async_computation.1 | async-start | bytes 4718592 | tf_op jit(solution)/shard_map/all_to_all | solution.py:362
  124.1 28.7 %copy-start = (bf16[90,128,128]{2,1,0:T(8,128)(2,1)S(1)}, bf16[90,128,128]{2,1,0:T(8,128)(2,1)}, u32[]{:S(2)}) copy-start(bf16[90,128,128]{2,1,0:T(8,128)(2,1)} %refs_5_.1) | copy-start | bytes 8847364
  124.1 28.7 %copy-start.1 = (bf16[90,128,128]{2,1,0:T(8,128)(2,1)S(1)}, bf16[90,128,128]{2,1,0:T(8,128)(2,1)}, u32[]{:S(2)}) copy-start(bf16[90,128,128]{2,1,0:T(8,128)(2,1)} %refs_6_.1) | copy-start | bytes 8847364
  130.9 10.9 %collective-permute-start.7 = (bf16[1080,128]{1,0:T(8,128)(2,1)S(1)}, bf16[1080,128]{1,0:T(8,128)(2,1)S(1)}, u32[]{:S(2)}, u32[]{:S(2)}) collective-permute-start(bf16[1080,128]{1,0:T(8,128)(2,1)S(1)} %get-tuple-element.81), channel_id=1, source_target_pairs={{0,64},{16,80},{32,96},{48,112},{64,0},{80,16},{96,32},{112,48},{1... | collective-permute-start | bytes 829448 | tf_op jit(solution)/shard_map/ppermute | solution.py:368
  132.8 12.0 %collective-permute-start.8 = (bf16[1080,128]{1,0:T(8,128)(2,1)S(1)}, bf16[1080,128]{1,0:T(8,128)(2,1)S(1)}, u32[]{:S(2)}, u32[]{:S(2)}) collective-permute-start(bf16[1080,128]{1,0:T(8,128)(2,1)S(1)} %get-tuple-element.82), channel_id=1, source_target_pairs={{0,48},{16,64},{32,80},{48,96},{64,112},{80,0},{96,16},{112,32},{1... | collective-permute-start | bytes 829448 | tf_op jit(solution)/shard_map/ppermute | solution.py:368
  134.0 18.8 %collective-permute-start.9 = (bf16[1080,128]{1,0:T(8,128)(2,1)S(1)}, bf16[1080,128]{1,0:T(8,128)(2,1)S(1)}, u32[]{:S(2)}, u32[]{:S(2)}) collective-permute-start(bf16[1080,128]{1,0:T(8,128)(2,1)S(1)} %get-tuple-element.83), channel_id=1, source_target_pairs={{0,80},{16,96},{32,112},{48,0},{64,16},{80,32},{96,48},{112,64},{1... | collective-permute-start | bytes 829448 | tf_op jit(solution)/shard_map/ppermute | solution.py:368
  136.1 22.3 %collective-permute-start.13 = (bf16[1080,128]{1,0:T(8,128)(2,1)S(1)}, bf16[1080,128]{1,0:T(8,128)(2,1)S(1)}, u32[]{:S(2)}, u32[]{:S(2)}) collective-permute-start(bf16[1080,128]{1,0:T(8,128)(2,1)S(1)} %get-tuple-element.87), channel_id=1, source_target_pairs={{0,32},{16,48},{32,64},{48,80},{64,96},{80,112},{96,0},{112,16},{1... | collective-permute-start | bytes 829448 | tf_op jit(solution)/shard_map/ppermute | solution.py:368
  137.2 22.1 %collective-permute-start.14 = (bf16[1080,128]{1,0:T(8,128)(2,1)S(1)}, bf16[1080,128]{1,0:T(8,128)(2,1)S(1)}, u32[]{:S(2)}, u32[]{:S(2)}) collective-permute-start(bf16[1080,128]{1,0:T(8,128)(2,1)S(1)} %get-tuple-element.88), channel_id=1, source_target_pairs={{0,96},{16,112},{32,0},{48,16},{64,32},{80,48},{96,64},{112,80},{1... | collective-permute-start | bytes 829448 | tf_op jit(solution)/shard_map/ppermute | solution.py:368
  141.7 18.4 %collective-permute-start.15 = (bf16[1080,128]{1,0:T(8,128)(2,1)S(1)}, bf16[1080,128]{1,0:T(8,128)(2,1)S(1)}, u32[]{:S(2)}, u32[]{:S(2)}) collective-permute-start(bf16[1080,128]{1,0:T(8,128)(2,1)S(1)} %get-tuple-element.89), channel_id=1, source_target_pairs={{0,16},{16,32},{32,48},{48,64},{64,80},{80,96},{96,112},{112,0},{1... | collective-permute-start | bytes 829448 | tf_op jit(solution)/shard_map/ppermute | solution.py:368
  144.8 15.3 %collective-permute-start.16 = (bf16[1080,128]{1,0:T(8,128)(2,1)S(1)}, bf16[1080,128]{1,0:T(8,128)(2,1)S(1)}, u32[]{:S(2)}, u32[]{:S(2)}) collective-permute-start(bf16[1080,128]{1,0:T(8,128)(2,1)S(1)} %get-tuple-element.90), channel_id=1, source_target_pairs={{0,112},{16,0},{32,16},{48,32},{64,48},{80,64},{96,80},{112,96},{1... | collective-permute-start | bytes 829448 | tf_op jit(solution)/shard_map/ppermute | solution.py:368
  156.0 11.1 %collective-permute-start.10 = (bf16[1080,128]{1,0:T(8,128)(2,1)S(1)}, bf16[1080,128]{1,0:T(8,128)(2,1)S(1)}, u32[]{:S(2)}, u32[]{:S(2)}) collective-permute-start(bf16[1080,128]{1,0:T(8,128)(2,1)S(1)} %get-tuple-element.84), channel_id=1, source_target_pairs={{0,64},{16,80},{32,96},{48,112},{64,0},{80,16},{96,32},{112,48},{1... | collective-permute-start | bytes 829448 | tf_op jit(solution)/shard_map/ppermute | solution.py:368
  158.4 13.0 %collective-permute-start.11 = (bf16[1080,128]{1,0:T(8,128)(2,1)S(1)}, bf16[1080,128]{1,0:T(8,128)(2,1)S(1)}, u32[]{:S(2)}, u32[]{:S(2)}) collective-permute-start(bf16[1080,128]{1,0:T(8,128)(2,1)S(1)} %get-tuple-element.85), channel_id=1, source_target_pairs={{0,80},{16,96},{32,112},{48,0},{64,16},{80,32},{96,48},{112,64},{1... | collective-permute-start | bytes 829448 | tf_op jit(solution)/shard_map/ppermute | solution.py:368
  159.4 16.3 %collective-permute-start.12 = (bf16[1080,128]{1,0:T(8,128)(2,1)S(1)}, bf16[1080,128]{1,0:T(8,128)(2,1)S(1)}, u32[]{:S(2)}, u32[]{:S(2)}) collective-permute-start(bf16[1080,128]{1,0:T(8,128)(2,1)S(1)} %get-tuple-element.86), channel_id=1, source_target_pairs={{0,48},{16,64},{32,80},{48,96},{64,112},{80,0},{96,16},{112,32},{1... | collective-permute-start | bytes 829448 | tf_op jit(solution)/shard_map/ppermute | solution.py:368
  160.1 24.2 %copy-start.5 = (bf16[6,96,768]{2,1,0:T(8,128)(2,1)S(1)}, bf16[6,96,768]{2,1,0:T(8,128)(2,1)}, u32[]{:S(2)}) copy-start(bf16[6,96,768]{2,1,0:T(8,128)(2,1)} %get-tuple-element.73.refs_0_.refs_8_) | copy-start | bytes 2654212
  160.1 68.2 %slice-start = ((s8[4718592]{0:T(1024)(128)(4,1)}), s8[524288]{0:T(1024)(128)(4,1)S(1)}, s32[]{:S(2)}) async-start(s8[4718592]{0:T(1024)(128)(4,1)} %bitcast.13), calls=%async_computation.4 | async-start | bytes 1048576
  163.5 15.5 %collective-permute-start.17 = (bf16[1080,128]{1,0:T(8,128)(2,1)S(1)}, bf16[1080,128]{1,0:T(8,128)(2,1)S(1)}, u32[]{:S(2)}, u32[]{:S(2)}) collective-permute-start(bf16[1080,128]{1,0:T(8,128)(2,1)S(1)} %get-tuple-element.92), channel_id=1, source_target_pairs={{0,96},{16,112},{32,0},{48,16},{64,32},{80,48},{96,64},{112,80},{1... | collective-permute-start | bytes 829448 | tf_op jit(solution)/shard_map/ppermute | solution.py:368
  166.5 17.7 %collective-permute-start.18 = (bf16[1080,128]{1,0:T(8,128)(2,1)S(1)}, bf16[1080,128]{1,0:T(8,128)(2,1)S(1)}, u32[]{:S(2)}, u32[]{:S(2)}) collective-permute-start(bf16[1080,128]{1,0:T(8,128)(2,1)S(1)} %get-tuple-element.93), channel_id=1, source_target_pairs={{0,32},{16,48},{32,64},{48,80},{64,96},{80,112},{96,0},{112,16},{1... | collective-permute-start | bytes 829448 | tf_op jit(solution)/shard_map/ppermute | solution.py:368
  167.1 17.2 %collective-permute-start.19 = (bf16[1080,128]{1,0:T(8,128)(2,1)S(1)}, bf16[1080,128]{1,0:T(8,128)(2,1)S(1)}, u32[]{:S(2)}, u32[]{:S(2)}) collective-permute-start(bf16[1080,128]{1,0:T(8,128)(2,1)S(1)} %get-tuple-element.94), channel_id=1, source_target_pairs={{0,112},{16,0},{32,16},{48,32},{64,48},{80,64},{96,80},{112,96},{1... | collective-permute-start | bytes 829448 | tf_op jit(solution)/shard_map/ppermute | solution.py:368
  171.4 12.9 %collective-permute-start.20 = (bf16[1080,128]{1,0:T(8,128)(2,1)S(1)}, bf16[1080,128]{1,0:T(8,128)(2,1)S(1)}, u32[]{:S(2)}, u32[]{:S(2)}) collective-permute-start(bf16[1080,128]{1,0:T(8,128)(2,1)S(1)} %get-tuple-element.95), channel_id=1, source_target_pairs={{0,16},{16,32},{32,48},{48,64},{64,80},{80,96},{96,112},{112,0},{1... | collective-permute-start | bytes 829448 | tf_op jit(solution)/shard_map/ppermute | solution.py:368
  184.3 44.0 %slice-start.1 = ((s8[4718592]{0:T(1024)(128)(4,1)}), s8[4194304]{0:T(1024)(128)(4,1)S(1)}, s32[]{:S(2)}) async-start(s8[4718592]{0:T(1024)(128)(4,1)} %bitcast.13), calls=%async_computation.5 | async-start | bytes 8388608
  234.4 34.6 %copy-start.7 = (bf16[90,90,128]{2,1,0:T(8,128)(2,1)S(1)}, bf16[90,90,128]{2,1,0:T(8,128)(2,1)}, u32[]{:S(2)}) copy-start(bf16[90,90,128]{2,1,0:T(8,128)(2,1)} %param.11) | copy-start | bytes 6220804
  (4 other events, 9.9 us)

commit v3 on v2

--- a/solution.py
+++ b/solution.py
@@ -1,3 +1,5 @@
+import functools
+
 import jax
 import jax.numpy as jnp
 import ml_dtypes
@@ -66,12 +68,12 @@
         dst[part, :] = src[part, :].astype(dst.dtype)
 
 
-def cut_kernel(scalars_ref, *refs):
+def cut_kernel(places, scalars_ref, *refs):
     ins, outs = refs[: len(refs) // 2], refs[len(refs) // 2 :]
     count = ins[0].shape[0]
     degree = lax.broadcasted_iota(jnp.int32, (BAND, DEG), 1)
     for s, (in_ref, out_ref) in enumerate(zip(ins, outs)):
-        first = scalars_ref[len(ins)] + (scalars_ref[s] + pl.program_id(0)) * count
+        first = scalars_ref[LAT] + (scalars_ref[places[s]] + pl.program_id(0)) * count
         out_ref[...] = jnp.zeros(out_ref.shape, out_ref.dtype)
         for j in range(count):
             part = in_ref[j].astype(jnp.float32)
@@ -82,6 +84,12 @@
 def pass_kernel(in_ref, out_ref):
     for i in range(in_ref.shape[0]):
         out_ref[i] = in_ref[i]
+
+
+def bring_kernel(table_hbm, table_ref, sem):
+    copy = pltpu.make_async_copy(table_hbm, table_ref, sem)
+    copy.start()
+    copy.wait()
 
 
 def part_of(p):
@@ -246,16 +254,16 @@
     return pl.BlockSpec(shape, lambda *_: (0,) * len(shape))
 
 
-def cut(table, scalars, n):
-    count = 3
-    return pl.pallas_call(
-        cut_kernel,
+def cut(table, scalars, places):
+    count, n = 3, len(places)
+    return pl.pallas_call(
+        functools.partial(cut_kernel, places),
         grid_spec=pltpu.PrefetchScalarGridSpec(
             num_scalar_prefetch=1,
             grid=(OWN // count,),
             in_specs=[
                 pl.BlockSpec((count, BAND, DEG), lambda i, ref, s=s: (ref[s] + i, 0, 0))
-                for s in range(n)
+                for s in places
             ],
             out_specs=[pl.BlockSpec((count, PAD, DEGPAD), lambda i, ref: (i, 0, 0))] * n,
         ),
@@ -266,6 +274,9 @@
         ),
         name="cut",
     )(scalars, *[table] * n)
+
+
+ORDER = pl.CostEstimate(flops=60_000_000_000, bytes_accessed=200_000_000, transcendentals=0)
 
 
 def in_order(token):
@@ -275,11 +286,21 @@
         out_specs=pl.BlockSpec(memory_space=pltpu.SMEM),
         out_shape=jax.ShapeDtypeStruct(token.shape, token.dtype),
         compiler_params=pltpu.CompilerParams(vmem_limit_bytes=1024 * 1024),
-        cost_estimate=pl.CostEstimate(
-            flops=60_000_000_000, bytes_accessed=200_000_000, transcendentals=0
-        ),
+        cost_estimate=ORDER,
         name="in_order",
     )(token)
+
+
+def bring(table):
+    return pl.pallas_call(
+        bring_kernel,
+        in_specs=[pl.BlockSpec(memory_space=pl.ANY)],
+        out_specs=pl.BlockSpec(memory_space=pltpu.VMEM),
+        out_shape=jax.ShapeDtypeStruct(table.shape, table.dtype),
+        scratch_shapes=[pltpu.SemaphoreType.DMA],
+        compiler_params=pltpu.CompilerParams(vmem_limit_bytes=12 * 1024 * 1024),
+        name="bring",
+    )(table)
 
 
 def dft(quad, x, table):
@@ -381,11 +402,11 @@
     src = lax.rem(p - shifts + LAT, LAT)
     dest = lax.rem(p + jnp.array(SENDS, jnp.int32), LAT)
     cuts = [None] * LAT
-    for group in ((1, 2, 3, 4), (5, 6, 7, 0)):
-        moves = jnp.array([SHIFTS[i] for i in group] + [0], jnp.int32)
-        firsts = jnp.minimum(lax.rem(p + moves, LAT) * (OWN // 3), (orders - OWN) // 3)
-        scalars = jnp.where(jnp.arange(len(group) + 1) == len(group), q * orders, firsts)
-        parts = cut(table, scalars, len(group))
+    firsts = lax.rem(p + jnp.array(SHIFTS + (0,), jnp.int32), LAT) * (OWN // 3)
+    firsts = jnp.minimum(firsts, (orders - OWN) // 3)
+    scalars = jnp.where(jnp.arange(LAT + 1) == LAT, q * orders, firsts)
+    for group in ((1, 2, 3, 4), (7,), (5, 6, 0)):
+        parts = cut(table, scalars, group)
         table, *parts = lax.optimization_barrier((table, *parts))
         for i, part in zip(group, parts):
             cuts[i] = part
@@ -400,9 +421,11 @@
             legs[i] = part
         return value
 
-    dest = in_order(end(dest, (1, 2, 3, 4, 7)))
+    dest = end(dest, (1, 2, 3, 4, 7))
+    dest, forward_table = lax.optimization_barrier((dest, bring(jnp.asarray(forward_table))))
+    dest = in_order(dest)
     cuts[5:7], rows, dest = lax.optimization_barrier((cuts[5:7], rows, dest))
-    spectrum = dft(quad, rows.reshape(LON, OWN, PAD, CH), jnp.asarray(forward_table))
+    spectrum = dft(quad, rows.reshape(LON, OWN, PAD, CH), forward_table)
     dest = in_order(end(dest, (5, 6)))
     weighted = swap(spectrum, ("lat", "lon"))
     coefficients = legendre_call(

time: 272 us -> 273 us (level)
  waiting for transfers between devices: 95.8 us -> 89.2 us
  local copies, waits for them, and re-layouts: 6.7 us -> 11.2 us
    all_to_all x2, waiting for transfers between devices: 28.2 us -> 21.2 us  [swap(): return lax.all_to_all(x, axes, split_axis=0, concat_axis=0, tiled=True)]
    unnamed x26 -> x30, local copies, waits for them, and re-layouts: 4.98 us -> 9.46 us
    pallas_call x2 -> x4, Pallas kernels: 8.47 us -> 10.9 us  [the longest x3 10.6 us: cut(): pl.pallas_call(functools.partial(cut_kernel, places), grid_spec=pltpu.Pre...]
  transfers between devices with their start and end apart: 23 -> 23, of which waited for: 16 -> 15; matrix products, arithmetic and copies ran while one was open for 1% -> 1% of each run, Pallas kernels for 7% -> 7%
where the time goes in v3:
time: 273 us
  waiting for transfers between devices  89.2 us (33%)
  blocking collectives  72 us (26%)
  starting transfers between devices  52.2 us (19%)
  Pallas kernels  44.8 us (16%)
  local copies, waits for them, and re-layouts  11.2 us (4%)
  other arithmetic  3.09 us (1%)
    all_to_all x2, blocking collectives, swap(): return lax.all_to_all(x, axes, split_axis=0, concat_axis=0, tiled=True)  72 us
    ppermute x21, waiting for transfers between devices, shifted(): lax.ppermute(part, 'lat', [(i, (i + shift) % LAT) for i in range(LAT)])  68 us
    ppermute x21, starting transfers between devices, shifted(): lax.ppermute(part, 'lat', [(i, (i + shift) % LAT) for i in range(LAT)])  33.5 us
    all_to_all x2, waiting for transfers between devices, swap(): return lax.all_to_all(x, axes, split_axis=0, concat_axis=0, tiled=True)  21.2 us
    all_to_all x2, starting transfers between devices, swap(): return lax.all_to_all(x, axes, split_axis=0, concat_axis=0, tiled=True)  18.7 us
    pallas_call x2, Pallas kernels, legendre_call(): pl.pallas_call(kernel, grid=(OWN,), in_specs=[pl.BlockSpec(memory_space=p...  13.3 us
    pallas_call x3, Pallas kernels, cut(): pl.pallas_call(functools.partial(cut_kernel, places), grid_spec=pltpu.Pre...  10.6 us
    unnamed x30, local copies, waits for them, and re-layouts  9.46 us
  transfers between devices with their start and end apart: 23, of which 15 were waited for; matrix products, arithmetic and copies ran while one was open for 1% of the time, Pallas kernels for 7%

profile of v3, /device:TPU:0, one launch (start us, length us, event | category | flops | bytes accessed | tf_op | source)
XLA Modules:
  0.0 272.7 jit_solution(6291608507619447632)
XLA Ops:
  1.1 4.1 %cut.3 = (bf16[6,96,768]{2,1,0:T(8,128)(2,1)}, bf16[6,96,768]{2,1,0:T(8,128)(2,1)}, bf16[6,96,768]{2,1,0:T(8,128)(2,1)}, bf16[6,96,768]{2,1,0:T(8,128)(2,1)}) custom-call(s32[9]{0:T(128)} %compare_select_fusion.6.scalars_ref, bf16[45,90,720]{2,1,0:T(8,128)(2,1)} %bitcast.15, bf16[45,90,720]{2,1,0:T(8,128)(2,1)} %bitcast.16, bf16[45,90,720]{2,1,0:T(8,128)(2,1)} %bitcast.17, ...), custom_call_target="tpu_custom_call" | custom-call | flops 4000000 | bytes 6800000 | tf_op jit(solution)/shard_map/cut/pallas_call | solution.py:259
  5.3 2.8 %cut.4 = bf16[6,96,768]{2,1,0:T(8,128)(2,1)} custom-call(s32[9]{0:T(128)} %compare_select_fusion.6.scalars_ref, bf16[45,90,720]{2,1,0:T(8,128)(2,1)} %bitcast.19), custom_call_target="tpu_custom_call" | custom-call | flops 1000000 | bytes 1700000 | tf_op jit(solution)/shard_map/cut/pallas_call | solution.py:259
  8.1 3.1 %collective-permute-start.4 = (bf16[6,96,768]{2,1,0:T(8,128)(2,1)}, bf16[6,96,768]{2,1,0:T(8,128)(2,1)S(1)}, u32[]{:S(2)}, u32[]{:S(2)}) collective-permute-start(bf16[6,96,768]{2,1,0:T(8,128)(2,1)} %cut.4), channel_id=1, source_target_pairs={{0,64},{16,80},{32,96},{48,112},{64,0},{80,16},{96,32},{112,48},{1... | collective-permute-start | bytes 2654216 | tf_op jit(solution)/shard_map/ppermute | solution.py:389
  11.2 3.0 %collective-permute-start.1 = (bf16[6,96,768]{2,1,0:T(8,128)(2,1)}, bf16[6,96,768]{2,1,0:T(8,128)(2,1)}, u32[]{:S(2)}, u32[]{:S(2)}) collective-permute-start(bf16[6,96,768]{2,1,0:T(8,128)(2,1)} %get-tuple-element.65), channel_id=1, source_target_pairs={{0,112},{16,0},{32,16},{48,32},{64,48},{80,64},{96,80},{112,96},{1... | collective-permute-start | bytes 2654216 | tf_op jit(solution)/shard_map/ppermute | solution.py:389
  14.2 3.2 %collective-permute-start.3 = (bf16[6,96,768]{2,1,0:T(8,128)(2,1)}, bf16[6,96,768]{2,1,0:T(8,128)(2,1)}, u32[]{:S(2)}, u32[]{:S(2)}) collective-permute-start(bf16[6,96,768]{2,1,0:T(8,128)(2,1)} %get-tuple-element.67), channel_id=1, source_target_pairs={{0,96},{16,112},{32,0},{48,16},{64,32},{80,48},{96,64},{112,80},{1... | collective-permute-start | bytes 2654216 | tf_op jit(solution)/shard_map/ppermute | solution.py:389
  19.0 8.0 %all-to-all-start = ((bf16[96,96,128]{2,1,0:T(8,128)(2,1)}), bf16[96,96,128]{2,1,0:T(8,128)(2,1)S(1)}, u32[]{:S(2)}, u32[]{:S(2)}) async-start(bf16[96,96,128]{2,1,0:T(8,128)(2,1)} %pad.8), calls=%async_computation | async-start | bytes 4718592 | tf_op jit(solution)/shard_map/all_to_all | solution.py:383
  27.1 3.6 %cut.5 = (bf16[6,96,768]{2,1,0:T(8,128)(2,1)}, bf16[6,96,768]{2,1,0:T(8,128)(2,1)}, bf16[6,96,768]{2,1,0:T(8,128)(2,1)}) custom-call(s32[9]{0:T(128)} %compare_select_fusion.6.scalars_ref, bf16[45,90,720]{2,1,0:T(8,128)(2,1)} %bitcast.20, bf16[45,90,720]{2,1,0:T(8,128)(2,1)} %bitcast.21, bf16[45,90,720]{2,1,0:T(8,128)(2,1)} %bitcast.22), custom_call_target="tpu_custom_call" | custom-call | flops 3000000 | bytes 5100000 | tf_op jit(solution)/shard_map/cut/pallas_call | solution.py:259
  30.7 2.3 copy-done.5
  35.6 14.8 %collective-permute-done.refs_1_.refs_9_ = bf16[6,96,768]{2,1,0:T(8,128)(2,1)} collective-permute-done((bf16[6,96,768]{2,1,0:T(8,128)(2,1)}, bf16[6,96,768]{2,1,0:T(8,128)(2,1)}, u32[]{:S(2)}, u32[]{:S(2)}) %collective-permute-start) | collective-permute-done | bytes 884768 | tf_op jit(solution)/shard_map/ppermute | solution.py:389
  50.6 9.4 %collective-permute-done.3.refs_4_.refs_12_ = bf16[6,96,768]{2,1,0:T(8,128)(2,1)} collective-permute-done((bf16[6,96,768]{2,1,0:T(8,128)(2,1)}, bf16[6,96,768]{2,1,0:T(8,128)(2,1)}, u32[]{:S(2)}, u32[]{:S(2)}) %collective-permute-start.3) | collective-permute-done | bytes 884768 | tf_op jit(solution)/shard_map/ppermute | solution.py:389
  64.5 2.3 copy-done.1
  66.9 5.8 %dft.1 = bf16[9216,128]{1,0:T(8,128)(2,1)S(1)} custom-call(f32[6]{0:T(128)S(1)} %pad_dynamic-slice_fusion.quad_ref, bf16[16,6,96,128]{3,2,1,0:T(8,128)(2,1)S(1)} %bitcast.8, bf16[1536,1536]{1,0:T(8,128)(2,1)S(1)} %copy-done.1), custom_call_target="tpu_custom_call" | custom-call | flops 1000000 | bytes 100000 | tf_op jit(solution)/shard_map/dft/pallas_call | solution.py:307
  74.1 10.7 %all-to-all-start.1 = ((bf16[128,72,128]{2,1,0:T(8,128)(2,1)}), bf16[128,72,128]{2,1,0:T(8,128)(2,1)S(1)}, u32[]{:S(2)}, u32[]{:S(2)}) async-start(bf16[128,72,128]{2,1,0:T(8,128)(2,1)} %bitcast.10), calls=%async_computation.1 | async-start | bytes 4718592 | tf_op jit(solution)/shard_map/all_to_all | solution.py:383
  85.0 17.1 %collective-permute-done.6.refs_6_.refs_14_ = bf16[6,96,768]{2,1,0:T(8,128)(2,1)} collective-permute-done((bf16[6,96,768]{2,1,0:T(8,128)(2,1)}, bf16[6,96,768]{2,1,0:T(8,128)(2,1)}, u32[]{:S(2)}, u32[]{:S(2)}) %collective-permute-start.6) | collective-permute-done | bytes 884768 | tf_op jit(solution)/shard_map/ppermute | solution.py:389
  103.2 21.2 %all-to-all-done.1 = bf16[128,72,128]{2,1,0:T(8,128)(2,1)S(1)} async-done(((bf16[128,72,128]{2,1,0:T(8,128)(2,1)}), bf16[128,72,128]{2,1,0:T(8,128)(2,1)S(1)}, u32[]{:S(2)}, u32[]{:S(2)}) %all-to-all-start.1) | async-done | bytes 2359328 | tf_op jit(solution)/shard_map/all_to_all | solution.py:383
  125.6 6.7 %legendre.1 = (bf16[1080,128]{1,0:T(8,128)(2,1)S(1)}, bf16[1080,128]{1,0:T(8,128)(2,1)S(1)}, bf16[1080,128]{1,0:T(8,128)(2,1)S(1)}, bf16[1080,128]{1,0:T(8,128)(...) custom-call(s32[8]{0:T(128)S(1)} %compare_select_fusion.4.src_ref, ...), custom_call_target="tpu_custom_call" | custom-call | flops 1811939328 | bytes 12000000 | tf_op jit(solution)/shard_map/legendre/pallas_call | solution.py:328
  132.3 2.5 collective-permute-start.7
  135.6 2.4 collective-permute-start.9
  138.8 2.5 collective-permute-start.14
  141.3 2.3 collective-permute-done.7.refs_0_
  143.6 4.3 %collective-permute-done.8.refs_1_ = bf16[1080,128]{1,0:T(8,128)(2,1)S(1)} collective-permute-done((bf16[1080,128]{1,0:T(8,128)(2,1)S(1)}, bf16[1080,128]{1,0:T(8,128)(2,1)S(1)}, u32[]{:S(2)}, u32[]{:S(2)}) %collective-permute-start.8) | collective-permute-done | bytes 276512 | tf_op jit(solution)/shard_map/ppermute | solution.py:389
  149.7 4.8 %collective-permute-done.9.refs_2_ = bf16[1080,128]{1,0:T(8,128)(2,1)S(1)} collective-permute-done((bf16[1080,128]{1,0:T(8,128)(2,1)S(1)}, bf16[1080,128]{1,0:T(8,128)(2,1)S(1)}, u32[]{:S(2)}, u32[]{:S(2)}) %collective-permute-start.9) | collective-permute-done | bytes 276512 | tf_op jit(solution)/shard_map/ppermute | solution.py:389
  154.5 3.1 %mix.2 = (bf16[1080,128]{1,0:T(8,128)(2,1)S(1)}, bf16[1080,128]{1,0:T(8,128)(2,1)S(1)}, bf16[1080,128]{1,0:T(8,128)(2,1)S(1)}) custom-call(bf16[1080,128]{1,0:T(8,128)(2,1)S(1)} %collective-permute-done.7.refs_0_, bf16[1080,128]{1,0:T(8,128)(2,1)S(1)} %collective-permute-done.8.refs_1_, bf16[1080,128]{1,0:T(8,128)(2,1)S(1)} %collective-permute-done.9.refs_2_, ...), custom_call_target="tpu_custom_call" | custom-call | flops 566231040 | bytes 10000000 | tf_op jit(solution)/shard_map/mix/pallas_call | solution.py:351
  161.5 3.4 %mix.3 = (bf16[1080,128]{1,0:T(8,128)(2,1)S(1)}, bf16[1080,128]{1,0:T(8,128)(2,1)S(1)}, bf16[1080,128]{1,0:T(8,128)(2,1)S(1)}, bf16[1080,128]{1,0:T(8,128)(2,1)S(1)}, bf16[1080,128]{1,0:T(8,128)(2,1)S(1)}) custom-call(bf16[1080,128]{1,0:T(8,128)(2,1)S(1)} %collective-permute-done.13.refs_0_, bf16[1080,128]{1,0:T(8,128)(2,1)S(1)} %collective-permute-done.14.refs_1_, ...), custom_call_target="tpu_custom_call" | custom-call | flops 566231040 | bytes 10000000 | tf_op jit(solution)/shard_map/mix/pallas_call | solution.py:351
  164.9 3.2 %collective-permute-start.17 = (bf16[1080,128]{1,0:T(8,128)(2,1)S(1)}, bf16[1080,128]{1,0:T(8,128)(2,1)S(1)}, u32[]{:S(2)}, u32[]{:S(2)}) collective-permute-start(bf16[1080,128]{1,0:T(8,128)(2,1)S(1)} %get-tuple-element.96), channel_id=1, source_target_pairs={{0,96},{16,112},{32,0},{48,16},{64,32},{80,48},{96,64},{112,80},{1... | collective-permute-start | bytes 829448 | tf_op jit(solution)/shard_map/ppermute | solution.py:389
  169.9 2.6 collective-permute-done.11.refs_1_
  174.5 4.0 %collective-permute-done.12.refs_2_ = bf16[1080,128]{1,0:T(8,128)(2,1)S(1)} collective-permute-done((bf16[1080,128]{1,0:T(8,128)(2,1)S(1)}, bf16[1080,128]{1,0:T(8,128)(2,1)S(1)}, u32[]{:S(2)}, u32[]{:S(2)}) %collective-permute-start.12) | collective-permute-done | bytes 276512 | tf_op jit(solution)/shard_map/ppermute | solution.py:389
  180.7 5.4 %collective-permute-done.18.refs_4_ = bf16[1080,128]{1,0:T(8,128)(2,1)S(1)} collective-permute-done((bf16[1080,128]{1,0:T(8,128)(2,1)S(1)}, bf16[1080,128]{1,0:T(8,128)(2,1)S(1)}, u32[]{:S(2)}, u32[]{:S(2)}) %collective-permute-start.18) | collective-permute-done | bytes 276512 | tf_op jit(solution)/shard_map/ppermute | solution.py:389
  186.1 6.6 %inverse_legendre.1 = bf16[9216,128]{1,0:T(8,128)(2,1)S(1)} custom-call(s32[8]{0:T(128)S(1)} %compare_select_fusion.4.src_ref, s32[8]{0:T(128)S(1)} %in_order.3.dest_ref, bf16[1080,128]{1,0:T(8,128)(2,1)S(1)} %collective-permute-done.10.refs_0_, bf16[1080,128]{1,0:T(8,128)(2,1)S(1)} %collective-permute-done.11.refs_1_, ...), custom_call_target="tpu_custom_call" | custom-call | flops 1811939328 | bytes 12000000 | tf_op jit(solution)/shard_map/inverse_legendre/pallas_call | solution.py:328
  192.7 37.4 %all_to_all.32 = bf16[128,72,128]{2,1,0:T(8,128)(2,1)S(1)} all-to-all(bf16[128,72,128]{2,1,0:T(8,128)(2,1)S(1)} %bitcast.9), channel_id=1, replica_groups=mesh['lat'=8,'lon'=16] {'lat','lon'}, dimensions={0} | all-to-all | bytes 4718592 | tf_op jit(solution)/shard_map/all_to_all | solution.py:383
  230.1 6.0 %inverse_dft.1 = bf16[16,6,96,128]{3,2,1,0:T(8,128)(2,1)S(1)} custom-call(bf16[9216,128]{1,0:T(8,128)(2,1)S(1)} %bitcast.11, bf16[1536,1536]{1,0:T(8,128)(2,1)S(1)} %bitcast.14), custom_call_target="tpu_custom_call" | custom-call | flops 3623878656 | bytes 10000000 | tf_op jit(solution)/shard_map/inverse_dft/pallas_call | solution.py:367
  236.2 34.6 %all_to_all.33 = bf16[96,96,128]{2,1,0:T(8,128)(2,1)S(1)} all-to-all(bf16[96,96,128]{2,1,0:T(8,128)(2,1)S(1)} %bitcast.12), channel_id=1, replica_groups=mesh['lat'=8,'lon'=16] {'lon'}, dimensions={0} | all-to-all | bytes 4718592 | tf_op jit(solution)/shard_map/all_to_all | solution.py:383
  (65 shorter events, 29.2 us)
Async XLA Ops:
  5.3 12.1 %copy-start.8 = (bf16[90,90,128]{2,1,0:T(8,128)(2,1)S(1)}, bf16[90,90,128]{2,1,0:T(8,128)(2,1)}, u32[]{:S(2)}) copy-start(bf16[90,90,128]{2,1,0:T(8,128)(2,1)} %param.10) | copy-start | bytes 6220804
  8.1 27.5 %collective-permute-start.4 = (bf16[6,96,768]{2,1,0:T(8,128)(2,1)}, bf16[6,96,768]{2,1,0:T(8,128)(2,1)S(1)}, u32[]{:S(2)}, u32[]{:S(2)}) collective-permute-start(bf16[6,96,768]{2,1,0:T(8,128)(2,1)} %cut.4), channel_id=1, source_target_pairs={{0,64},{16,80},{32,96},{48,112},{64,0},{80,16},{96,32},{112,48},{1... | collective-permute-start | bytes 2654216 | tf_op jit(solution)/shard_map/ppermute | solution.py:389
  11.2 39.2 %collective-permute-start = (bf16[6,96,768]{2,1,0:T(8,128)(2,1)}, bf16[6,96,768]{2,1,0:T(8,128)(2,1)}, u32[]{:S(2)}, u32[]{:S(2)}) collective-permute-start(bf16[6,96,768]{2,1,0:T(8,128)(2,1)} %get-tuple-element.64), channel_id=1, source_target_pairs={{0,16},{16,32},{32,48},{48,64},{64,80},{80,96},{96,112},{112,0},{1... | collective-permute-start | bytes 2654216 | tf_op jit(solution)/shard_map/ppermute | solution.py:389
  11.2 39.2 %collective-permute-start.1 = (bf16[6,96,768]{2,1,0:T(8,128)(2,1)}, bf16[6,96,768]{2,1,0:T(8,128)(2,1)}, u32[]{:S(2)}, u32[]{:S(2)}) collective-permute-start(bf16[6,96,768]{2,1,0:T(8,128)(2,1)} %get-tuple-element.65), channel_id=1, source_target_pairs={{0,112},{16,0},{32,16},{48,32},{64,48},{80,64},{96,80},{112,96},{1... | collective-permute-start | bytes 2654216 | tf_op jit(solution)/shard_map/ppermute | solution.py:389
  14.2 36.4 %collective-permute-start.2 = (bf16[6,96,768]{2,1,0:T(8,128)(2,1)}, bf16[6,96,768]{2,1,0:T(8,128)(2,1)}, u32[]{:S(2)}, u32[]{:S(2)}) collective-permute-start(bf16[6,96,768]{2,1,0:T(8,128)(2,1)} %get-tuple-element.66), channel_id=1, source_target_pairs={{0,32},{16,48},{32,64},{48,80},{64,96},{80,112},{96,0},{112,16},{1... | collective-permute-start | bytes 2654216 | tf_op jit(solution)/shard_map/ppermute | solution.py:389
  14.2 45.8 %collective-permute-start.3 = (bf16[6,96,768]{2,1,0:T(8,128)(2,1)}, bf16[6,96,768]{2,1,0:T(8,128)(2,1)}, u32[]{:S(2)}, u32[]{:S(2)}) collective-permute-start(bf16[6,96,768]{2,1,0:T(8,128)(2,1)} %get-tuple-element.67), channel_id=1, source_target_pairs={{0,96},{16,112},{32,0},{48,16},{64,32},{80,48},{96,64},{112,80},{1... | collective-permute-start | bytes 2654216 | tf_op jit(solution)/shard_map/ppermute | solution.py:389
  19.0 42.1 %all-to-all-start = ((bf16[96,96,128]{2,1,0:T(8,128)(2,1)}), bf16[96,96,128]{2,1,0:T(8,128)(2,1)S(1)}, u32[]{:S(2)}, u32[]{:S(2)}) async-start(bf16[96,96,128]{2,1,0:T(8,128)(2,1)} %pad.8), calls=%async_computation | async-start | bytes 4718592 | tf_op jit(solution)/shard_map/all_to_all | solution.py:383
  35.6 28.9 %copy-start.10 = (f32[90]{0:T(128)S(1)}, f32[90]{0:T(128)}, u32[]{:S(2)}) copy-start(f32[90]{0:T(128)} %param.12) | copy-start | bytes 1084
  35.6 29.0 %copy-start.11 = (s32[8]{0:T(128)S(1)}, s32[8]{0:T(128)}, u32[]{:S(2)}) copy-start(s32[8]{0:T(128)} %constant.59) | copy-start | bytes 100
  61.1 23.9 %collective-permute-start.5 = (bf16[6,96,768]{2,1,0:T(8,128)(2,1)}, bf16[6,96,768]{2,1,0:T(8,128)(2,1)}, u32[]{:S(2)}, u32[]{:S(2)}) collective-permute-start(bf16[6,96,768]{2,1,0:T(8,128)(2,1)} %get-tuple-element.72), channel_id=1, source_target_pairs={{0,48},{16,64},{32,80},{48,96},{64,112},{80,0},{96,16},{112,32},{1... | collective-permute-start | bytes 2654216 | tf_op jit(solution)/shard_map/ppermute | solution.py:389
  62.4 39.7 %collective-permute-start.6 = (bf16[6,96,768]{2,1,0:T(8,128)(2,1)}, bf16[6,96,768]{2,1,0:T(8,128)(2,1)}, u32[]{:S(2)}, u32[]{:S(2)}) collective-permute-start(bf16[6,96,768]{2,1,0:T(8,128)(2,1)} %get-tuple-element.73), channel_id=1, source_target_pairs={{0,80},{16,96},{32,112},{48,0},{64,16},{80,32},{96,48},{112,64},{1... | collective-permute-start | bytes 2654216 | tf_op jit(solution)/shard_map/ppermute | solution.py:389
  74.1 50.3 %all-to-all-start.1 = ((bf16[128,72,128]{2,1,0:T(8,128)(2,1)}), bf16[128,72,128]{2,1,0:T(8,128)(2,1)S(1)}, u32[]{:S(2)}, u32[]{:S(2)}) async-start(bf16[128,72,128]{2,1,0:T(8,128)(2,1)} %bitcast.10), calls=%async_computation.1 | async-start | bytes 4718592 | tf_op jit(solution)/shard_map/all_to_all | solution.py:383
  125.6 29.0 %copy-start.2 = (bf16[90,128,128]{2,1,0:T(8,128)(2,1)S(1)}, bf16[90,128,128]{2,1,0:T(8,128)(2,1)}, u32[]{:S(2)}) copy-start(bf16[90,128,128]{2,1,0:T(8,128)(2,1)} %refs_5_.1) | copy-start | bytes 8847364
  125.6 29.0 %copy-start.3 = (bf16[90,128,128]{2,1,0:T(8,128)(2,1)S(1)}, bf16[90,128,128]{2,1,0:T(8,128)(2,1)}, u32[]{:S(2)}) copy-start(bf16[90,128,128]{2,1,0:T(8,128)(2,1)} %refs_6_.1) | copy-start | bytes 8847364
  132.3 11.2 %collective-permute-start.7 = (bf16[1080,128]{1,0:T(8,128)(2,1)S(1)}, bf16[1080,128]{1,0:T(8,128)(2,1)S(1)}, u32[]{:S(2)}, u32[]{:S(2)}) collective-permute-start(bf16[1080,128]{1,0:T(8,128)(2,1)S(1)} %get-tuple-element.85), channel_id=1, source_target_pairs={{0,64},{16,80},{32,96},{48,112},{64,0},{80,16},{96,32},{112,48},{1... | collective-permute-start | bytes 829448 | tf_op jit(solution)/shard_map/ppermute | solution.py:389
  134.8 13.0 %collective-permute-start.8 = (bf16[1080,128]{1,0:T(8,128)(2,1)S(1)}, bf16[1080,128]{1,0:T(8,128)(2,1)S(1)}, u32[]{:S(2)}, u32[]{:S(2)}) collective-permute-start(bf16[1080,128]{1,0:T(8,128)(2,1)S(1)} %get-tuple-element.86), channel_id=1, source_target_pairs={{0,48},{16,64},{32,80},{48,96},{64,112},{80,0},{96,16},{112,32},{1... | collective-permute-start | bytes 829448 | tf_op jit(solution)/shard_map/ppermute | solution.py:389
  135.6 18.9 %collective-permute-start.9 = (bf16[1080,128]{1,0:T(8,128)(2,1)S(1)}, bf16[1080,128]{1,0:T(8,128)(2,1)S(1)}, u32[]{:S(2)}, u32[]{:S(2)}) collective-permute-start(bf16[1080,128]{1,0:T(8,128)(2,1)S(1)} %get-tuple-element.87), channel_id=1, source_target_pairs={{0,80},{16,96},{32,112},{48,0},{64,16},{80,32},{96,48},{112,64},{1... | collective-permute-start | bytes 829448 | tf_op jit(solution)/shard_map/ppermute | solution.py:389
  138.0 21.7 %collective-permute-start.13 = (bf16[1080,128]{1,0:T(8,128)(2,1)S(1)}, bf16[1080,128]{1,0:T(8,128)(2,1)S(1)}, u32[]{:S(2)}, u32[]{:S(2)}) collective-permute-start(bf16[1080,128]{1,0:T(8,128)(2,1)S(1)} %get-tuple-element.91), channel_id=1, source_target_pairs={{0,32},{16,48},{32,64},{48,80},{64,96},{80,112},{96,0},{112,16},{1... | collective-permute-start | bytes 829448 | tf_op jit(solution)/shard_map/ppermute | solution.py:389
  138.8 22.4 %collective-permute-start.14 = (bf16[1080,128]{1,0:T(8,128)(2,1)S(1)}, bf16[1080,128]{1,0:T(8,128)(2,1)S(1)}, u32[]{:S(2)}, u32[]{:S(2)}) collective-permute-start(bf16[1080,128]{1,0:T(8,128)(2,1)S(1)} %get-tuple-element.92), channel_id=1, source_target_pairs={{0,96},{16,112},{32,0},{48,16},{64,32},{80,48},{96,64},{112,80},{1... | collective-permute-start | bytes 829448 | tf_op jit(solution)/shard_map/ppermute | solution.py:389
  143.5 17.9 %collective-permute-start.15 = (bf16[1080,128]{1,0:T(8,128)(2,1)S(1)}, bf16[1080,128]{1,0:T(8,128)(2,1)S(1)}, u32[]{:S(2)}, u32[]{:S(2)}) collective-permute-start(bf16[1080,128]{1,0:T(8,128)(2,1)S(1)} %get-tuple-element.93), channel_id=1, source_target_pairs={{0,16},{16,32},{32,48},{48,64},{64,80},{80,96},{96,112},{112,0},{1... | collective-permute-start | bytes 829448 | tf_op jit(solution)/shard_map/ppermute | solution.py:389
  147.8 13.6 %collective-permute-start.16 = (bf16[1080,128]{1,0:T(8,128)(2,1)S(1)}, bf16[1080,128]{1,0:T(8,128)(2,1)S(1)}, u32[]{:S(2)}, u32[]{:S(2)}) collective-permute-start(bf16[1080,128]{1,0:T(8,128)(2,1)S(1)} %get-tuple-element.94), channel_id=1, source_target_pairs={{0,112},{16,0},{32,16},{48,32},{64,48},{80,64},{96,80},{112,96},{1... | collective-permute-start | bytes 829448 | tf_op jit(solution)/shard_map/ppermute | solution.py:389
  157.6 11.2 %collective-permute-start.10 = (bf16[1080,128]{1,0:T(8,128)(2,1)S(1)}, bf16[1080,128]{1,0:T(8,128)(2,1)S(1)}, u32[]{:S(2)}, u32[]{:S(2)}) collective-permute-start(bf16[1080,128]{1,0:T(8,128)(2,1)S(1)} %get-tuple-element.88), channel_id=1, source_target_pairs={{0,64},{16,80},{32,96},{48,112},{64,0},{80,16},{96,32},{112,48},{1... | collective-permute-start | bytes 829448 | tf_op jit(solution)/shard_map/ppermute | solution.py:389
  159.7 12.9 %collective-permute-start.11 = (bf16[1080,128]{1,0:T(8,128)(2,1)S(1)}, bf16[1080,128]{1,0:T(8,128)(2,1)S(1)}, u32[]{:S(2)}, u32[]{:S(2)}) collective-permute-start(bf16[1080,128]{1,0:T(8,128)(2,1)S(1)} %get-tuple-element.89), channel_id=1, source_target_pairs={{0,80},{16,96},{32,112},{48,0},{64,16},{80,32},{96,48},{112,64},{1... | collective-permute-start | bytes 829448 | tf_op jit(solution)/shard_map/ppermute | solution.py:389
  161.2 17.3 %collective-permute-start.12 = (bf16[1080,128]{1,0:T(8,128)(2,1)S(1)}, bf16[1080,128]{1,0:T(8,128)(2,1)S(1)}, u32[]{:S(2)}, u32[]{:S(2)}) collective-permute-start(bf16[1080,128]{1,0:T(8,128)(2,1)S(1)} %get-tuple-element.90), channel_id=1, source_target_pairs={{0,48},{16,64},{32,80},{48,96},{64,112},{80,0},{96,16},{112,32},{1... | collective-permute-start | bytes 829448 | tf_op jit(solution)/shard_map/ppermute | solution.py:389
  161.4 24.7 %copy-start.7 = (bf16[6,96,768]{2,1,0:T(8,128)(2,1)S(1)}, bf16[6,96,768]{2,1,0:T(8,128)(2,1)}, u32[]{:S(2)}) copy-start(bf16[6,96,768]{2,1,0:T(8,128)(2,1)} %get-tuple-element.77.refs_0_.refs_8_) | copy-start | bytes 2654212
  161.4 68.7 %slice-start = ((s8[4718592]{0:T(1024)(128)(4,1)}), s8[524288]{0:T(1024)(128)(4,1)S(1)}, s32[]{:S(2)}) async-start(s8[4718592]{0:T(1024)(128)(4,1)} %bitcast.13), calls=%async_computation.4 | async-start | bytes 1048576
  164.9 15.8 %collective-permute-start.17 = (bf16[1080,128]{1,0:T(8,128)(2,1)S(1)}, bf16[1080,128]{1,0:T(8,128)(2,1)S(1)}, u32[]{:S(2)}, u32[]{:S(2)}) collective-permute-start(bf16[1080,128]{1,0:T(8,128)(2,1)S(1)} %get-tuple-element.96), channel_id=1, source_target_pairs={{0,96},{16,112},{32,0},{48,16},{64,32},{80,48},{96,64},{112,80},{1... | collective-permute-start | bytes 829448 | tf_op jit(solution)/shard_map/ppermute | solution.py:389
  168.1 18.0 %collective-permute-start.18 = (bf16[1080,128]{1,0:T(8,128)(2,1)S(1)}, bf16[1080,128]{1,0:T(8,128)(2,1)S(1)}, u32[]{:S(2)}, u32[]{:S(2)}) collective-permute-start(bf16[1080,128]{1,0:T(8,128)(2,1)S(1)} %get-tuple-element.97), channel_id=1, source_target_pairs={{0,32},{16,48},{32,64},{48,80},{64,96},{80,112},{96,0},{112,16},{1... | collective-permute-start | bytes 829448 | tf_op jit(solution)/shard_map/ppermute | solution.py:389
  168.8 17.3 %collective-permute-start.19 = (bf16[1080,128]{1,0:T(8,128)(2,1)S(1)}, bf16[1080,128]{1,0:T(8,128)(2,1)S(1)}, u32[]{:S(2)}, u32[]{:S(2)}) collective-permute-start(bf16[1080,128]{1,0:T(8,128)(2,1)S(1)} %get-tuple-element.98), channel_id=1, source_target_pairs={{0,112},{16,0},{32,16},{48,32},{64,48},{80,64},{96,80},{112,96},{1... | collective-permute-start | bytes 829448 | tf_op jit(solution)/shard_map/ppermute | solution.py:389
  172.6 13.6 %collective-permute-start.20 = (bf16[1080,128]{1,0:T(8,128)(2,1)S(1)}, bf16[1080,128]{1,0:T(8,128)(2,1)S(1)}, u32[]{:S(2)}, u32[]{:S(2)}) collective-permute-start(bf16[1080,128]{1,0:T(8,128)(2,1)S(1)} %get-tuple-element.99), channel_id=1, source_target_pairs={{0,16},{16,32},{32,48},{48,64},{64,80},{80,96},{96,112},{112,0},{1... | collective-permute-start | bytes 829448 | tf_op jit(solution)/shard_map/ppermute | solution.py:389
  186.1 44.0 %slice-start.1 = ((s8[4718592]{0:T(1024)(128)(4,1)}), s8[4194304]{0:T(1024)(128)(4,1)S(1)}, s32[]{:S(2)}) async-start(s8[4718592]{0:T(1024)(128)(4,1)} %bitcast.13), calls=%async_computation.5 | async-start | bytes 8388608
  236.2 34.6 %copy-start.9 = (bf16[90,90,128]{2,1,0:T(8,128)(2,1)S(1)}, bf16[90,90,128]{2,1,0:T(8,128)(2,1)}, u32[]{:S(2)}) copy-start(bf16[90,90,128]{2,1,0:T(8,128)(2,1)} %param.10) | copy-start | bytes 6220804
  (6 other events, 11.9 us)

commit v4 on v2

--- a/solution.py
+++ b/solution.py
@@ -401,7 +401,8 @@
         return value
 
     dest = in_order(end(dest, (1, 2, 3, 4, 7)))
-    cuts[5:7], rows, dest = lax.optimization_barrier((cuts[5:7], rows, dest))
+    cuts[5:7], dest = lax.optimization_barrier((cuts[5:7], dest))
+    rows, dest = lax.optimization_barrier((rows, dest))
     spectrum = dft(quad, rows.reshape(LON, OWN, PAD, CH), jnp.asarray(forward_table))
     dest = in_order(end(dest, (5, 6)))
     weighted = swap(spectrum, ("lat", "lon"))

time: 272 us -> 272 us (level)
  starting transfers between devices: 50.6 us -> 57.6 us
  waiting for transfers between devices: 95.8 us -> 89.1 us
    all_to_all x2, waiting for transfers between devices: 28.2 us -> 21.5 us  [swap(): return lax.all_to_all(x, axes, split_axis=0, concat_axis=0, tiled=True)]
    ppermute x21, starting transfers between devices: 31.4 us -> 37.3 us  [shifted(): lax.ppermute(part, 'lat', [(i, (i + shift) % LAT) for i in range(LAT)])]
  transfers between devices with their start and end apart: 23 -> 23, of which waited for: 16 -> 15; matrix products, arithmetic and copies ran while one was open for 1% -> 1% of each run, Pallas kernels for 7% -> 7%
where the time goes in v4:
time: 272 us; the launch traced here: 271 us
  waiting for transfers between devices  89.1 us (33%)
  blocking collectives  72 us (26%)
  starting transfers between devices  57.6 us (21%)
  Pallas kernels  42.4 us (16%)
  local copies, waits for them, and re-layouts  6.7 us (2%)
  other arithmetic  3.22 us (1%)
    all_to_all x2, blocking collectives, swap(): return lax.all_to_all(x, axes, split_axis=0, concat_axis=0, tiled=True)  72 us
    ppermute x21, waiting for transfers between devices, shifted(): lax.ppermute(part, 'lat', [(i, (i + shift) % LAT) for i in range(LAT)])  67.6 us
    ppermute x21, starting transfers between devices, shifted(): lax.ppermute(part, 'lat', [(i, (i + shift) % LAT) for i in range(LAT)])  37.3 us
    all_to_all x2, waiting for transfers between devices, swap(): return lax.all_to_all(x, axes, split_axis=0, concat_axis=0, tiled=True)  21.5 us
    all_to_all x2, starting transfers between devices, swap(): return lax.all_to_all(x, axes, split_axis=0, concat_axis=0, tiled=True)  20.3 us
    pallas_call x2, Pallas kernels, legendre_call(): pl.pallas_call(kernel, grid=(OWN,), in_specs=[pl.BlockSpec(memory_space=p...  13.3 us
    pallas_call x2, Pallas kernels, cut(): pl.pallas_call(cut_kernel, grid_spec=pltpu.PrefetchScalarGridSpec(num_sca...  8.47 us
    pallas_call x2, Pallas kernels, mix(): pl.pallas_call(mix_kernel, grid=(BAND // STEP,), in_specs=[whole((PART, C...  6.49 us
  transfers between devices with their start and end apart: 23, of which 15 were waited for; matrix products, arithmetic and copies ran while one was open for 1% of the time, Pallas kernels for 7%

profile of v4, /device:TPU:0, one launch (start us, length us, event | category | flops | bytes accessed | tf_op | source)
XLA Modules:
  0.0 271.3 jit_solution(6869439208491027422)
XLA Ops:
  1.3 4.2 %cut.2 = (bf16[6,96,768]{2,1,0:T(8,128)(2,1)}, bf16[6,96,768]{2,1,0:T(8,128)(2,1)}, bf16[6,96,768]{2,1,0:T(8,128)(2,1)}, bf16[6,96,768]{2,1,0:T(8,128)(2,1)}) custom-call(s32[5]{0:T(128)} %get-tuple-element.100.scalars_ref, bf16[45,90,720]{2,1,0:T(8,128)(2,1)} %bitcast.15, bf16[45,90,720]{2,1,0:T(8,128)(2,1)} %bitcast.16, bf16[45,90,720]{2,1,0:T(8,128)(2,1)} %bitcast.17, ...), custom_call_target="tpu_custom_call" | custom-call | flops 4000000 | bytes 6800000 | tf_op jit(solution)/shard_map/cut/pallas_call | solution.py:251
  5.5 3.0 %collective-permute-start.1 = (bf16[6,96,768]{2,1,0:T(8,128)(2,1)}, bf16[6,96,768]{2,1,0:T(8,128)(2,1)}, u32[]{:S(2)}, u32[]{:S(2)}) collective-permute-start(bf16[6,96,768]{2,1,0:T(8,128)(2,1)} %get-tuple-element.64), channel_id=1, source_target_pairs={{0,112},{16,0},{32,16},{48,32},{64,48},{80,64},{96,80},{112,96},{1... | collective-permute-start | bytes 2654216 | tf_op jit(solution)/shard_map/ppermute | solution.py:368
  8.8 2.9 %collective-permute-start.3 = (bf16[6,96,768]{2,1,0:T(8,128)(2,1)}, bf16[6,96,768]{2,1,0:T(8,128)(2,1)}, u32[]{:S(2)}, u32[]{:S(2)}) collective-permute-start(bf16[6,96,768]{2,1,0:T(8,128)(2,1)} %get-tuple-element.66), channel_id=1, source_target_pairs={{0,96},{16,112},{32,0},{48,16},{64,32},{80,48},{96,64},{112,80},{1... | collective-permute-start | bytes 2654216 | tf_op jit(solution)/shard_map/ppermute | solution.py:368
  11.7 4.3 %cut.3 = (bf16[6,96,768]{2,1,0:T(8,128)(2,1)}, bf16[6,96,768]{2,1,0:T(8,128)(2,1)}, bf16[6,96,768]{2,1,0:T(8,128)(2,1)}, bf16[6,96,768]{2,1,0:T(8,128)(2,1)}) custom-call(s32[5]{0:T(128)} %get-tuple-element.99.scalars_ref, bf16[45,90,720]{2,1,0:T(8,128)(2,1)} %bitcast.19, bf16[45,90,720]{2,1,0:T(8,128)(2,1)} %bitcast.20, bf16[45,90,720]{2,1,0:T(8,128)(2,1)} %bitcast.21, ...), custom_call_target="tpu_custom_call" | custom-call | flops 4000000 | bytes 6800000 | tf_op jit(solution)/shard_map/cut/pallas_call | solution.py:251
  18.3 8.2 %all-to-all-start = ((bf16[96,96,128]{2,1,0:T(8,128)(2,1)}), bf16[96,96,128]{2,1,0:T(8,128)(2,1)S(1)}, u32[]{:S(2)}, u32[]{:S(2)}) async-start(bf16[96,96,128]{2,1,0:T(8,128)(2,1)} %pad.8), calls=%async_computation | async-start | bytes 4718592 | tf_op jit(solution)/shard_map/all_to_all | solution.py:362
  28.1 4.6 %collective-permute-done.2.refs_3_.refs_11_ = bf16[6,96,768]{2,1,0:T(8,128)(2,1)} collective-permute-done((bf16[6,96,768]{2,1,0:T(8,128)(2,1)}, bf16[6,96,768]{2,1,0:T(8,128)(2,1)}, u32[]{:S(2)}, u32[]{:S(2)}) %collective-permute-start.2) | collective-permute-done | bytes 884768 | tf_op jit(solution)/shard_map/ppermute | solution.py:368
  32.7 15.3 %collective-permute-done.3.refs_4_.refs_12_ = bf16[6,96,768]{2,1,0:T(8,128)(2,1)} collective-permute-done((bf16[6,96,768]{2,1,0:T(8,128)(2,1)}, bf16[6,96,768]{2,1,0:T(8,128)(2,1)}, u32[]{:S(2)}, u32[]{:S(2)}) %collective-permute-start.3) | collective-permute-done | bytes 884768 | tf_op jit(solution)/shard_map/ppermute | solution.py:368
  48.0 3.4 %collective-permute-done.4.refs_7_.refs_15_ = bf16[6,96,768]{2,1,0:T(8,128)(2,1)} collective-permute-done((bf16[6,96,768]{2,1,0:T(8,128)(2,1)}, bf16[6,96,768]{2,1,0:T(8,128)(2,1)}, u32[]{:S(2)}, u32[]{:S(2)}) %collective-permute-start.4) | collective-permute-done | bytes 884768 | tf_op jit(solution)/shard_map/ppermute | solution.py:368
  52.6 8.8 %collective-permute-start.6 = (bf16[6,96,768]{2,1,0:T(8,128)(2,1)}, bf16[6,96,768]{2,1,0:T(8,128)(2,1)}, u32[]{:S(2)}, u32[]{:S(2)}) collective-permute-start(bf16[6,96,768]{2,1,0:T(8,128)(2,1)} %get-tuple-element.72), channel_id=1, source_target_pairs={{0,80},{16,96},{32,112},{48,0},{64,16},{80,32},{96,48},{112,64},{1... | collective-permute-start | bytes 2654216 | tf_op jit(solution)/shard_map/ppermute | solution.py:368
  61.5 2.3 copy-done.3
  63.8 5.8 %dft.1 = bf16[9216,128]{1,0:T(8,128)(2,1)S(1)} custom-call(f32[6]{0:T(128)S(1)} %pad_dynamic-slice_fusion.quad_ref, bf16[16,6,96,128]{3,2,1,0:T(8,128)(2,1)S(1)} %bitcast.8, bf16[1536,1536]{1,0:T(8,128)(2,1)S(1)} %copy-done.3), custom_call_target="tpu_custom_call" | custom-call | flops 1000000 | bytes 100000 | tf_op jit(solution)/shard_map/dft/pallas_call | solution.py:286
  71.1 12.1 %all-to-all-start.1 = ((bf16[128,72,128]{2,1,0:T(8,128)(2,1)}), bf16[128,72,128]{2,1,0:T(8,128)(2,1)S(1)}, u32[]{:S(2)}, u32[]{:S(2)}) async-start(bf16[128,72,128]{2,1,0:T(8,128)(2,1)} %bitcast.10), calls=%async_computation.1 | async-start | bytes 4718592 | tf_op jit(solution)/shard_map/all_to_all | solution.py:362
  83.2 17.1 %collective-permute-done.6.refs_6_.refs_14_ = bf16[6,96,768]{2,1,0:T(8,128)(2,1)} collective-permute-done((bf16[6,96,768]{2,1,0:T(8,128)(2,1)}, bf16[6,96,768]{2,1,0:T(8,128)(2,1)}, u32[]{:S(2)}, u32[]{:S(2)}) %collective-permute-start.6) | collective-permute-done | bytes 884768 | tf_op jit(solution)/shard_map/ppermute | solution.py:368
  101.4 21.5 %all-to-all-done.1 = bf16[128,72,128]{2,1,0:T(8,128)(2,1)S(1)} async-done(((bf16[128,72,128]{2,1,0:T(8,128)(2,1)}), bf16[128,72,128]{2,1,0:T(8,128)(2,1)S(1)}, u32[]{:S(2)}, u32[]{:S(2)}) %all-to-all-start.1) | async-done | bytes 2359328 | tf_op jit(solution)/shard_map/all_to_all | solution.py:362
  124.1 6.7 %legendre.1 = (bf16[1080,128]{1,0:T(8,128)(2,1)S(1)}, bf16[1080,128]{1,0:T(8,128)(2,1)S(1)}, bf16[1080,128]{1,0:T(8,128)(2,1)S(1)}, bf16[1080,128]{1,0:T(8,128)(...) custom-call(s32[8]{0:T(128)S(1)} %compare_select_fusion.6.src_ref, ...), custom_call_target="tpu_custom_call" | custom-call | flops 1811939328 | bytes 12000000 | tf_op jit(solution)/shard_map/legendre/pallas_call | solution.py:307
  134.1 2.2 collective-permute-start.9
  139.5 2.6 collective-permute-done.7.refs_0_
  142.0 3.3 %collective-permute-done.8.refs_1_ = bf16[1080,128]{1,0:T(8,128)(2,1)S(1)} collective-permute-done((bf16[1080,128]{1,0:T(8,128)(2,1)S(1)}, bf16[1080,128]{1,0:T(8,128)(2,1)S(1)}, u32[]{:S(2)}, u32[]{:S(2)}) %collective-permute-start.8) | collective-permute-done | bytes 276512 | tf_op jit(solution)/shard_map/ppermute | solution.py:368
  145.4 2.8 %collective-permute-start.16 = (bf16[1080,128]{1,0:T(8,128)(2,1)S(1)}, bf16[1080,128]{1,0:T(8,128)(2,1)S(1)}, u32[]{:S(2)}, u32[]{:S(2)}) collective-permute-start(bf16[1080,128]{1,0:T(8,128)(2,1)S(1)} %get-tuple-element.92), channel_id=1, source_target_pairs={{0,112},{16,0},{32,16},{48,32},{64,48},{80,64},{96,80},{112,96},{1... | collective-permute-start | bytes 829448 | tf_op jit(solution)/shard_map/ppermute | solution.py:368
  148.2 4.5 %collective-permute-done.9.refs_2_ = bf16[1080,128]{1,0:T(8,128)(2,1)S(1)} collective-permute-done((bf16[1080,128]{1,0:T(8,128)(2,1)S(1)}, bf16[1080,128]{1,0:T(8,128)(2,1)S(1)}, u32[]{:S(2)}, u32[]{:S(2)}) %collective-permute-start.9) | collective-permute-done | bytes 276512 | tf_op jit(solution)/shard_map/ppermute | solution.py:368
  152.7 3.1 %mix.2 = (bf16[1080,128]{1,0:T(8,128)(2,1)S(1)}, bf16[1080,128]{1,0:T(8,128)(2,1)S(1)}, bf16[1080,128]{1,0:T(8,128)(2,1)S(1)}) custom-call(bf16[1080,128]{1,0:T(8,128)(2,1)S(1)} %collective-permute-done.7.refs_0_, bf16[1080,128]{1,0:T(8,128)(2,1)S(1)} %collective-permute-done.8.refs_1_, bf16[1080,128]{1,0:T(8,128)(2,1)S(1)} %collective-permute-done.9.refs_2_, ...), custom_call_target="tpu_custom_call" | custom-call | flops 566231040 | bytes 10000000 | tf_op jit(solution)/shard_map/mix/pallas_call | solution.py:330
  155.8 2.5 collective-permute-start.10
  160.1 3.4 %mix.3 = (bf16[1080,128]{1,0:T(8,128)(2,1)S(1)}, bf16[1080,128]{1,0:T(8,128)(2,1)S(1)}, bf16[1080,128]{1,0:T(8,128)(2,1)S(1)}, bf16[1080,128]{1,0:T(8,128)(2,1)S(1)}, bf16[1080,128]{1,0:T(8,128)(2,1)S(1)}) custom-call(bf16[1080,128]{1,0:T(8,128)(2,1)S(1)} %collective-permute-done.13.refs_0_, bf16[1080,128]{1,0:T(8,128)(2,1)S(1)} %collective-permute-done.14.refs_1_, ...), custom_call_target="tpu_custom_call" | custom-call | flops 566231040 | bytes 10000000 | tf_op jit(solution)/shard_map/mix/pallas_call | solution.py:330
  163.5 3.0 %collective-permute-start.17 = (bf16[1080,128]{1,0:T(8,128)(2,1)S(1)}, bf16[1080,128]{1,0:T(8,128)(2,1)S(1)}, u32[]{:S(2)}, u32[]{:S(2)}) collective-permute-start(bf16[1080,128]{1,0:T(8,128)(2,1)S(1)} %get-tuple-element.94), channel_id=1, source_target_pairs={{0,96},{16,112},{32,0},{48,16},{64,32},{80,48},{96,64},{112,80},{1... | collective-permute-start | bytes 829448 | tf_op jit(solution)/shard_map/ppermute | solution.py:368
  168.3 3.0 %collective-permute-done.11.refs_1_ = bf16[1080,128]{1,0:T(8,128)(2,1)S(1)} collective-permute-done((bf16[1080,128]{1,0:T(8,128)(2,1)S(1)}, bf16[1080,128]{1,0:T(8,128)(2,1)S(1)}, u32[]{:S(2)}, u32[]{:S(2)}) %collective-permute-start.11) | collective-permute-done | bytes 276512 | tf_op jit(solution)/shard_map/ppermute | solution.py:368
  172.9 3.0 %collective-permute-done.12.refs_2_ = bf16[1080,128]{1,0:T(8,128)(2,1)S(1)} collective-permute-done((bf16[1080,128]{1,0:T(8,128)(2,1)S(1)}, bf16[1080,128]{1,0:T(8,128)(2,1)S(1)}, u32[]{:S(2)}, u32[]{:S(2)}) %collective-permute-start.12) | collective-permute-done | bytes 276512 | tf_op jit(solution)/shard_map/ppermute | solution.py:368
  175.9 3.2 %collective-permute-done.17.refs_3_ = bf16[1080,128]{1,0:T(8,128)(2,1)S(1)} collective-permute-done((bf16[1080,128]{1,0:T(8,128)(2,1)S(1)}, bf16[1080,128]{1,0:T(8,128)(2,1)S(1)}, u32[]{:S(2)}, u32[]{:S(2)}) %collective-permute-start.17) | collective-permute-done | bytes 276512 | tf_op jit(solution)/shard_map/ppermute | solution.py:368
  179.1 5.5 %collective-permute-done.18.refs_4_ = bf16[1080,128]{1,0:T(8,128)(2,1)S(1)} collective-permute-done((bf16[1080,128]{1,0:T(8,128)(2,1)S(1)}, bf16[1080,128]{1,0:T(8,128)(2,1)S(1)}, u32[]{:S(2)}, u32[]{:S(2)}) %collective-permute-start.18) | collective-permute-done | bytes 276512 | tf_op jit(solution)/shard_map/ppermute | solution.py:368
  184.6 6.6 %inverse_legendre.1 = bf16[9216,128]{1,0:T(8,128)(2,1)S(1)} custom-call(s32[8]{0:T(128)S(1)} %compare_select_fusion.6.src_ref, s32[8]{0:T(128)S(1)} %in_order.3.dest_ref, bf16[1080,128]{1,0:T(8,128)(2,1)S(1)} %collective-permute-done.10.refs_0_, bf16[1080,128]{1,0:T(8,128)(2,1)S(1)} %collective-permute-done.11.refs_1_, ...), custom_call_target="tpu_custom_call" | custom-call | flops 1811939328 | bytes 12000000 | tf_op jit(solution)/shard_map/inverse_legendre/pallas_call | solution.py:307
  191.2 37.4 %all_to_all.32 = bf16[128,72,128]{2,1,0:T(8,128)(2,1)S(1)} all-to-all(bf16[128,72,128]{2,1,0:T(8,128)(2,1)S(1)} %bitcast.9), channel_id=1, replica_groups=mesh['lat'=8,'lon'=16] {'lat','lon'}, dimensions={0} | all-to-all | bytes 4718592 | tf_op jit(solution)/shard_map/all_to_all | solution.py:362
  228.6 6.0 %inverse_dft.1 = bf16[16,6,96,128]{3,2,1,0:T(8,128)(2,1)S(1)} custom-call(bf16[9216,128]{1,0:T(8,128)(2,1)S(1)} %bitcast.11, bf16[1536,1536]{1,0:T(8,128)(2,1)S(1)} %bitcast.14), custom_call_target="tpu_custom_call" | custom-call | flops 3623878656 | bytes 10000000 | tf_op jit(solution)/shard_map/inverse_dft/pallas_call | solution.py:346
  234.7 34.6 %all_to_all.33 = bf16[96,96,128]{2,1,0:T(8,128)(2,1)S(1)} all-to-all(bf16[96,96,128]{2,1,0:T(8,128)(2,1)S(1)} %bitcast.12), channel_id=1, replica_groups=mesh['lat'=8,'lon'=16] {'lon'}, dimensions={0} | all-to-all | bytes 4718592 | tf_op jit(solution)/shard_map/all_to_all | solution.py:362
  (59 shorter events, 24.3 us)
Async XLA Ops:
  5.5 21.0 %collective-permute-start = (bf16[6,96,768]{2,1,0:T(8,128)(2,1)}, bf16[6,96,768]{2,1,0:T(8,128)(2,1)S(1)}, u32[]{:S(2)}, u32[]{:S(2)}) collective-permute-start(bf16[6,96,768]{2,1,0:T(8,128)(2,1)} %get-tuple-element.63), channel_id=1, source_target_pairs={{0,16},{16,32},{32,48},{48,64},{64,80},{80,96},{96,112},{112,0},{1... | collective-permute-start | bytes 2654216 | tf_op jit(solution)/shard_map/ppermute | solution.py:368
  5.5 22.6 %collective-permute-start.1 = (bf16[6,96,768]{2,1,0:T(8,128)(2,1)}, bf16[6,96,768]{2,1,0:T(8,128)(2,1)}, u32[]{:S(2)}, u32[]{:S(2)}) collective-permute-start(bf16[6,96,768]{2,1,0:T(8,128)(2,1)} %get-tuple-element.64), channel_id=1, source_target_pairs={{0,112},{16,0},{32,16},{48,32},{64,48},{80,64},{96,80},{112,96},{1... | collective-permute-start | bytes 2654216 | tf_op jit(solution)/shard_map/ppermute | solution.py:368
  8.4 24.2 %collective-permute-start.2 = (bf16[6,96,768]{2,1,0:T(8,128)(2,1)}, bf16[6,96,768]{2,1,0:T(8,128)(2,1)}, u32[]{:S(2)}, u32[]{:S(2)}) collective-permute-start(bf16[6,96,768]{2,1,0:T(8,128)(2,1)} %get-tuple-element.65), channel_id=1, source_target_pairs={{0,32},{16,48},{32,64},{48,80},{64,96},{80,112},{96,0},{112,16},{1... | collective-permute-start | bytes 2654216 | tf_op jit(solution)/shard_map/ppermute | solution.py:368
  8.8 39.2 %collective-permute-start.3 = (bf16[6,96,768]{2,1,0:T(8,128)(2,1)}, bf16[6,96,768]{2,1,0:T(8,128)(2,1)}, u32[]{:S(2)}, u32[]{:S(2)}) collective-permute-start(bf16[6,96,768]{2,1,0:T(8,128)(2,1)} %get-tuple-element.66), channel_id=1, source_target_pairs={{0,96},{16,112},{32,0},{48,16},{64,32},{80,48},{96,64},{112,80},{1... | collective-permute-start | bytes 2654216 | tf_op jit(solution)/shard_map/ppermute | solution.py:368
  15.9 35.4 %collective-permute-start.4 = (bf16[6,96,768]{2,1,0:T(8,128)(2,1)}, bf16[6,96,768]{2,1,0:T(8,128)(2,1)}, u32[]{:S(2)}, u32[]{:S(2)}) collective-permute-start(bf16[6,96,768]{2,1,0:T(8,128)(2,1)} %get-tuple-element.67), channel_id=1, source_target_pairs={{0,64},{16,80},{32,96},{48,112},{64,0},{80,16},{96,32},{112,48},{1... | collective-permute-start | bytes 2654216 | tf_op jit(solution)/shard_map/ppermute | solution.py:368
  18.3 8.2 %copy-start.10 = (s32[8]{0:T(128)S(1)}, s32[8]{0:T(128)}, u32[]{:S(2)}) copy-start(s32[8]{0:T(128)} %constant.52.clone) | copy-start | bytes 100
  18.3 43.2 %all-to-all-start = ((bf16[96,96,128]{2,1,0:T(8,128)(2,1)}), bf16[96,96,128]{2,1,0:T(8,128)(2,1)S(1)}, u32[]{:S(2)}, u32[]{:S(2)}) async-start(bf16[96,96,128]{2,1,0:T(8,128)(2,1)} %pad.8), calls=%async_computation | async-start | bytes 4718592 | tf_op jit(solution)/shard_map/all_to_all | solution.py:362
  26.5 34.9 %copy-start.8 = (f32[90]{0:T(128)S(1)}, f32[90]{0:T(128)}, u32[]{:S(2)}) copy-start(f32[90]{0:T(128)} %param.13) | copy-start | bytes 1084
  26.5 35.0 %copy-start.9 = (s32[8]{0:T(128)S(1)}, s32[8]{0:T(128)}, u32[]{:S(2)}) copy-start(s32[8]{0:T(128)} %constant.66) | copy-start | bytes 100
  52.5 30.7 %collective-permute-start.5 = (bf16[6,96,768]{2,1,0:T(8,128)(2,1)}, bf16[6,96,768]{2,1,0:T(8,128)(2,1)}, u32[]{:S(2)}, u32[]{:S(2)}) collective-permute-start(bf16[6,96,768]{2,1,0:T(8,128)(2,1)} %get-tuple-element.71), channel_id=1, source_target_pairs={{0,48},{16,64},{32,80},{48,96},{64,112},{80,0},{96,16},{112,32},{1... | collective-permute-start | bytes 2654216 | tf_op jit(solution)/shard_map/ppermute | solution.py:368
  52.6 47.7 %collective-permute-start.6 = (bf16[6,96,768]{2,1,0:T(8,128)(2,1)}, bf16[6,96,768]{2,1,0:T(8,128)(2,1)}, u32[]{:S(2)}, u32[]{:S(2)}) collective-permute-start(bf16[6,96,768]{2,1,0:T(8,128)(2,1)} %get-tuple-element.72), channel_id=1, source_target_pairs={{0,80},{16,96},{32,112},{48,0},{64,16},{80,32},{96,48},{112,64},{1... | collective-permute-start | bytes 2654216 | tf_op jit(solution)/shard_map/ppermute | solution.py:368
  71.1 51.9 %all-to-all-start.1 = ((bf16[128,72,128]{2,1,0:T(8,128)(2,1)}), bf16[128,72,128]{2,1,0:T(8,128)(2,1)S(1)}, u32[]{:S(2)}, u32[]{:S(2)}) async-start(bf16[128,72,128]{2,1,0:T(8,128)(2,1)} %bitcast.10), calls=%async_computation.1 | async-start | bytes 4718592 | tf_op jit(solution)/shard_map/all_to_all | solution.py:362
  124.1 28.6 %copy-start = (bf16[90,128,128]{2,1,0:T(8,128)(2,1)S(1)}, bf16[90,128,128]{2,1,0:T(8,128)(2,1)}, u32[]{:S(2)}) copy-start(bf16[90,128,128]{2,1,0:T(8,128)(2,1)} %refs_5_.1) | copy-start | bytes 8847364
  124.1 28.6 %copy-start.1 = (bf16[90,128,128]{2,1,0:T(8,128)(2,1)S(1)}, bf16[90,128,128]{2,1,0:T(8,128)(2,1)}, u32[]{:S(2)}) copy-start(bf16[90,128,128]{2,1,0:T(8,128)(2,1)} %refs_6_.1) | copy-start | bytes 8847364
  130.8 11.2 %collective-permute-start.7 = (bf16[1080,128]{1,0:T(8,128)(2,1)S(1)}, bf16[1080,128]{1,0:T(8,128)(2,1)S(1)}, u32[]{:S(2)}, u32[]{:S(2)}) collective-permute-start(bf16[1080,128]{1,0:T(8,128)(2,1)S(1)} %get-tuple-element.83), channel_id=1, source_target_pairs={{0,64},{16,80},{32,96},{48,112},{64,0},{80,16},{96,32},{112,48},{1... | collective-permute-start | bytes 829448 | tf_op jit(solution)/shard_map/ppermute | solution.py:368
  133.0 12.4 %collective-permute-start.8 = (bf16[1080,128]{1,0:T(8,128)(2,1)S(1)}, bf16[1080,128]{1,0:T(8,128)(2,1)S(1)}, u32[]{:S(2)}, u32[]{:S(2)}) collective-permute-start(bf16[1080,128]{1,0:T(8,128)(2,1)S(1)} %get-tuple-element.84), channel_id=1, source_target_pairs={{0,48},{16,64},{32,80},{48,96},{64,112},{80,0},{96,16},{112,32},{1... | collective-permute-start | bytes 829448 | tf_op jit(solution)/shard_map/ppermute | solution.py:368
  134.1 18.7 %collective-permute-start.9 = (bf16[1080,128]{1,0:T(8,128)(2,1)S(1)}, bf16[1080,128]{1,0:T(8,128)(2,1)S(1)}, u32[]{:S(2)}, u32[]{:S(2)}) collective-permute-start(bf16[1080,128]{1,0:T(8,128)(2,1)S(1)} %get-tuple-element.85), channel_id=1, source_target_pairs={{0,80},{16,96},{32,112},{48,0},{64,16},{80,32},{96,48},{112,64},{1... | collective-permute-start | bytes 829448 | tf_op jit(solution)/shard_map/ppermute | solution.py:368
  136.2 22.1 %collective-permute-start.13 = (bf16[1080,128]{1,0:T(8,128)(2,1)S(1)}, bf16[1080,128]{1,0:T(8,128)(2,1)S(1)}, u32[]{:S(2)}, u32[]{:S(2)}) collective-permute-start(bf16[1080,128]{1,0:T(8,128)(2,1)S(1)} %get-tuple-element.89), channel_id=1, source_target_pairs={{0,32},{16,48},{32,64},{48,80},{64,96},{80,112},{96,0},{112,16},{1... | collective-permute-start | bytes 829448 | tf_op jit(solution)/shard_map/ppermute | solution.py:368
  137.5 22.2 %collective-permute-start.14 = (bf16[1080,128]{1,0:T(8,128)(2,1)S(1)}, bf16[1080,128]{1,0:T(8,128)(2,1)S(1)}, u32[]{:S(2)}, u32[]{:S(2)}) collective-permute-start(bf16[1080,128]{1,0:T(8,128)(2,1)S(1)} %get-tuple-element.90), channel_id=1, source_target_pairs={{0,96},{16,112},{32,0},{48,16},{64,32},{80,48},{96,64},{112,80},{1... | collective-permute-start | bytes 829448 | tf_op jit(solution)/shard_map/ppermute | solution.py:368
  142.0 18.1 %collective-permute-start.15 = (bf16[1080,128]{1,0:T(8,128)(2,1)S(1)}, bf16[1080,128]{1,0:T(8,128)(2,1)S(1)}, u32[]{:S(2)}, u32[]{:S(2)}) collective-permute-start(bf16[1080,128]{1,0:T(8,128)(2,1)S(1)} %get-tuple-element.91), channel_id=1, source_target_pairs={{0,16},{16,32},{32,48},{48,64},{64,80},{80,96},{96,112},{112,0},{1... | collective-permute-start | bytes 829448 | tf_op jit(solution)/shard_map/ppermute | solution.py:368
  145.4 14.7 %collective-permute-start.16 = (bf16[1080,128]{1,0:T(8,128)(2,1)S(1)}, bf16[1080,128]{1,0:T(8,128)(2,1)S(1)}, u32[]{:S(2)}, u32[]{:S(2)}) collective-permute-start(bf16[1080,128]{1,0:T(8,128)(2,1)S(1)} %get-tuple-element.92), channel_id=1, source_target_pairs={{0,112},{16,0},{32,16},{48,32},{64,48},{80,64},{96,80},{112,96},{1... | collective-permute-start | bytes 829448 | tf_op jit(solution)/shard_map/ppermute | solution.py:368
  155.8 11.2 %collective-permute-start.10 = (bf16[1080,128]{1,0:T(8,128)(2,1)S(1)}, bf16[1080,128]{1,0:T(8,128)(2,1)S(1)}, u32[]{:S(2)}, u32[]{:S(2)}) collective-permute-start(bf16[1080,128]{1,0:T(8,128)(2,1)S(1)} %get-tuple-element.86), channel_id=1, source_target_pairs={{0,64},{16,80},{32,96},{48,112},{64,0},{80,16},{96,32},{112,48},{1... | collective-permute-start | bytes 829448 | tf_op jit(solution)/shard_map/ppermute | solution.py:368
  158.4 13.0 %collective-permute-start.11 = (bf16[1080,128]{1,0:T(8,128)(2,1)S(1)}, bf16[1080,128]{1,0:T(8,128)(2,1)S(1)}, u32[]{:S(2)}, u32[]{:S(2)}) collective-permute-start(bf16[1080,128]{1,0:T(8,128)(2,1)S(1)} %get-tuple-element.87), channel_id=1, source_target_pairs={{0,80},{16,96},{32,112},{48,0},{64,16},{80,32},{96,48},{112,64},{1... | collective-permute-start | bytes 829448 | tf_op jit(solution)/shard_map/ppermute | solution.py:368
  159.7 16.2 %collective-permute-start.12 = (bf16[1080,128]{1,0:T(8,128)(2,1)S(1)}, bf16[1080,128]{1,0:T(8,128)(2,1)S(1)}, u32[]{:S(2)}, u32[]{:S(2)}) collective-permute-start(bf16[1080,128]{1,0:T(8,128)(2,1)S(1)} %get-tuple-element.88), channel_id=1, source_target_pairs={{0,48},{16,64},{32,80},{48,96},{64,112},{80,0},{96,16},{112,32},{1... | collective-permute-start | bytes 829448 | tf_op jit(solution)/shard_map/ppermute | solution.py:368
  160.1 24.5 %copy-start.5 = (bf16[6,96,768]{2,1,0:T(8,128)(2,1)S(1)}, bf16[6,96,768]{2,1,0:T(8,128)(2,1)}, u32[]{:S(2)}) copy-start(bf16[6,96,768]{2,1,0:T(8,128)(2,1)} %get-tuple-element.75.refs_0_.refs_8_) | copy-start | bytes 2654212
  160.1 68.5 %slice-start = ((s8[4718592]{0:T(1024)(128)(4,1)}), s8[524288]{0:T(1024)(128)(4,1)S(1)}, s32[]{:S(2)}) async-start(s8[4718592]{0:T(1024)(128)(4,1)} %bitcast.13), calls=%async_computation.4 | async-start | bytes 1048576
  163.5 15.5 %collective-permute-start.17 = (bf16[1080,128]{1,0:T(8,128)(2,1)S(1)}, bf16[1080,128]{1,0:T(8,128)(2,1)S(1)}, u32[]{:S(2)}, u32[]{:S(2)}) collective-permute-start(bf16[1080,128]{1,0:T(8,128)(2,1)S(1)} %get-tuple-element.94), channel_id=1, source_target_pairs={{0,96},{16,112},{32,0},{48,16},{64,32},{80,48},{96,64},{112,80},{1... | collective-permute-start | bytes 829448 | tf_op jit(solution)/shard_map/ppermute | solution.py:368
  166.5 18.0 %collective-permute-start.18 = (bf16[1080,128]{1,0:T(8,128)(2,1)S(1)}, bf16[1080,128]{1,0:T(8,128)(2,1)S(1)}, u32[]{:S(2)}, u32[]{:S(2)}) collective-permute-start(bf16[1080,128]{1,0:T(8,128)(2,1)S(1)} %get-tuple-element.95), channel_id=1, source_target_pairs={{0,32},{16,48},{32,64},{48,80},{64,96},{80,112},{96,0},{112,16},{1... | collective-permute-start | bytes 829448 | tf_op jit(solution)/shard_map/ppermute | solution.py:368
  167.0 17.5 %collective-permute-start.19 = (bf16[1080,128]{1,0:T(8,128)(2,1)S(1)}, bf16[1080,128]{1,0:T(8,128)(2,1)S(1)}, u32[]{:S(2)}, u32[]{:S(2)}) collective-permute-start(bf16[1080,128]{1,0:T(8,128)(2,1)S(1)} %get-tuple-element.96), channel_id=1, source_target_pairs={{0,112},{16,0},{32,16},{48,32},{64,48},{80,64},{96,80},{112,96},{1... | collective-permute-start | bytes 829448 | tf_op jit(solution)/shard_map/ppermute | solution.py:368
  171.4 13.3 %collective-permute-start.20 = (bf16[1080,128]{1,0:T(8,128)(2,1)S(1)}, bf16[1080,128]{1,0:T(8,128)(2,1)S(1)}, u32[]{:S(2)}, u32[]{:S(2)}) collective-permute-start(bf16[1080,128]{1,0:T(8,128)(2,1)S(1)} %get-tuple-element.97), channel_id=1, source_target_pairs={{0,16},{16,32},{32,48},{48,64},{64,80},{80,96},{96,112},{112,0},{1... | collective-permute-start | bytes 829448 | tf_op jit(solution)/shard_map/ppermute | solution.py:368
  184.6 44.0 %slice-start.1 = ((s8[4718592]{0:T(1024)(128)(4,1)}), s8[4194304]{0:T(1024)(128)(4,1)S(1)}, s32[]{:S(2)}) async-start(s8[4718592]{0:T(1024)(128)(4,1)} %bitcast.13), calls=%async_computation.5 | async-start | bytes 8388608
  234.7 34.6 %copy-start.7 = (bf16[90,90,128]{2,1,0:T(8,128)(2,1)S(1)}, bf16[90,90,128]{2,1,0:T(8,128)(2,1)}, u32[]{:S(2)}) copy-start(bf16[90,90,128]{2,1,0:T(8,128)(2,1)} %param.11) | copy-start | bytes 6220804
  (4 other events, 9.9 us)

commit v5 on v4

--- a/solution.py
+++ b/solution.py
@@ -1,3 +1,5 @@
+import functools
+
 import jax
 import jax.numpy as jnp
 import ml_dtypes
@@ -66,13 +68,18 @@
         dst[part, :] = src[part, :].astype(dst.dtype)
 
 
-def cut_kernel(scalars_ref, *refs):
+def block_of(p, s):
+    return jnp.minimum(lax.rem(p + SHIFTS[s], LAT) * (OWN // 3), 45 // 3 - OWN // 3)
+
+
+def cut_kernel(places, p_ref, q_ref, *refs):
     ins, outs = refs[: len(refs) // 2], refs[len(refs) // 2 :]
     count = ins[0].shape[0]
     degree = lax.broadcasted_iota(jnp.int32, (BAND, DEG), 1)
-    for s, (in_ref, out_ref) in enumerate(zip(ins, outs)):
-        first = scalars_ref[len(ins)] + (scalars_ref[s] + pl.program_id(0)) * count
-        out_ref[...] = jnp.zeros(out_ref.shape, out_ref.dtype)
+    for s, in_ref, out_ref in zip(places, ins, outs):
+        first = q_ref[0] * 45 + (block_of(p_ref[0], s) + pl.program_id(0)) * count
+        out_ref[:, PAD - 16 :, :] = jnp.zeros((count, 16, DEGPAD), out_ref.dtype)
+        out_ref[:, :, DEGPAD - CH :] = jnp.zeros((count, PAD, CH), out_ref.dtype)
         for j in range(count):
             part = in_ref[j].astype(jnp.float32)
             part = jnp.where(degree >= first + j, part, 0.0)
@@ -246,18 +253,18 @@
     return pl.BlockSpec(shape, lambda *_: (0,) * len(shape))
 
 
-def cut(table, scalars, n):
-    count = 3
-    return pl.pallas_call(
-        cut_kernel,
+def cut(table, p, q, places):
+    count, n = 3, len(places)
+    return pl.pallas_call(
+        functools.partial(cut_kernel, places),
         grid_spec=pltpu.PrefetchScalarGridSpec(
-            num_scalar_prefetch=1,
+            num_scalar_prefetch=2,
             grid=(OWN // count,),
             in_specs=[
-                pl.BlockSpec((count, BAND, DEG), lambda i, ref, s=s: (ref[s] + i, 0, 0))
-                for s in range(n)
+                pl.BlockSpec((count, BAND, DEG), lambda i, p, q, s=s: (block_of(p[0], s) + i, 0, 0))
+                for s in places
             ],
-            out_specs=[pl.BlockSpec((count, PAD, DEGPAD), lambda i, ref: (i, 0, 0))] * n,
+            out_specs=[pl.BlockSpec((count, PAD, DEGPAD), lambda i, p, q: (i, 0, 0))] * n,
         ),
         out_shape=[jax.ShapeDtypeStruct((OWN, PAD, DEGPAD), jnp.bfloat16)] * n,
         compiler_params=params(CUT_VMEM),
@@ -265,7 +272,7 @@
             flops=1_000_000 * n, bytes_accessed=1_700_000 * n, transcendentals=0
         ),
         name="cut",
-    )(scalars, *[table] * n)
+    )(p.reshape(1), q.reshape(1), *[table] * n)
 
 
 def in_order(token):
@@ -375,17 +382,13 @@
 
     rows = swap(jnp.pad(field, ((0, PAD - BAND), (0, PAD - BAND), (0, 0))), "lon")
 
-    orders = legendre.shape[0]
     table = jnp.transpose(legendre, (0, 2, 1))
     shifts = jnp.array(SHIFTS, jnp.int32)
     src = lax.rem(p - shifts + LAT, LAT)
     dest = lax.rem(p + jnp.array(SENDS, jnp.int32), LAT)
     cuts = [None] * LAT
-    for group in ((1, 2, 3, 4), (5, 6, 7, 0)):
-        moves = jnp.array([SHIFTS[i] for i in group] + [0], jnp.int32)
-        firsts = jnp.minimum(lax.rem(p + moves, LAT) * (OWN // 3), (orders - OWN) // 3)
-        scalars = jnp.where(jnp.arange(len(group) + 1) == len(group), q * orders, firsts)
-        parts = cut(table, scalars, len(group))
+    for group in ((1, 2), (3, 4), (5, 6, 7, 0)):
+        parts = cut(table, p, q, group)
         table, *parts = lax.optimization_barrier((table, *parts))
         for i, part in zip(group, parts):
             cuts[i] = part

time: 272 us -> 269 us (0.989)
  starting transfers between devices: 57.6 us -> 53.3 us
    ppermute x21, starting transfers between devices: 37.3 us -> 32.5 us  [shifted(): lax.ppermute(part, 'lat', [(i, (i + shift) % LAT) for i in range(LAT)])]
    pallas_call x2 -> x3, Pallas kernels: 8.47 us -> 8.45 us  [cut(): pl.pallas_call(functools.partial(cut_kernel, places), grid_spec=pltpu.Pre...]
  transfers between devices with their start and end apart: 23 -> 23, of which waited for: 15 -> 15; matrix products, arithmetic and copies ran while one was open for 1% -> 1% of each run, Pallas kernels for 7% -> 8%
where the time goes in v5:
time: 269 us; the launch traced here: 268 us
  waiting for transfers between devices  90.9 us (34%)
  blocking collectives  73 us (27%)
  starting transfers between devices  53.3 us (20%)
  Pallas kernels  42.4 us (16%)
  local copies, waits for them, and re-layouts  6.7 us (2%)
    all_to_all x2, blocking collectives, swap(): return lax.all_to_all(x, axes, split_axis=0, concat_axis=0, tiled=True)  73 us
    ppermute x21, waiting for transfers between devices, shifted(): lax.ppermute(part, 'lat', [(i, (i + shift) % LAT) for i in range(LAT)])  68.5 us
    ppermute x21, starting transfers between devices, shifted(): lax.ppermute(part, 'lat', [(i, (i + shift) % LAT) for i in range(LAT)])  32.5 us
    all_to_all x2, waiting for transfers between devices, swap(): return lax.all_to_all(x, axes, split_axis=0, concat_axis=0, tiled=True)  22.4 us
    all_to_all x2, starting transfers between devices, swap(): return lax.all_to_all(x, axes, split_axis=0, concat_axis=0, tiled=True)  20.8 us
    pallas_call x2, Pallas kernels, legendre_call(): pl.pallas_call(kernel, grid=(OWN,), in_specs=[pl.BlockSpec(memory_space=p...  13.3 us
    pallas_call x3, Pallas kernels, cut(): pl.pallas_call(functools.partial(cut_kernel, places), grid_spec=pltpu.Pre...  8.45 us
    pallas_call x2, Pallas kernels, mix(): pl.pallas_call(mix_kernel, grid=(BAND // STEP,), in_specs=[whole((PART, C...  6.52 us
  transfers between devices with their start and end apart: 23, of which 15 were waited for; matrix products, arithmetic and copies ran while one was open for 1% of the time, Pallas kernels for 8%

profile of v5, /device:TPU:0, one launch (start us, length us, event | category | flops | bytes accessed | tf_op | source)
XLA Modules:
  0.0 268.5 jit_solution(461753662154975413)
XLA Ops:
  0.0 2.5 cut.3
  2.5 3.0 %collective-permute-start.1 = (bf16[6,96,768]{2,1,0:T(8,128)(2,1)}, bf16[6,96,768]{2,1,0:T(8,128)(2,1)}, u32[]{:S(2)}, u32[]{:S(2)}) collective-permute-start(bf16[6,96,768]{2,1,0:T(8,128)(2,1)} %get-tuple-element.66), channel_id=1, source_target_pairs={{0,112},{16,0},{32,16},{48,32},{64,48},{80,64},{96,80},{112,96},{1... | collective-permute-start | bytes 2654216 | tf_op jit(solution)/shard_map/ppermute | solution.py:375
  5.5 2.5 cut.4
  8.3 2.9 %collective-permute-start.3 = (bf16[6,96,768]{2,1,0:T(8,128)(2,1)}, bf16[6,96,768]{2,1,0:T(8,128)(2,1)}, u32[]{:S(2)}, u32[]{:S(2)}) collective-permute-start(bf16[6,96,768]{2,1,0:T(8,128)(2,1)} %get-tuple-element.68), channel_id=1, source_target_pairs={{0,96},{16,112},{32,0},{48,16},{64,32},{80,48},{96,64},{112,80},{1... | collective-permute-start | bytes 2654216 | tf_op jit(solution)/shard_map/ppermute | solution.py:375
  11.2 3.5 %cut.5 = (bf16[6,96,768]{2,1,0:T(8,128)(2,1)}, bf16[6,96,768]{2,1,0:T(8,128)(2,1)}, bf16[6,96,768]{2,1,0:T(8,128)(2,1)}, bf16[6,96,768]{2,1,0:T(8,128)(2,1)}) custom-call(s32[1]{0:T(128)} %bitcast.1.p_ref, s32[1]{0:T(128)} %bitcast.2.q_ref, bf16[45,90,720]{2,1,0:T(8,128)(2,1)} %bitcast.21, bf16[45,90,720]{2,1,0:T(8,128)(2,1)} %bitcast.22, ...), custom_call_target="tpu_custom_call" | custom-call | flops 4000000 | bytes 6800000 | tf_op jit(solution)/shard_map/cut/pallas_call | solution.py:258
  17.0 8.2 %all-to-all-start = ((bf16[96,96,128]{2,1,0:T(8,128)(2,1)}), bf16[96,96,128]{2,1,0:T(8,128)(2,1)S(1)}, u32[]{:S(2)}, u32[]{:S(2)}) async-start(bf16[96,96,128]{2,1,0:T(8,128)(2,1)} %pad.8), calls=%async_computation | async-start | bytes 4718592 | tf_op jit(solution)/shard_map/all_to_all | solution.py:369
  25.2 7.0 %collective-permute-done.2.refs_3_.refs_11_ = bf16[6,96,768]{2,1,0:T(8,128)(2,1)} collective-permute-done((bf16[6,96,768]{2,1,0:T(8,128)(2,1)}, bf16[6,96,768]{2,1,0:T(8,128)(2,1)}, u32[]{:S(2)}, u32[]{:S(2)}) %collective-permute-start.2) | collective-permute-done | bytes 884768 | tf_op jit(solution)/shard_map/ppermute | solution.py:375
  32.2 10.2 %collective-permute-done.3.refs_4_.refs_12_ = bf16[6,96,768]{2,1,0:T(8,128)(2,1)} collective-permute-done((bf16[6,96,768]{2,1,0:T(8,128)(2,1)}, bf16[6,96,768]{2,1,0:T(8,128)(2,1)}, u32[]{:S(2)}, u32[]{:S(2)}) %collective-permute-start.3) | collective-permute-done | bytes 884768 | tf_op jit(solution)/shard_map/ppermute | solution.py:375
  42.4 8.4 %collective-permute-done.4.refs_7_.refs_15_ = bf16[6,96,768]{2,1,0:T(8,128)(2,1)} collective-permute-done((bf16[6,96,768]{2,1,0:T(8,128)(2,1)}, bf16[6,96,768]{2,1,0:T(8,128)(2,1)}, u32[]{:S(2)}, u32[]{:S(2)}) %collective-permute-start.4) | collective-permute-done | bytes 884768 | tf_op jit(solution)/shard_map/ppermute | solution.py:375
  52.1 5.0 %collective-permute-start.6 = (bf16[6,96,768]{2,1,0:T(8,128)(2,1)}, bf16[6,96,768]{2,1,0:T(8,128)(2,1)}, u32[]{:S(2)}, u32[]{:S(2)}) collective-permute-start(bf16[6,96,768]{2,1,0:T(8,128)(2,1)} %get-tuple-element.74), channel_id=1, source_target_pairs={{0,80},{16,96},{32,112},{48,0},{64,16},{80,32},{96,48},{112,64},{1... | collective-permute-start | bytes 2654216 | tf_op jit(solution)/shard_map/ppermute | solution.py:375
  60.3 5.8 %dft.1 = bf16[9216,128]{1,0:T(8,128)(2,1)S(1)} custom-call(f32[6]{0:T(128)S(1)} %pad_dynamic-slice_fusion.quad_ref, bf16[16,6,96,128]{3,2,1,0:T(8,128)(2,1)S(1)} %bitcast.10, bf16[1536,1536]{1,0:T(8,128)(2,1)S(1)} %copy-done.3), custom_call_target="tpu_custom_call" | custom-call | flops 1000000 | bytes 100000 | tf_op jit(solution)/shard_map/dft/pallas_call | solution.py:293
  67.6 12.7 %all-to-all-start.1 = ((bf16[128,72,128]{2,1,0:T(8,128)(2,1)}), bf16[128,72,128]{2,1,0:T(8,128)(2,1)S(1)}, u32[]{:S(2)}, u32[]{:S(2)}) async-start(bf16[128,72,128]{2,1,0:T(8,128)(2,1)} %bitcast.12), calls=%async_computation.1 | async-start | bytes 4718592 | tf_op jit(solution)/shard_map/all_to_all | solution.py:369
  80.3 16.8 %collective-permute-done.6.refs_6_.refs_14_ = bf16[6,96,768]{2,1,0:T(8,128)(2,1)} collective-permute-done((bf16[6,96,768]{2,1,0:T(8,128)(2,1)}, bf16[6,96,768]{2,1,0:T(8,128)(2,1)}, u32[]{:S(2)}, u32[]{:S(2)}) %collective-permute-start.6) | collective-permute-done | bytes 884768 | tf_op jit(solution)/shard_map/ppermute | solution.py:375
  98.2 21.6 %all-to-all-done.1 = bf16[128,72,128]{2,1,0:T(8,128)(2,1)S(1)} async-done(((bf16[128,72,128]{2,1,0:T(8,128)(2,1)}), bf16[128,72,128]{2,1,0:T(8,128)(2,1)S(1)}, u32[]{:S(2)}, u32[]{:S(2)}) %all-to-all-start.1) | async-done | bytes 2359328 | tf_op jit(solution)/shard_map/all_to_all | solution.py:369
  121.0 6.7 %legendre.1 = (bf16[1080,128]{1,0:T(8,128)(2,1)S(1)}, bf16[1080,128]{1,0:T(8,128)(2,1)S(1)}, bf16[1080,128]{1,0:T(8,128)(2,1)S(1)}, bf16[1080,128]{1,0:T(8,128)(...) custom-call(s32[8]{0:T(128)S(1)} %compare_select_fusion.2.src_ref, ...), custom_call_target="tpu_custom_call" | custom-call | flops 1811939328 | bytes 12000000 | tf_op jit(solution)/shard_map/legendre/pallas_call | solution.py:314
  127.7 2.5 collective-permute-start.7
  131.1 2.4 collective-permute-start.9
  134.3 2.4 collective-permute-start.14
  138.3 4.4 %collective-permute-done.8.refs_1_ = bf16[1080,128]{1,0:T(8,128)(2,1)S(1)} collective-permute-done((bf16[1080,128]{1,0:T(8,128)(2,1)S(1)}, bf16[1080,128]{1,0:T(8,128)(2,1)S(1)}, u32[]{:S(2)}, u32[]{:S(2)}) %collective-permute-start.8) | collective-permute-done | bytes 276512 | tf_op jit(solution)/shard_map/ppermute | solution.py:375
  144.5 5.5 %collective-permute-done.9.refs_2_ = bf16[1080,128]{1,0:T(8,128)(2,1)S(1)} collective-permute-done((bf16[1080,128]{1,0:T(8,128)(2,1)S(1)}, bf16[1080,128]{1,0:T(8,128)(2,1)S(1)}, u32[]{:S(2)}, u32[]{:S(2)}) %collective-permute-start.9) | collective-permute-done | bytes 276512 | tf_op jit(solution)/shard_map/ppermute | solution.py:375
  149.9 3.1 %mix.2 = (bf16[1080,128]{1,0:T(8,128)(2,1)S(1)}, bf16[1080,128]{1,0:T(8,128)(2,1)S(1)}, bf16[1080,128]{1,0:T(8,128)(2,1)S(1)}) custom-call(bf16[1080,128]{1,0:T(8,128)(2,1)S(1)} %collective-permute-done.7.refs_0_, bf16[1080,128]{1,0:T(8,128)(2,1)S(1)} %collective-permute-done.8.refs_1_, bf16[1080,128]{1,0:T(8,128)(2,1)S(1)} %collective-permute-done.9.refs_2_, ...), custom_call_target="tpu_custom_call" | custom-call | flops 566231040 | bytes 10000000 | tf_op jit(solution)/shard_map/mix/pallas_call | solution.py:337
  153.0 2.7 %collective-permute-start.10 = (bf16[1080,128]{1,0:T(8,128)(2,1)S(1)}, bf16[1080,128]{1,0:T(8,128)(2,1)S(1)}, u32[]{:S(2)}, u32[]{:S(2)}) collective-permute-start(bf16[1080,128]{1,0:T(8,128)(2,1)S(1)} %get-tuple-element.88), channel_id=1, source_target_pairs={{0,64},{16,80},{32,96},{48,112},{64,0},{80,16},{96,32},{112,48},{1... | collective-permute-start | bytes 829448 | tf_op jit(solution)/shard_map/ppermute | solution.py:375
  157.6 3.4 %mix.3 = (bf16[1080,128]{1,0:T(8,128)(2,1)S(1)}, bf16[1080,128]{1,0:T(8,128)(2,1)S(1)}, bf16[1080,128]{1,0:T(8,128)(2,1)S(1)}, bf16[1080,128]{1,0:T(8,128)(2,1)S(1)}, bf16[1080,128]{1,0:T(8,128)(2,1)S(1)}) custom-call(bf16[1080,128]{1,0:T(8,128)(2,1)S(1)} %collective-permute-done.13.refs_0_, bf16[1080,128]{1,0:T(8,128)(2,1)S(1)} %collective-permute-done.14.refs_1_, ...), custom_call_target="tpu_custom_call" | custom-call | flops 566231040 | bytes 10000000 | tf_op jit(solution)/shard_map/mix/pallas_call | solution.py:337
  161.0 3.0 %collective-permute-start.17 = (bf16[1080,128]{1,0:T(8,128)(2,1)S(1)}, bf16[1080,128]{1,0:T(8,128)(2,1)S(1)}, u32[]{:S(2)}, u32[]{:S(2)}) collective-permute-start(bf16[1080,128]{1,0:T(8,128)(2,1)S(1)} %get-tuple-element.96), channel_id=1, source_target_pairs={{0,96},{16,112},{32,0},{48,16},{64,32},{80,48},{96,64},{112,80},{1... | collective-permute-start | bytes 829448 | tf_op jit(solution)/shard_map/ppermute | solution.py:375
  165.4 3.3 %collective-permute-done.11.refs_1_ = bf16[1080,128]{1,0:T(8,128)(2,1)S(1)} collective-permute-done((bf16[1080,128]{1,0:T(8,128)(2,1)S(1)}, bf16[1080,128]{1,0:T(8,128)(2,1)S(1)}, u32[]{:S(2)}, u32[]{:S(2)}) %collective-permute-start.11) | collective-permute-done | bytes 276512 | tf_op jit(solution)/shard_map/ppermute | solution.py:375
  169.9 3.7 %collective-permute-done.12.refs_2_ = bf16[1080,128]{1,0:T(8,128)(2,1)S(1)} collective-permute-done((bf16[1080,128]{1,0:T(8,128)(2,1)S(1)}, bf16[1080,128]{1,0:T(8,128)(2,1)S(1)}, u32[]{:S(2)}, u32[]{:S(2)}) %collective-permute-start.12) | collective-permute-done | bytes 276512 | tf_op jit(solution)/shard_map/ppermute | solution.py:375
  173.6 2.5 collective-permute-done.17.refs_3_
  176.1 4.7 %collective-permute-done.18.refs_4_ = bf16[1080,128]{1,0:T(8,128)(2,1)S(1)} collective-permute-done((bf16[1080,128]{1,0:T(8,128)(2,1)S(1)}, bf16[1080,128]{1,0:T(8,128)(2,1)S(1)}, u32[]{:S(2)}, u32[]{:S(2)}) %collective-permute-start.18) | collective-permute-done | bytes 276512 | tf_op jit(solution)/shard_map/ppermute | solution.py:375
  180.9 6.6 %inverse_legendre.1 = bf16[9216,128]{1,0:T(8,128)(2,1)S(1)} custom-call(s32[8]{0:T(128)S(1)} %compare_select_fusion.2.src_ref, s32[8]{0:T(128)S(1)} %in_order.3.dest_ref, bf16[1080,128]{1,0:T(8,128)(2,1)S(1)} %collective-permute-done.10.refs_0_, bf16[1080,128]{1,0:T(8,128)(2,1)S(1)} %collective-permute-done.11.refs_1_, ...), custom_call_target="tpu_custom_call" | custom-call | flops 1811939328 | bytes 12000000 | tf_op jit(solution)/shard_map/inverse_legendre/pallas_call | solution.py:314
  187.5 38.3 %all_to_all.32 = bf16[128,72,128]{2,1,0:T(8,128)(2,1)S(1)} all-to-all(bf16[128,72,128]{2,1,0:T(8,128)(2,1)S(1)} %bitcast.11), channel_id=1, replica_groups=mesh['lat'=8,'lon'=16] {'lat','lon'}, dimensions={0} | all-to-all | bytes 4718592 | tf_op jit(solution)/shard_map/all_to_all | solution.py:369
  225.8 6.0 %inverse_dft.1 = bf16[16,6,96,128]{3,2,1,0:T(8,128)(2,1)S(1)} custom-call(bf16[9216,128]{1,0:T(8,128)(2,1)S(1)} %bitcast.13, bf16[1536,1536]{1,0:T(8,128)(2,1)S(1)} %bitcast.16), custom_call_target="tpu_custom_call" | custom-call | flops 3623878656 | bytes 10000000 | tf_op jit(solution)/shard_map/inverse_dft/pallas_call | solution.py:353
  231.9 34.6 %all_to_all.33 = bf16[96,96,128]{2,1,0:T(8,128)(2,1)S(1)} all-to-all(bf16[96,96,128]{2,1,0:T(8,128)(2,1)S(1)} %bitcast.14), channel_id=1, replica_groups=mesh['lat'=8,'lon'=16] {'lon'}, dimensions={0} | all-to-all | bytes 4718592 | tf_op jit(solution)/shard_map/all_to_all | solution.py:369
  (59 shorter events, 22.3 us)
Async XLA Ops:
  2.5 22.7 %collective-permute-start = (bf16[6,96,768]{2,1,0:T(8,128)(2,1)}, bf16[6,96,768]{2,1,0:T(8,128)(2,1)S(1)}, u32[]{:S(2)}, u32[]{:S(2)}) collective-permute-start(bf16[6,96,768]{2,1,0:T(8,128)(2,1)} %get-tuple-element.65), channel_id=1, source_target_pairs={{0,16},{16,32},{32,48},{48,64},{64,80},{80,96},{96,112},{112,0},{1... | collective-permute-start | bytes 2654216 | tf_op jit(solution)/shard_map/ppermute | solution.py:375
  2.5 22.7 %collective-permute-start.1 = (bf16[6,96,768]{2,1,0:T(8,128)(2,1)}, bf16[6,96,768]{2,1,0:T(8,128)(2,1)}, u32[]{:S(2)}, u32[]{:S(2)}) collective-permute-start(bf16[6,96,768]{2,1,0:T(8,128)(2,1)} %get-tuple-element.66), channel_id=1, source_target_pairs={{0,112},{16,0},{32,16},{48,32},{64,48},{80,64},{96,80},{112,96},{1... | collective-permute-start | bytes 2654216 | tf_op jit(solution)/shard_map/ppermute | solution.py:375
  7.9 24.2 %collective-permute-start.2 = (bf16[6,96,768]{2,1,0:T(8,128)(2,1)}, bf16[6,96,768]{2,1,0:T(8,128)(2,1)}, u32[]{:S(2)}, u32[]{:S(2)}) collective-permute-start(bf16[6,96,768]{2,1,0:T(8,128)(2,1)} %get-tuple-element.67), channel_id=1, source_target_pairs={{0,32},{16,48},{32,64},{48,80},{64,96},{80,112},{96,0},{112,16},{1... | collective-permute-start | bytes 2654216 | tf_op jit(solution)/shard_map/ppermute | solution.py:375
  8.3 34.1 %collective-permute-start.3 = (bf16[6,96,768]{2,1,0:T(8,128)(2,1)}, bf16[6,96,768]{2,1,0:T(8,128)(2,1)}, u32[]{:S(2)}, u32[]{:S(2)}) collective-permute-start(bf16[6,96,768]{2,1,0:T(8,128)(2,1)} %get-tuple-element.68), channel_id=1, source_target_pairs={{0,96},{16,112},{32,0},{48,16},{64,32},{80,48},{96,64},{112,80},{1... | collective-permute-start | bytes 2654216 | tf_op jit(solution)/shard_map/ppermute | solution.py:375
  14.6 36.2 %collective-permute-start.4 = (bf16[6,96,768]{2,1,0:T(8,128)(2,1)}, bf16[6,96,768]{2,1,0:T(8,128)(2,1)}, u32[]{:S(2)}, u32[]{:S(2)}) collective-permute-start(bf16[6,96,768]{2,1,0:T(8,128)(2,1)} %get-tuple-element.69), channel_id=1, source_target_pairs={{0,64},{16,80},{32,96},{48,112},{64,0},{80,16},{96,32},{112,48},{1... | collective-permute-start | bytes 2654216 | tf_op jit(solution)/shard_map/ppermute | solution.py:375
  17.0 8.2 %copy-start.10 = (s32[8]{0:T(128)S(1)}, s32[8]{0:T(128)}, u32[]{:S(2)}) copy-start(s32[8]{0:T(128)} %constant.35.clone) | copy-start | bytes 100
  17.0 41.0 %all-to-all-start = ((bf16[96,96,128]{2,1,0:T(8,128)(2,1)}), bf16[96,96,128]{2,1,0:T(8,128)(2,1)S(1)}, u32[]{:S(2)}, u32[]{:S(2)}) async-start(bf16[96,96,128]{2,1,0:T(8,128)(2,1)} %pad.8), calls=%async_computation | async-start | bytes 4718592 | tf_op jit(solution)/shard_map/all_to_all | solution.py:369
  25.2 31.9 %copy-start.8 = (f32[90]{0:T(128)S(1)}, f32[90]{0:T(128)}, u32[]{:S(2)}) copy-start(f32[90]{0:T(128)} %param.11) | copy-start | bytes 1084
  25.2 31.9 %copy-start.9 = (s32[8]{0:T(128)S(1)}, s32[8]{0:T(128)}, u32[]{:S(2)}) copy-start(s32[8]{0:T(128)} %constant.47) | copy-start | bytes 100
  52.0 28.2 %collective-permute-start.5 = (bf16[6,96,768]{2,1,0:T(8,128)(2,1)}, bf16[6,96,768]{2,1,0:T(8,128)(2,1)}, u32[]{:S(2)}, u32[]{:S(2)}) collective-permute-start(bf16[6,96,768]{2,1,0:T(8,128)(2,1)} %get-tuple-element.73), channel_id=1, source_target_pairs={{0,48},{16,64},{32,80},{48,96},{64,112},{80,0},{96,16},{112,32},{1... | collective-permute-start | bytes 2654216 | tf_op jit(solution)/shard_map/ppermute | solution.py:375
  52.1 45.0 %collective-permute-start.6 = (bf16[6,96,768]{2,1,0:T(8,128)(2,1)}, bf16[6,96,768]{2,1,0:T(8,128)(2,1)}, u32[]{:S(2)}, u32[]{:S(2)}) collective-permute-start(bf16[6,96,768]{2,1,0:T(8,128)(2,1)} %get-tuple-element.74), channel_id=1, source_target_pairs={{0,80},{16,96},{32,112},{48,0},{64,16},{80,32},{96,48},{112,64},{1... | collective-permute-start | bytes 2654216 | tf_op jit(solution)/shard_map/ppermute | solution.py:375
  67.6 52.2 %all-to-all-start.1 = ((bf16[128,72,128]{2,1,0:T(8,128)(2,1)}), bf16[128,72,128]{2,1,0:T(8,128)(2,1)S(1)}, u32[]{:S(2)}, u32[]{:S(2)}) async-start(bf16[128,72,128]{2,1,0:T(8,128)(2,1)} %bitcast.12), calls=%async_computation.1 | async-start | bytes 4718592 | tf_op jit(solution)/shard_map/all_to_all | solution.py:369
  121.0 29.0 %copy-start = (bf16[90,128,128]{2,1,0:T(8,128)(2,1)S(1)}, bf16[90,128,128]{2,1,0:T(8,128)(2,1)}, u32[]{:S(2)}) copy-start(bf16[90,128,128]{2,1,0:T(8,128)(2,1)} %refs_5_.1) | copy-start | bytes 8847364
  121.0 29.0 %copy-start.1 = (bf16[90,128,128]{2,1,0:T(8,128)(2,1)S(1)}, bf16[90,128,128]{2,1,0:T(8,128)(2,1)}, u32[]{:S(2)}) copy-start(bf16[90,128,128]{2,1,0:T(8,128)(2,1)} %refs_6_.1) | copy-start | bytes 8847364
  127.7 10.6 %collective-permute-start.7 = (bf16[1080,128]{1,0:T(8,128)(2,1)S(1)}, bf16[1080,128]{1,0:T(8,128)(2,1)S(1)}, u32[]{:S(2)}, u32[]{:S(2)}) collective-permute-start(bf16[1080,128]{1,0:T(8,128)(2,1)S(1)} %get-tuple-element.85), channel_id=1, source_target_pairs={{0,64},{16,80},{32,96},{48,112},{64,0},{80,16},{96,32},{112,48},{1... | collective-permute-start | bytes 829448 | tf_op jit(solution)/shard_map/ppermute | solution.py:375
  130.2 12.5 %collective-permute-start.8 = (bf16[1080,128]{1,0:T(8,128)(2,1)S(1)}, bf16[1080,128]{1,0:T(8,128)(2,1)S(1)}, u32[]{:S(2)}, u32[]{:S(2)}) collective-permute-start(bf16[1080,128]{1,0:T(8,128)(2,1)S(1)} %get-tuple-element.86), channel_id=1, source_target_pairs={{0,48},{16,64},{32,80},{48,96},{64,112},{80,0},{96,16},{112,32},{1... | collective-permute-start | bytes 829448 | tf_op jit(solution)/shard_map/ppermute | solution.py:375
  131.1 18.8 %collective-permute-start.9 = (bf16[1080,128]{1,0:T(8,128)(2,1)S(1)}, bf16[1080,128]{1,0:T(8,128)(2,1)S(1)}, u32[]{:S(2)}, u32[]{:S(2)}) collective-permute-start(bf16[1080,128]{1,0:T(8,128)(2,1)S(1)} %get-tuple-element.87), channel_id=1, source_target_pairs={{0,80},{16,96},{32,112},{48,0},{64,16},{80,32},{96,48},{112,64},{1... | collective-permute-start | bytes 829448 | tf_op jit(solution)/shard_map/ppermute | solution.py:375
  133.5 22.3 %collective-permute-start.13 = (bf16[1080,128]{1,0:T(8,128)(2,1)S(1)}, bf16[1080,128]{1,0:T(8,128)(2,1)S(1)}, u32[]{:S(2)}, u32[]{:S(2)}) collective-permute-start(bf16[1080,128]{1,0:T(8,128)(2,1)S(1)} %get-tuple-element.91), channel_id=1, source_target_pairs={{0,32},{16,48},{32,64},{48,80},{64,96},{80,112},{96,0},{112,16},{1... | collective-permute-start | bytes 829448 | tf_op jit(solution)/shard_map/ppermute | solution.py:375
  134.3 21.7 %collective-permute-start.14 = (bf16[1080,128]{1,0:T(8,128)(2,1)S(1)}, bf16[1080,128]{1,0:T(8,128)(2,1)S(1)}, u32[]{:S(2)}, u32[]{:S(2)}) collective-permute-start(bf16[1080,128]{1,0:T(8,128)(2,1)S(1)} %get-tuple-element.92), channel_id=1, source_target_pairs={{0,96},{16,112},{32,0},{48,16},{64,32},{80,48},{96,64},{112,80},{1... | collective-permute-start | bytes 829448 | tf_op jit(solution)/shard_map/ppermute | solution.py:375
  138.3 19.2 %collective-permute-start.15 = (bf16[1080,128]{1,0:T(8,128)(2,1)S(1)}, bf16[1080,128]{1,0:T(8,128)(2,1)S(1)}, u32[]{:S(2)}, u32[]{:S(2)}) collective-permute-start(bf16[1080,128]{1,0:T(8,128)(2,1)S(1)} %get-tuple-element.93), channel_id=1, source_target_pairs={{0,16},{16,32},{32,48},{48,64},{64,80},{80,96},{96,112},{112,0},{1... | collective-permute-start | bytes 829448 | tf_op jit(solution)/shard_map/ppermute | solution.py:375
  142.7 14.8 %collective-permute-start.16 = (bf16[1080,128]{1,0:T(8,128)(2,1)S(1)}, bf16[1080,128]{1,0:T(8,128)(2,1)S(1)}, u32[]{:S(2)}, u32[]{:S(2)}) collective-permute-start(bf16[1080,128]{1,0:T(8,128)(2,1)S(1)} %get-tuple-element.94), channel_id=1, source_target_pairs={{0,112},{16,0},{32,16},{48,32},{64,48},{80,64},{96,80},{112,96},{1... | collective-permute-start | bytes 829448 | tf_op jit(solution)/shard_map/ppermute | solution.py:375
  153.0 11.2 %collective-permute-start.10 = (bf16[1080,128]{1,0:T(8,128)(2,1)S(1)}, bf16[1080,128]{1,0:T(8,128)(2,1)S(1)}, u32[]{:S(2)}, u32[]{:S(2)}) collective-permute-start(bf16[1080,128]{1,0:T(8,128)(2,1)S(1)} %get-tuple-element.88), channel_id=1, source_target_pairs={{0,64},{16,80},{32,96},{48,112},{64,0},{80,16},{96,32},{112,48},{1... | collective-permute-start | bytes 829448 | tf_op jit(solution)/shard_map/ppermute | solution.py:375
  155.8 13.0 %collective-permute-start.11 = (bf16[1080,128]{1,0:T(8,128)(2,1)S(1)}, bf16[1080,128]{1,0:T(8,128)(2,1)S(1)}, u32[]{:S(2)}, u32[]{:S(2)}) collective-permute-start(bf16[1080,128]{1,0:T(8,128)(2,1)S(1)} %get-tuple-element.89), channel_id=1, source_target_pairs={{0,80},{16,96},{32,112},{48,0},{64,16},{80,32},{96,48},{112,64},{1... | collective-permute-start | bytes 829448 | tf_op jit(solution)/shard_map/ppermute | solution.py:375
  156.0 17.6 %collective-permute-start.12 = (bf16[1080,128]{1,0:T(8,128)(2,1)S(1)}, bf16[1080,128]{1,0:T(8,128)(2,1)S(1)}, u32[]{:S(2)}, u32[]{:S(2)}) collective-permute-start(bf16[1080,128]{1,0:T(8,128)(2,1)S(1)} %get-tuple-element.90), channel_id=1, source_target_pairs={{0,48},{16,64},{32,80},{48,96},{64,112},{80,0},{96,16},{112,32},{1... | collective-permute-start | bytes 829448 | tf_op jit(solution)/shard_map/ppermute | solution.py:375
  157.5 23.4 %copy-start.5 = (bf16[6,96,768]{2,1,0:T(8,128)(2,1)S(1)}, bf16[6,96,768]{2,1,0:T(8,128)(2,1)}, u32[]{:S(2)}) copy-start(bf16[6,96,768]{2,1,0:T(8,128)(2,1)} %get-tuple-element.77.refs_0_.refs_8_) | copy-start | bytes 2654212
  157.5 68.3 %slice-start = ((s8[4718592]{0:T(1024)(128)(4,1)}), s8[524288]{0:T(1024)(128)(4,1)S(1)}, s32[]{:S(2)}) async-start(s8[4718592]{0:T(1024)(128)(4,1)} %bitcast.15), calls=%async_computation.4 | async-start | bytes 1048576
  161.0 15.1 %collective-permute-start.17 = (bf16[1080,128]{1,0:T(8,128)(2,1)S(1)}, bf16[1080,128]{1,0:T(8,128)(2,1)S(1)}, u32[]{:S(2)}, u32[]{:S(2)}) collective-permute-start(bf16[1080,128]{1,0:T(8,128)(2,1)S(1)} %get-tuple-element.96), channel_id=1, source_target_pairs={{0,96},{16,112},{32,0},{48,16},{64,32},{80,48},{96,64},{112,80},{1... | collective-permute-start | bytes 829448 | tf_op jit(solution)/shard_map/ppermute | solution.py:375
  164.0 16.8 %collective-permute-start.18 = (bf16[1080,128]{1,0:T(8,128)(2,1)S(1)}, bf16[1080,128]{1,0:T(8,128)(2,1)S(1)}, u32[]{:S(2)}, u32[]{:S(2)}) collective-permute-start(bf16[1080,128]{1,0:T(8,128)(2,1)S(1)} %get-tuple-element.97), channel_id=1, source_target_pairs={{0,32},{16,48},{32,64},{48,80},{64,96},{80,112},{96,0},{112,16},{1... | collective-permute-start | bytes 829448 | tf_op jit(solution)/shard_map/ppermute | solution.py:375
  164.2 16.6 %collective-permute-start.19 = (bf16[1080,128]{1,0:T(8,128)(2,1)S(1)}, bf16[1080,128]{1,0:T(8,128)(2,1)S(1)}, u32[]{:S(2)}, u32[]{:S(2)}) collective-permute-start(bf16[1080,128]{1,0:T(8,128)(2,1)S(1)} %get-tuple-element.98), channel_id=1, source_target_pairs={{0,112},{16,0},{32,16},{48,32},{64,48},{80,64},{96,80},{112,96},{1... | collective-permute-start | bytes 829448 | tf_op jit(solution)/shard_map/ppermute | solution.py:375
  168.8 12.2 %collective-permute-start.20 = (bf16[1080,128]{1,0:T(8,128)(2,1)S(1)}, bf16[1080,128]{1,0:T(8,128)(2,1)S(1)}, u32[]{:S(2)}, u32[]{:S(2)}) collective-permute-start(bf16[1080,128]{1,0:T(8,128)(2,1)S(1)} %get-tuple-element.99), channel_id=1, source_target_pairs={{0,16},{16,32},{32,48},{48,64},{64,80},{80,96},{96,112},{112,0},{1... | collective-permute-start | bytes 829448 | tf_op jit(solution)/shard_map/ppermute | solution.py:375
  180.9 44.9 %slice-start.1 = ((s8[4718592]{0:T(1024)(128)(4,1)}), s8[4194304]{0:T(1024)(128)(4,1)S(1)}, s32[]{:S(2)}) async-start(s8[4718592]{0:T(1024)(128)(4,1)} %bitcast.15), calls=%async_computation.5 | async-start | bytes 8388608
  231.9 34.6 %copy-start.7 = (bf16[90,90,128]{2,1,0:T(8,128)(2,1)S(1)}, bf16[90,90,128]{2,1,0:T(8,128)(2,1)}, u32[]{:S(2)}) copy-start(bf16[90,90,128]{2,1,0:T(8,128)(2,1)} %param.9) | copy-start | bytes 6220804
  (4 other events, 12.3 us)

commit v6 on v5

--- a/solution.py
+++ b/solution.py
@@ -22,7 +22,7 @@
 DEGPAD = 768
 COEF = DEG * RM
 PART = BAND * RM
-STEP = 15
+STEP = 30
 SHIFTS = (0, 1, 7, 2, 6, 3, 5, 4)
 GROUPS = ((4, 3, 5), (2, 6, 1, 7, 0))
 SENDS = GROUPS[0] + GROUPS[1]
@@ -100,7 +100,7 @@
     x = jnp.concatenate(
         [x_ref[:, 0].reshape(LON * PAD, CH), x_ref[:, 1].reshape(LON * PAD, CH)], axis=1
     )
-    rows = 768
+    rows = 1536
 
     @pl.loop(0, RM * ALL // rows)
     def _(chunk):
@@ -232,7 +232,7 @@
         ],
         axis=1,
     ).astype(jnp.bfloat16)
-    blocks = 8
+    blocks = 16
     rows = blocks * PAD
 
     @pl.loop(0, LON // blocks)

time: 269 us -> 267 us (level)
  Pallas kernels: 42.4 us -> 39.7 us
  transfers between devices with their start and end apart: 23 -> 23, of which waited for: 15 -> 15; matrix products, arithmetic and copies ran while one was open for 1% -> 1% of each run, Pallas kernels for 8% -> 7%
where the time goes in v6:
time: 267 us
  waiting for transfers between devices  92.3 us (35%)
  blocking collectives  73 us (27%)
  starting transfers between devices  52.9 us (20%)
  Pallas kernels  39.7 us (15%)
  local copies, waits for them, and re-layouts  6.7 us (3%)
    all_to_all x2, blocking collectives, swap(): return lax.all_to_all(x, axes, split_axis=0, concat_axis=0, tiled=True)  73 us
    ppermute x21, waiting for transfers between devices, shifted(): lax.ppermute(part, 'lat', [(i, (i + shift) % LAT) for i in range(LAT)])  69.9 us
    ppermute x21, starting transfers between devices, shifted(): lax.ppermute(part, 'lat', [(i, (i + shift) % LAT) for i in range(LAT)])  32.1 us
    all_to_all x2, waiting for transfers between devices, swap(): return lax.all_to_all(x, axes, split_axis=0, concat_axis=0, tiled=True)  22.4 us
    all_to_all x2, starting transfers between devices, swap(): return lax.all_to_all(x, axes, split_axis=0, concat_axis=0, tiled=True)  20.8 us
    pallas_call x2, Pallas kernels, legendre_call(): pl.pallas_call(kernel, grid=(OWN,), in_specs=[pl.BlockSpec(memory_space=p...  13.3 us
    pallas_call x3, Pallas kernels, cut(): pl.pallas_call(functools.partial(cut_kernel, places), grid_spec=pltpu.Pre...  8.45 us
    pallas_call x2, Pallas kernels, mix(): pl.pallas_call(mix_kernel, grid=(BAND // STEP,), in_specs=[whole((PART, C...  5.7 us
  transfers between devices with their start and end apart: 23, of which 15 were waited for; matrix products, arithmetic and copies ran while one was open for 1% of the time, Pallas kernels for 7%

profile of v6, /device:TPU:0, one launch (start us, length us, event | category | flops | bytes accessed | tf_op | source)
XLA Modules:
  0.0 266.8 jit_solution(3211201464925714418)
XLA Ops:
  0.0 2.5 cut.3
  2.5 3.0 %collective-permute-start.1 = (bf16[6,96,768]{2,1,0:T(8,128)(2,1)}, bf16[6,96,768]{2,1,0:T(8,128)(2,1)}, u32[]{:S(2)}, u32[]{:S(2)}) collective-permute-start(bf16[6,96,768]{2,1,0:T(8,128)(2,1)} %get-tuple-element.66), channel_id=1, source_target_pairs={{0,112},{16,0},{32,16},{48,32},{64,48},{80,64},{96,80},{112,96},{1... | collective-permute-start | bytes 2654216 | tf_op jit(solution)/shard_map/ppermute | solution.py:375
  5.5 2.5 cut.4
  8.3 2.9 %collective-permute-start.3 = (bf16[6,96,768]{2,1,0:T(8,128)(2,1)}, bf16[6,96,768]{2,1,0:T(8,128)(2,1)}, u32[]{:S(2)}, u32[]{:S(2)}) collective-permute-start(bf16[6,96,768]{2,1,0:T(8,128)(2,1)} %get-tuple-element.68), channel_id=1, source_target_pairs={{0,96},{16,112},{32,0},{48,16},{64,32},{80,48},{96,64},{112,80},{1... | collective-permute-start | bytes 2654216 | tf_op jit(solution)/shard_map/ppermute | solution.py:375
  11.2 3.5 %cut.5 = (bf16[6,96,768]{2,1,0:T(8,128)(2,1)}, bf16[6,96,768]{2,1,0:T(8,128)(2,1)}, bf16[6,96,768]{2,1,0:T(8,128)(2,1)}, bf16[6,96,768]{2,1,0:T(8,128)(2,1)}) custom-call(s32[1]{0:T(128)} %bitcast.1.p_ref, s32[1]{0:T(128)} %bitcast.2.q_ref, bf16[45,90,720]{2,1,0:T(8,128)(2,1)} %bitcast.21, bf16[45,90,720]{2,1,0:T(8,128)(2,1)} %bitcast.22, ...), custom_call_target="tpu_custom_call" | custom-call | flops 4000000 | bytes 6800000 | tf_op jit(solution)/shard_map/cut/pallas_call | solution.py:258
  17.0 8.2 %all-to-all-start = ((bf16[96,96,128]{2,1,0:T(8,128)(2,1)}), bf16[96,96,128]{2,1,0:T(8,128)(2,1)S(1)}, u32[]{:S(2)}, u32[]{:S(2)}) async-start(bf16[96,96,128]{2,1,0:T(8,128)(2,1)} %pad.8), calls=%async_computation | async-start | bytes 4718592 | tf_op jit(solution)/shard_map/all_to_all | solution.py:369
  25.2 7.0 %collective-permute-done.2.refs_3_.refs_11_ = bf16[6,96,768]{2,1,0:T(8,128)(2,1)} collective-permute-done((bf16[6,96,768]{2,1,0:T(8,128)(2,1)}, bf16[6,96,768]{2,1,0:T(8,128)(2,1)}, u32[]{:S(2)}, u32[]{:S(2)}) %collective-permute-start.2) | collective-permute-done | bytes 884768 | tf_op jit(solution)/shard_map/ppermute | solution.py:375
  32.2 10.2 %collective-permute-done.3.refs_4_.refs_12_ = bf16[6,96,768]{2,1,0:T(8,128)(2,1)} collective-permute-done((bf16[6,96,768]{2,1,0:T(8,128)(2,1)}, bf16[6,96,768]{2,1,0:T(8,128)(2,1)}, u32[]{:S(2)}, u32[]{:S(2)}) %collective-permute-start.3) | collective-permute-done | bytes 884768 | tf_op jit(solution)/shard_map/ppermute | solution.py:375
  42.4 8.4 %collective-permute-done.4.refs_7_.refs_15_ = bf16[6,96,768]{2,1,0:T(8,128)(2,1)} collective-permute-done((bf16[6,96,768]{2,1,0:T(8,128)(2,1)}, bf16[6,96,768]{2,1,0:T(8,128)(2,1)}, u32[]{:S(2)}, u32[]{:S(2)}) %collective-permute-start.4) | collective-permute-done | bytes 884768 | tf_op jit(solution)/shard_map/ppermute | solution.py:375
  52.1 5.0 %collective-permute-start.6 = (bf16[6,96,768]{2,1,0:T(8,128)(2,1)}, bf16[6,96,768]{2,1,0:T(8,128)(2,1)}, u32[]{:S(2)}, u32[]{:S(2)}) collective-permute-start(bf16[6,96,768]{2,1,0:T(8,128)(2,1)} %get-tuple-element.74), channel_id=1, source_target_pairs={{0,80},{16,96},{32,112},{48,0},{64,16},{80,32},{96,48},{112,64},{1... | collective-permute-start | bytes 2654216 | tf_op jit(solution)/shard_map/ppermute | solution.py:375
  60.3 5.2 %dft.1 = bf16[9216,128]{1,0:T(8,128)(2,1)S(1)} custom-call(f32[6]{0:T(128)S(1)} %pad_dynamic-slice_fusion.quad_ref, bf16[16,6,96,128]{3,2,1,0:T(8,128)(2,1)S(1)} %bitcast.10, bf16[1536,1536]{1,0:T(8,128)(2,1)S(1)} %copy-done.3), custom_call_target="tpu_custom_call" | custom-call | flops 1000000 | bytes 100000 | tf_op jit(solution)/shard_map/dft/pallas_call | solution.py:293
  67.0 12.7 %all-to-all-start.1 = ((bf16[128,72,128]{2,1,0:T(8,128)(2,1)}), bf16[128,72,128]{2,1,0:T(8,128)(2,1)S(1)}, u32[]{:S(2)}, u32[]{:S(2)}) async-start(bf16[128,72,128]{2,1,0:T(8,128)(2,1)} %bitcast.12), calls=%async_computation.1 | async-start | bytes 4718592 | tf_op jit(solution)/shard_map/all_to_all | solution.py:369
  79.6 17.4 %collective-permute-done.6.refs_6_.refs_14_ = bf16[6,96,768]{2,1,0:T(8,128)(2,1)} collective-permute-done((bf16[6,96,768]{2,1,0:T(8,128)(2,1)}, bf16[6,96,768]{2,1,0:T(8,128)(2,1)}, u32[]{:S(2)}, u32[]{:S(2)}) %collective-permute-start.6) | collective-permute-done | bytes 884768 | tf_op jit(solution)/shard_map/ppermute | solution.py:375
  98.2 21.6 %all-to-all-done.1 = bf16[128,72,128]{2,1,0:T(8,128)(2,1)S(1)} async-done(((bf16[128,72,128]{2,1,0:T(8,128)(2,1)}), bf16[128,72,128]{2,1,0:T(8,128)(2,1)S(1)}, u32[]{:S(2)}, u32[]{:S(2)}) %all-to-all-start.1) | async-done | bytes 2359328 | tf_op jit(solution)/shard_map/all_to_all | solution.py:369
  121.0 6.7 %legendre.1 = (bf16[1080,128]{1,0:T(8,128)(2,1)S(1)}, bf16[1080,128]{1,0:T(8,128)(2,1)S(1)}, bf16[1080,128]{1,0:T(8,128)(2,1)S(1)}, bf16[1080,128]{1,0:T(8,128)(...) custom-call(s32[8]{0:T(128)S(1)} %compare_select_fusion.2.src_ref, ...), custom_call_target="tpu_custom_call" | custom-call | flops 1811939328 | bytes 12000000 | tf_op jit(solution)/shard_map/legendre/pallas_call | solution.py:314
  127.7 2.5 collective-permute-start.7
  131.1 2.4 collective-permute-start.9
  134.3 2.4 collective-permute-start.14
  138.3 4.4 %collective-permute-done.8.refs_1_ = bf16[1080,128]{1,0:T(8,128)(2,1)S(1)} collective-permute-done((bf16[1080,128]{1,0:T(8,128)(2,1)S(1)}, bf16[1080,128]{1,0:T(8,128)(2,1)S(1)}, u32[]{:S(2)}, u32[]{:S(2)}) %collective-permute-start.8) | collective-permute-done | bytes 276512 | tf_op jit(solution)/shard_map/ppermute | solution.py:375
  144.5 5.5 %collective-permute-done.9.refs_2_ = bf16[1080,128]{1,0:T(8,128)(2,1)S(1)} collective-permute-done((bf16[1080,128]{1,0:T(8,128)(2,1)S(1)}, bf16[1080,128]{1,0:T(8,128)(2,1)S(1)}, u32[]{:S(2)}, u32[]{:S(2)}) %collective-permute-start.9) | collective-permute-done | bytes 276512 | tf_op jit(solution)/shard_map/ppermute | solution.py:375
  149.9 2.7 %mix.2 = (bf16[1080,128]{1,0:T(8,128)(2,1)S(1)}, bf16[1080,128]{1,0:T(8,128)(2,1)S(1)}, bf16[1080,128]{1,0:T(8,128)(2,1)S(1)}) custom-call(bf16[1080,128]{1,0:T(8,128)(2,1)S(1)} %collective-permute-done.7.refs_0_, bf16[1080,128]{1,0:T(8,128)(2,1)S(1)} %collective-permute-done.8.refs_1_, bf16[1080,128]{1,0:T(8,128)(2,1)S(1)} %collective-permute-done.9.refs_2_, ...), custom_call_target="tpu_custom_call" | custom-call | flops 566231040 | bytes 10000000 | tf_op jit(solution)/shard_map/mix/pallas_call | solution.py:337
  152.6 2.7 %collective-permute-start.10 = (bf16[1080,128]{1,0:T(8,128)(2,1)S(1)}, bf16[1080,128]{1,0:T(8,128)(2,1)S(1)}, u32[]{:S(2)}, u32[]{:S(2)}) collective-permute-start(bf16[1080,128]{1,0:T(8,128)(2,1)S(1)} %get-tuple-element.88), channel_id=1, source_target_pairs={{0,64},{16,80},{32,96},{48,112},{64,0},{80,16},{96,32},{112,48},{1... | collective-permute-start | bytes 829448 | tf_op jit(solution)/shard_map/ppermute | solution.py:375
  157.1 3.0 %mix.3 = (bf16[1080,128]{1,0:T(8,128)(2,1)S(1)}, bf16[1080,128]{1,0:T(8,128)(2,1)S(1)}, bf16[1080,128]{1,0:T(8,128)(2,1)S(1)}, bf16[1080,128]{1,0:T(8,128)(2,1)S(1)}, bf16[1080,128]{1,0:T(8,128)(2,1)S(1)}) custom-call(bf16[1080,128]{1,0:T(8,128)(2,1)S(1)} %collective-permute-done.13.refs_0_, bf16[1080,128]{1,0:T(8,128)(2,1)S(1)} %collective-permute-done.14.refs_1_, ...), custom_call_target="tpu_custom_call" | custom-call | flops 566231040 | bytes 10000000 | tf_op jit(solution)/shard_map/mix/pallas_call | solution.py:337
  160.2 3.0 %collective-permute-start.17 = (bf16[1080,128]{1,0:T(8,128)(2,1)S(1)}, bf16[1080,128]{1,0:T(8,128)(2,1)S(1)}, u32[]{:S(2)}, u32[]{:S(2)}) collective-permute-start(bf16[1080,128]{1,0:T(8,128)(2,1)S(1)} %get-tuple-element.96), channel_id=1, source_target_pairs={{0,96},{16,112},{32,0},{48,16},{64,32},{80,48},{96,64},{112,80},{1... | collective-permute-start | bytes 829448 | tf_op jit(solution)/shard_map/ppermute | solution.py:375
  164.6 3.7 %collective-permute-done.11.refs_1_ = bf16[1080,128]{1,0:T(8,128)(2,1)S(1)} collective-permute-done((bf16[1080,128]{1,0:T(8,128)(2,1)S(1)}, bf16[1080,128]{1,0:T(8,128)(2,1)S(1)}, u32[]{:S(2)}, u32[]{:S(2)}) %collective-permute-start.11) | collective-permute-done | bytes 276512 | tf_op jit(solution)/shard_map/ppermute | solution.py:375
  169.5 3.7 %collective-permute-done.12.refs_2_ = bf16[1080,128]{1,0:T(8,128)(2,1)S(1)} collective-permute-done((bf16[1080,128]{1,0:T(8,128)(2,1)S(1)}, bf16[1080,128]{1,0:T(8,128)(2,1)S(1)}, u32[]{:S(2)}, u32[]{:S(2)}) %collective-permute-start.12) | collective-permute-done | bytes 276512 | tf_op jit(solution)/shard_map/ppermute | solution.py:375
  173.2 2.5 collective-permute-done.17.refs_3_
  175.7 4.7 %collective-permute-done.18.refs_4_ = bf16[1080,128]{1,0:T(8,128)(2,1)S(1)} collective-permute-done((bf16[1080,128]{1,0:T(8,128)(2,1)S(1)}, bf16[1080,128]{1,0:T(8,128)(2,1)S(1)}, u32[]{:S(2)}, u32[]{:S(2)}) %collective-permute-start.18) | collective-permute-done | bytes 276512 | tf_op jit(solution)/shard_map/ppermute | solution.py:375
  180.5 6.6 %inverse_legendre.1 = bf16[9216,128]{1,0:T(8,128)(2,1)S(1)} custom-call(s32[8]{0:T(128)S(1)} %compare_select_fusion.2.src_ref, s32[8]{0:T(128)S(1)} %in_order.3.dest_ref, bf16[1080,128]{1,0:T(8,128)(2,1)S(1)} %collective-permute-done.10.refs_0_, bf16[1080,128]{1,0:T(8,128)(2,1)S(1)} %collective-permute-done.11.refs_1_, ...), custom_call_target="tpu_custom_call" | custom-call | flops 1811939328 | bytes 12000000 | tf_op jit(solution)/shard_map/inverse_legendre/pallas_call | solution.py:314
  187.1 38.3 %all_to_all.32 = bf16[128,72,128]{2,1,0:T(8,128)(2,1)S(1)} all-to-all(bf16[128,72,128]{2,1,0:T(8,128)(2,1)S(1)} %bitcast.11), channel_id=1, replica_groups=mesh['lat'=8,'lon'=16] {'lat','lon'}, dimensions={0} | all-to-all | bytes 4718592 | tf_op jit(solution)/shard_map/all_to_all | solution.py:369
  225.4 4.8 %inverse_dft.1 = bf16[16,6,96,128]{3,2,1,0:T(8,128)(2,1)S(1)} custom-call(bf16[9216,128]{1,0:T(8,128)(2,1)S(1)} %bitcast.13, bf16[1536,1536]{1,0:T(8,128)(2,1)S(1)} %bitcast.16), custom_call_target="tpu_custom_call" | custom-call | flops 3623878656 | bytes 10000000 | tf_op jit(solution)/shard_map/inverse_dft/pallas_call | solution.py:353
  230.2 34.6 %all_to_all.33 = bf16[96,96,128]{2,1,0:T(8,128)(2,1)S(1)} all-to-all(bf16[96,96,128]{2,1,0:T(8,128)(2,1)S(1)} %bitcast.14), channel_id=1, replica_groups=mesh['lat'=8,'lon'=16] {'lon'}, dimensions={0} | all-to-all | bytes 4718592 | tf_op jit(solution)/shard_map/all_to_all | solution.py:369
  (59 shorter events, 22.3 us)
Async XLA Ops:
  2.5 22.7 %collective-permute-start = (bf16[6,96,768]{2,1,0:T(8,128)(2,1)}, bf16[6,96,768]{2,1,0:T(8,128)(2,1)S(1)}, u32[]{:S(2)}, u32[]{:S(2)}) collective-permute-start(bf16[6,96,768]{2,1,0:T(8,128)(2,1)} %get-tuple-element.65), channel_id=1, source_target_pairs={{0,16},{16,32},{32,48},{48,64},{64,80},{80,96},{96,112},{112,0},{1... | collective-permute-start | bytes 2654216 | tf_op jit(solution)/shard_map/ppermute | solution.py:375
  2.5 22.7 %collective-permute-start.1 = (bf16[6,96,768]{2,1,0:T(8,128)(2,1)}, bf16[6,96,768]{2,1,0:T(8,128)(2,1)}, u32[]{:S(2)}, u32[]{:S(2)}) collective-permute-start(bf16[6,96,768]{2,1,0:T(8,128)(2,1)} %get-tuple-element.66), channel_id=1, source_target_pairs={{0,112},{16,0},{32,16},{48,32},{64,48},{80,64},{96,80},{112,96},{1... | collective-permute-start | bytes 2654216 | tf_op jit(solution)/shard_map/ppermute | solution.py:375
  7.9 24.2 %collective-permute-start.2 = (bf16[6,96,768]{2,1,0:T(8,128)(2,1)}, bf16[6,96,768]{2,1,0:T(8,128)(2,1)}, u32[]{:S(2)}, u32[]{:S(2)}) collective-permute-start(bf16[6,96,768]{2,1,0:T(8,128)(2,1)} %get-tuple-element.67), channel_id=1, source_target_pairs={{0,32},{16,48},{32,64},{48,80},{64,96},{80,112},{96,0},{112,16},{1... | collective-permute-start | bytes 2654216 | tf_op jit(solution)/shard_map/ppermute | solution.py:375
  8.3 34.1 %collective-permute-start.3 = (bf16[6,96,768]{2,1,0:T(8,128)(2,1)}, bf16[6,96,768]{2,1,0:T(8,128)(2,1)}, u32[]{:S(2)}, u32[]{:S(2)}) collective-permute-start(bf16[6,96,768]{2,1,0:T(8,128)(2,1)} %get-tuple-element.68), channel_id=1, source_target_pairs={{0,96},{16,112},{32,0},{48,16},{64,32},{80,48},{96,64},{112,80},{1... | collective-permute-start | bytes 2654216 | tf_op jit(solution)/shard_map/ppermute | solution.py:375
  14.6 36.2 %collective-permute-start.4 = (bf16[6,96,768]{2,1,0:T(8,128)(2,1)}, bf16[6,96,768]{2,1,0:T(8,128)(2,1)}, u32[]{:S(2)}, u32[]{:S(2)}) collective-permute-start(bf16[6,96,768]{2,1,0:T(8,128)(2,1)} %get-tuple-element.69), channel_id=1, source_target_pairs={{0,64},{16,80},{32,96},{48,112},{64,0},{80,16},{96,32},{112,48},{1... | collective-permute-start | bytes 2654216 | tf_op jit(solution)/shard_map/ppermute | solution.py:375
  17.0 8.2 %copy-start.10 = (s32[8]{0:T(128)S(1)}, s32[8]{0:T(128)}, u32[]{:S(2)}) copy-start(s32[8]{0:T(128)} %constant.35.clone) | copy-start | bytes 100
  17.0 41.0 %all-to-all-start = ((bf16[96,96,128]{2,1,0:T(8,128)(2,1)}), bf16[96,96,128]{2,1,0:T(8,128)(2,1)S(1)}, u32[]{:S(2)}, u32[]{:S(2)}) async-start(bf16[96,96,128]{2,1,0:T(8,128)(2,1)} %pad.8), calls=%async_computation | async-start | bytes 4718592 | tf_op jit(solution)/shard_map/all_to_all | solution.py:369
  25.2 31.9 %copy-start.8 = (f32[90]{0:T(128)S(1)}, f32[90]{0:T(128)}, u32[]{:S(2)}) copy-start(f32[90]{0:T(128)} %param.11) | copy-start | bytes 1084
  25.2 31.9 %copy-start.9 = (s32[8]{0:T(128)S(1)}, s32[8]{0:T(128)}, u32[]{:S(2)}) copy-start(s32[8]{0:T(128)} %constant.47) | copy-start | bytes 100
  52.0 27.6 %collective-permute-start.5 = (bf16[6,96,768]{2,1,0:T(8,128)(2,1)}, bf16[6,96,768]{2,1,0:T(8,128)(2,1)}, u32[]{:S(2)}, u32[]{:S(2)}) collective-permute-start(bf16[6,96,768]{2,1,0:T(8,128)(2,1)} %get-tuple-element.73), channel_id=1, source_target_pairs={{0,48},{16,64},{32,80},{48,96},{64,112},{80,0},{96,16},{112,32},{1... | collective-permute-start | bytes 2654216 | tf_op jit(solution)/shard_map/ppermute | solution.py:375
  52.1 45.0 %collective-permute-start.6 = (bf16[6,96,768]{2,1,0:T(8,128)(2,1)}, bf16[6,96,768]{2,1,0:T(8,128)(2,1)}, u32[]{:S(2)}, u32[]{:S(2)}) collective-permute-start(bf16[6,96,768]{2,1,0:T(8,128)(2,1)} %get-tuple-element.74), channel_id=1, source_target_pairs={{0,80},{16,96},{32,112},{48,0},{64,16},{80,32},{96,48},{112,64},{1... | collective-permute-start | bytes 2654216 | tf_op jit(solution)/shard_map/ppermute | solution.py:375
  67.0 52.8 %all-to-all-start.1 = ((bf16[128,72,128]{2,1,0:T(8,128)(2,1)}), bf16[128,72,128]{2,1,0:T(8,128)(2,1)S(1)}, u32[]{:S(2)}, u32[]{:S(2)}) async-start(bf16[128,72,128]{2,1,0:T(8,128)(2,1)} %bitcast.12), calls=%async_computation.1 | async-start | bytes 4718592 | tf_op jit(solution)/shard_map/all_to_all | solution.py:369
  121.0 29.0 %copy-start = (bf16[90,128,128]{2,1,0:T(8,128)(2,1)S(1)}, bf16[90,128,128]{2,1,0:T(8,128)(2,1)}, u32[]{:S(2)}) copy-start(bf16[90,128,128]{2,1,0:T(8,128)(2,1)} %refs_5_.1) | copy-start | bytes 8847364
  121.0 29.0 %copy-start.1 = (bf16[90,128,128]{2,1,0:T(8,128)(2,1)S(1)}, bf16[90,128,128]{2,1,0:T(8,128)(2,1)}, u32[]{:S(2)}) copy-start(bf16[90,128,128]{2,1,0:T(8,128)(2,1)} %refs_6_.1) | copy-start | bytes 8847364
  127.7 10.6 %collective-permute-start.7 = (bf16[1080,128]{1,0:T(8,128)(2,1)S(1)}, bf16[1080,128]{1,0:T(8,128)(2,1)S(1)}, u32[]{:S(2)}, u32[]{:S(2)}) collective-permute-start(bf16[1080,128]{1,0:T(8,128)(2,1)S(1)} %get-tuple-element.85), channel_id=1, source_target_pairs={{0,64},{16,80},{32,96},{48,112},{64,0},{80,16},{96,32},{112,48},{1... | collective-permute-start | bytes 829448 | tf_op jit(solution)/shard_map/ppermute | solution.py:375
  130.2 12.5 %collective-permute-start.8 = (bf16[1080,128]{1,0:T(8,128)(2,1)S(1)}, bf16[1080,128]{1,0:T(8,128)(2,1)S(1)}, u32[]{:S(2)}, u32[]{:S(2)}) collective-permute-start(bf16[1080,128]{1,0:T(8,128)(2,1)S(1)} %get-tuple-element.86), channel_id=1, source_target_pairs={{0,48},{16,64},{32,80},{48,96},{64,112},{80,0},{96,16},{112,32},{1... | collective-permute-start | bytes 829448 | tf_op jit(solution)/shard_map/ppermute | solution.py:375
  131.1 18.8 %collective-permute-start.9 = (bf16[1080,128]{1,0:T(8,128)(2,1)S(1)}, bf16[1080,128]{1,0:T(8,128)(2,1)S(1)}, u32[]{:S(2)}, u32[]{:S(2)}) collective-permute-start(bf16[1080,128]{1,0:T(8,128)(2,1)S(1)} %get-tuple-element.87), channel_id=1, source_target_pairs={{0,80},{16,96},{32,112},{48,0},{64,16},{80,32},{96,48},{112,64},{1... | collective-permute-start | bytes 829448 | tf_op jit(solution)/shard_map/ppermute | solution.py:375
  133.5 21.9 %collective-permute-start.13 = (bf16[1080,128]{1,0:T(8,128)(2,1)S(1)}, bf16[1080,128]{1,0:T(8,128)(2,1)S(1)}, u32[]{:S(2)}, u32[]{:S(2)}) collective-permute-start(bf16[1080,128]{1,0:T(8,128)(2,1)S(1)} %get-tuple-element.91), channel_id=1, source_target_pairs={{0,32},{16,48},{32,64},{48,80},{64,96},{80,112},{96,0},{112,16},{1... | collective-permute-start | bytes 829448 | tf_op jit(solution)/shard_map/ppermute | solution.py:375
  134.3 21.3 %collective-permute-start.14 = (bf16[1080,128]{1,0:T(8,128)(2,1)S(1)}, bf16[1080,128]{1,0:T(8,128)(2,1)S(1)}, u32[]{:S(2)}, u32[]{:S(2)}) collective-permute-start(bf16[1080,128]{1,0:T(8,128)(2,1)S(1)} %get-tuple-element.92), channel_id=1, source_target_pairs={{0,96},{16,112},{32,0},{48,16},{64,32},{80,48},{96,64},{112,80},{1... | collective-permute-start | bytes 829448 | tf_op jit(solution)/shard_map/ppermute | solution.py:375
  138.3 18.8 %collective-permute-start.15 = (bf16[1080,128]{1,0:T(8,128)(2,1)S(1)}, bf16[1080,128]{1,0:T(8,128)(2,1)S(1)}, u32[]{:S(2)}, u32[]{:S(2)}) collective-permute-start(bf16[1080,128]{1,0:T(8,128)(2,1)S(1)} %get-tuple-element.93), channel_id=1, source_target_pairs={{0,16},{16,32},{32,48},{48,64},{64,80},{80,96},{96,112},{112,0},{1... | collective-permute-start | bytes 829448 | tf_op jit(solution)/shard_map/ppermute | solution.py:375
  142.7 14.4 %collective-permute-start.16 = (bf16[1080,128]{1,0:T(8,128)(2,1)S(1)}, bf16[1080,128]{1,0:T(8,128)(2,1)S(1)}, u32[]{:S(2)}, u32[]{:S(2)}) collective-permute-start(bf16[1080,128]{1,0:T(8,128)(2,1)S(1)} %get-tuple-element.94), channel_id=1, source_target_pairs={{0,112},{16,0},{32,16},{48,32},{64,48},{80,64},{96,80},{112,96},{1... | collective-permute-start | bytes 829448 | tf_op jit(solution)/shard_map/ppermute | solution.py:375
  152.6 11.2 %collective-permute-start.10 = (bf16[1080,128]{1,0:T(8,128)(2,1)S(1)}, bf16[1080,128]{1,0:T(8,128)(2,1)S(1)}, u32[]{:S(2)}, u32[]{:S(2)}) collective-permute-start(bf16[1080,128]{1,0:T(8,128)(2,1)S(1)} %get-tuple-element.88), channel_id=1, source_target_pairs={{0,64},{16,80},{32,96},{48,112},{64,0},{80,16},{96,32},{112,48},{1... | collective-permute-start | bytes 829448 | tf_op jit(solution)/shard_map/ppermute | solution.py:375
  155.3 13.0 %collective-permute-start.11 = (bf16[1080,128]{1,0:T(8,128)(2,1)S(1)}, bf16[1080,128]{1,0:T(8,128)(2,1)S(1)}, u32[]{:S(2)}, u32[]{:S(2)}) collective-permute-start(bf16[1080,128]{1,0:T(8,128)(2,1)S(1)} %get-tuple-element.89), channel_id=1, source_target_pairs={{0,80},{16,96},{32,112},{48,0},{64,16},{80,32},{96,48},{112,64},{1... | collective-permute-start | bytes 829448 | tf_op jit(solution)/shard_map/ppermute | solution.py:375
  155.5 17.6 %collective-permute-start.12 = (bf16[1080,128]{1,0:T(8,128)(2,1)S(1)}, bf16[1080,128]{1,0:T(8,128)(2,1)S(1)}, u32[]{:S(2)}, u32[]{:S(2)}) collective-permute-start(bf16[1080,128]{1,0:T(8,128)(2,1)S(1)} %get-tuple-element.90), channel_id=1, source_target_pairs={{0,48},{16,64},{32,80},{48,96},{64,112},{80,0},{96,16},{112,32},{1... | collective-permute-start | bytes 829448 | tf_op jit(solution)/shard_map/ppermute | solution.py:375
  157.1 23.4 %copy-start.5 = (bf16[6,96,768]{2,1,0:T(8,128)(2,1)S(1)}, bf16[6,96,768]{2,1,0:T(8,128)(2,1)}, u32[]{:S(2)}) copy-start(bf16[6,96,768]{2,1,0:T(8,128)(2,1)} %get-tuple-element.77.refs_0_.refs_8_) | copy-start | bytes 2654212
  157.1 68.3 %slice-start = ((s8[4718592]{0:T(1024)(128)(4,1)}), s8[524288]{0:T(1024)(128)(4,1)S(1)}, s32[]{:S(2)}) async-start(s8[4718592]{0:T(1024)(128)(4,1)} %bitcast.15), calls=%async_computation.4 | async-start | bytes 1048576
  160.2 15.5 %collective-permute-start.17 = (bf16[1080,128]{1,0:T(8,128)(2,1)S(1)}, bf16[1080,128]{1,0:T(8,128)(2,1)S(1)}, u32[]{:S(2)}, u32[]{:S(2)}) collective-permute-start(bf16[1080,128]{1,0:T(8,128)(2,1)S(1)} %get-tuple-element.96), channel_id=1, source_target_pairs={{0,96},{16,112},{32,0},{48,16},{64,32},{80,48},{96,64},{112,80},{1... | collective-permute-start | bytes 829448 | tf_op jit(solution)/shard_map/ppermute | solution.py:375
  163.2 17.2 %collective-permute-start.18 = (bf16[1080,128]{1,0:T(8,128)(2,1)S(1)}, bf16[1080,128]{1,0:T(8,128)(2,1)S(1)}, u32[]{:S(2)}, u32[]{:S(2)}) collective-permute-start(bf16[1080,128]{1,0:T(8,128)(2,1)S(1)} %get-tuple-element.97), channel_id=1, source_target_pairs={{0,32},{16,48},{32,64},{48,80},{64,96},{80,112},{96,0},{112,16},{1... | collective-permute-start | bytes 829448 | tf_op jit(solution)/shard_map/ppermute | solution.py:375
  163.8 16.6 %collective-permute-start.19 = (bf16[1080,128]{1,0:T(8,128)(2,1)S(1)}, bf16[1080,128]{1,0:T(8,128)(2,1)S(1)}, u32[]{:S(2)}, u32[]{:S(2)}) collective-permute-start(bf16[1080,128]{1,0:T(8,128)(2,1)S(1)} %get-tuple-element.98), channel_id=1, source_target_pairs={{0,112},{16,0},{32,16},{48,32},{64,48},{80,64},{96,80},{112,96},{1... | collective-permute-start | bytes 829448 | tf_op jit(solution)/shard_map/ppermute | solution.py:375
  168.3 12.2 %collective-permute-start.20 = (bf16[1080,128]{1,0:T(8,128)(2,1)S(1)}, bf16[1080,128]{1,0:T(8,128)(2,1)S(1)}, u32[]{:S(2)}, u32[]{:S(2)}) collective-permute-start(bf16[1080,128]{1,0:T(8,128)(2,1)S(1)} %get-tuple-element.99), channel_id=1, source_target_pairs={{0,16},{16,32},{32,48},{48,64},{64,80},{80,96},{96,112},{112,0},{1... | collective-permute-start | bytes 829448 | tf_op jit(solution)/shard_map/ppermute | solution.py:375
  180.5 44.9 %slice-start.1 = ((s8[4718592]{0:T(1024)(128)(4,1)}), s8[4194304]{0:T(1024)(128)(4,1)S(1)}, s32[]{:S(2)}) async-start(s8[4718592]{0:T(1024)(128)(4,1)} %bitcast.15), calls=%async_computation.5 | async-start | bytes 8388608
  230.2 34.6 %copy-start.7 = (bf16[90,90,128]{2,1,0:T(8,128)(2,1)S(1)}, bf16[90,90,128]{2,1,0:T(8,128)(2,1)}, u32[]{:S(2)}) copy-start(bf16[90,90,128]{2,1,0:T(8,128)(2,1)} %param.9) | copy-start | bytes 6220804
  (4 other events, 12.3 us)

commit v7 on v6

--- a/solution.py
+++ b/solution.py
@@ -387,7 +387,7 @@
     src = lax.rem(p - shifts + LAT, LAT)
     dest = lax.rem(p + jnp.array(SENDS, jnp.int32), LAT)
     cuts = [None] * LAT
-    for group in ((1, 2), (3, 4), (5, 6, 7, 0)):
+    for group in ((1, 2), (3, 4), (7,), (5, 6, 0)):
         parts = cut(table, p, q, group)
         table, *parts = lax.optimization_barrier((table, *parts))
         for i, part in zip(group, parts):
@@ -403,8 +403,9 @@
             legs[i] = part
         return value
 
-    dest = in_order(end(dest, (1, 2, 3, 4, 7)))
+    dest = end(dest, (1, 2, 3, 4, 7))
     cuts[5:7], dest = lax.optimization_barrier((cuts[5:7], dest))
+    dest = in_order(dest)
     rows, dest = lax.optimization_barrier((rows, dest))
     spectrum = dft(quad, rows.reshape(LON, OWN, PAD, CH), jnp.asarray(forward_table))
     dest = in_order(end(dest, (5, 6)))

time: 267 us -> 265 us (level)
    pallas_call x3 -> x4, Pallas kernels: 8.45 us -> 10.2 us  [cut(): pl.pallas_call(functools.partial(cut_kernel, places), grid_spec=pltpu.Pre...]
  transfers between devices with their start and end apart: 23 -> 23, of which waited for: 15 -> 15; matrix products, arithmetic and copies ran while one was open for 1% -> 1% of each run, Pallas kernels for 7% -> 8%
where the time goes in v7:
time: 265 us
  waiting for transfers between devices  92.6 us (35%)
  blocking collectives  71.3 us (27%)
  starting transfers between devices  50.7 us (19%)
  Pallas kernels  41.5 us (16%)
  local copies, waits for them, and re-layouts  6.7 us (3%)
    all_to_all x2, blocking collectives, swap(): return lax.all_to_all(x, axes, split_axis=0, concat_axis=0, tiled=True)  71.3 us
    ppermute x21, waiting for transfers between devices, shifted(): lax.ppermute(part, 'lat', [(i, (i + shift) % LAT) for i in range(LAT)])  70.6 us
    ppermute x21, starting transfers between devices, shifted(): lax.ppermute(part, 'lat', [(i, (i + shift) % LAT) for i in range(LAT)])  31.7 us
    all_to_all x2, waiting for transfers between devices, swap(): return lax.all_to_all(x, axes, split_axis=0, concat_axis=0, tiled=True)  22.1 us
    all_to_all x2, starting transfers between devices, swap(): return lax.all_to_all(x, axes, split_axis=0, concat_axis=0, tiled=True)  19 us
    pallas_call x2, Pallas kernels, legendre_call(): pl.pallas_call(kernel, grid=(OWN,), in_specs=[pl.BlockSpec(memory_space=p...  13.3 us
    pallas_call x4, Pallas kernels, cut(): pl.pallas_call(functools.partial(cut_kernel, places), grid_spec=pltpu.Pre...  10.2 us
    pallas_call x2, Pallas kernels, mix(): pl.pallas_call(mix_kernel, grid=(BAND // STEP,), in_specs=[whole((PART, C...  5.7 us
  transfers between devices with their start and end apart: 23, of which 15 were waited for; matrix products, arithmetic and copies ran while one was open for 1% of the time, Pallas kernels for 8%

profile of v7, /device:TPU:0, one launch (start us, length us, event | category | flops | bytes accessed | tf_op | source)
XLA Modules:
  0.0 264.9 jit_solution(15541267056414227998)
XLA Ops:
  0.0 2.5 cut.4
  2.5 3.0 %collective-permute-start.1 = (bf16[6,96,768]{2,1,0:T(8,128)(2,1)}, bf16[6,96,768]{2,1,0:T(8,128)(2,1)}, u32[]{:S(2)}, u32[]{:S(2)}) collective-permute-start(bf16[6,96,768]{2,1,0:T(8,128)(2,1)} %get-tuple-element.66), channel_id=1, source_target_pairs={{0,112},{16,0},{32,16},{48,32},{64,48},{80,64},{96,80},{112,96},{1... | collective-permute-start | bytes 2654216 | tf_op jit(solution)/shard_map/ppermute | solution.py:375
  5.5 2.5 cut.5
  8.0 2.2 cut.6
  12.6 2.6 collective-permute-start.3
  16.9 8.0 %all-to-all-start = ((bf16[96,96,128]{2,1,0:T(8,128)(2,1)}), bf16[96,96,128]{2,1,0:T(8,128)(2,1)S(1)}, u32[]{:S(2)}, u32[]{:S(2)}) async-start(bf16[96,96,128]{2,1,0:T(8,128)(2,1)} %pad.8), calls=%async_computation | async-start | bytes 4718592 | tf_op jit(solution)/shard_map/all_to_all | solution.py:369
  25.0 3.0 %cut.7 = (bf16[6,96,768]{2,1,0:T(8,128)(2,1)}, bf16[6,96,768]{2,1,0:T(8,128)(2,1)}, bf16[6,96,768]{2,1,0:T(8,128)(2,1)}) custom-call(s32[1]{0:T(128)} %bitcast.1.p_ref, s32[1]{0:T(128)} %bitcast.2.q_ref, bf16[45,90,720]{2,1,0:T(8,128)(2,1)} %bitcast.22, bf16[45,90,720]{2,1,0:T(8,128)(2,1)} %bitcast.23, bf16[45,90,720]{2,1,0:T(8,128)(2,1)} %bitcast.24), custom_call_target="tpu_custom_call" | custom-call | flops 3000000 | bytes 5100000 | tf_op jit(solution)/shard_map/cut/pallas_call | solution.py:258
  28.1 8.6 %collective-permute-done.1.refs_2_.refs_10_ = bf16[6,96,768]{2,1,0:T(8,128)(2,1)} collective-permute-done((bf16[6,96,768]{2,1,0:T(8,128)(2,1)}, bf16[6,96,768]{2,1,0:T(8,128)(2,1)}, u32[]{:S(2)}, u32[]{:S(2)}) %collective-permute-start.1) | collective-permute-done | bytes 884768 | tf_op jit(solution)/shard_map/ppermute | solution.py:375
  36.7 17.7 %collective-permute-done.2.refs_3_.refs_11_ = bf16[6,96,768]{2,1,0:T(8,128)(2,1)} collective-permute-done((bf16[6,96,768]{2,1,0:T(8,128)(2,1)}, bf16[6,96,768]{2,1,0:T(8,128)(2,1)}, u32[]{:S(2)}, u32[]{:S(2)}) %collective-permute-start.2) | collective-permute-done | bytes 884768 | tf_op jit(solution)/shard_map/ppermute | solution.py:375
  55.2 3.2 %collective-permute-start.6 = (bf16[6,96,768]{2,1,0:T(8,128)(2,1)}, bf16[6,96,768]{2,1,0:T(8,128)(2,1)}, u32[]{:S(2)}, u32[]{:S(2)}) collective-permute-start(bf16[6,96,768]{2,1,0:T(8,128)(2,1)} %get-tuple-element.74), channel_id=1, source_target_pairs={{0,80},{16,96},{32,112},{48,0},{64,16},{80,32},{96,48},{112,64},{1... | collective-permute-start | bytes 2654216 | tf_op jit(solution)/shard_map/ppermute | solution.py:375
  59.6 2.3 copy-done.3
  61.9 5.2 %dft.1 = bf16[9216,128]{1,0:T(8,128)(2,1)S(1)} custom-call(f32[6]{0:T(128)S(1)} %pad_dynamic-slice_fusion.quad_ref, bf16[16,6,96,128]{3,2,1,0:T(8,128)(2,1)S(1)} %bitcast.10, bf16[1536,1536]{1,0:T(8,128)(2,1)S(1)} %copy-done.3), custom_call_target="tpu_custom_call" | custom-call | flops 1000000 | bytes 100000 | tf_op jit(solution)/shard_map/dft/pallas_call | solution.py:293
  68.5 10.9 %all-to-all-start.1 = ((bf16[128,72,128]{2,1,0:T(8,128)(2,1)}), bf16[128,72,128]{2,1,0:T(8,128)(2,1)S(1)}, u32[]{:S(2)}, u32[]{:S(2)}) async-start(bf16[128,72,128]{2,1,0:T(8,128)(2,1)} %bitcast.12), calls=%async_computation.1 | async-start | bytes 4718592 | tf_op jit(solution)/shard_map/all_to_all | solution.py:369
  79.5 16.2 %collective-permute-done.6.refs_6_.refs_14_ = bf16[6,96,768]{2,1,0:T(8,128)(2,1)} collective-permute-done((bf16[6,96,768]{2,1,0:T(8,128)(2,1)}, bf16[6,96,768]{2,1,0:T(8,128)(2,1)}, u32[]{:S(2)}, u32[]{:S(2)}) %collective-permute-start.6) | collective-permute-done | bytes 884768 | tf_op jit(solution)/shard_map/ppermute | solution.py:375
  96.8 22.1 %all-to-all-done.1 = bf16[128,72,128]{2,1,0:T(8,128)(2,1)S(1)} async-done(((bf16[128,72,128]{2,1,0:T(8,128)(2,1)}), bf16[128,72,128]{2,1,0:T(8,128)(2,1)S(1)}, u32[]{:S(2)}, u32[]{:S(2)}) %all-to-all-start.1) | async-done | bytes 2359328 | tf_op jit(solution)/shard_map/all_to_all | solution.py:369
  120.1 6.7 %legendre.1 = (bf16[1080,128]{1,0:T(8,128)(2,1)S(1)}, bf16[1080,128]{1,0:T(8,128)(2,1)S(1)}, bf16[1080,128]{1,0:T(8,128)(2,1)S(1)}, bf16[1080,128]{1,0:T(8,128)(...) custom-call(s32[8]{0:T(128)S(1)} %compare_select_fusion.2.src_ref, ...), custom_call_target="tpu_custom_call" | custom-call | flops 1811939328 | bytes 12000000 | tf_op jit(solution)/shard_map/legendre/pallas_call | solution.py:314
  132.9 2.1 collective-permute-start.14
  134.9 3.1 %collective-permute-done.7.refs_0_ = bf16[1080,128]{1,0:T(8,128)(2,1)S(1)} collective-permute-done((bf16[1080,128]{1,0:T(8,128)(2,1)S(1)}, bf16[1080,128]{1,0:T(8,128)(2,1)S(1)}, u32[]{:S(2)}, u32[]{:S(2)}) %collective-permute-start.7) | collective-permute-done | bytes 276512 | tf_op jit(solution)/shard_map/ppermute | solution.py:375
  138.1 2.7 %collective-permute-done.8.refs_1_ = bf16[1080,128]{1,0:T(8,128)(2,1)S(1)} collective-permute-done((bf16[1080,128]{1,0:T(8,128)(2,1)S(1)}, bf16[1080,128]{1,0:T(8,128)(2,1)S(1)}, u32[]{:S(2)}, u32[]{:S(2)}) %collective-permute-start.8) | collective-permute-done | bytes 276512 | tf_op jit(solution)/shard_map/ppermute | solution.py:375
  140.8 3.4 %collective-permute-start.16 = (bf16[1080,128]{1,0:T(8,128)(2,1)S(1)}, bf16[1080,128]{1,0:T(8,128)(2,1)S(1)}, u32[]{:S(2)}, u32[]{:S(2)}) collective-permute-start(bf16[1080,128]{1,0:T(8,128)(2,1)S(1)} %get-tuple-element.94), channel_id=1, source_target_pairs={{0,112},{16,0},{32,16},{48,32},{64,48},{80,64},{96,80},{112,96},{1... | collective-permute-start | bytes 829448 | tf_op jit(solution)/shard_map/ppermute | solution.py:375
  144.2 4.7 %collective-permute-done.9.refs_2_ = bf16[1080,128]{1,0:T(8,128)(2,1)S(1)} collective-permute-done((bf16[1080,128]{1,0:T(8,128)(2,1)S(1)}, bf16[1080,128]{1,0:T(8,128)(2,1)S(1)}, u32[]{:S(2)}, u32[]{:S(2)}) %collective-permute-start.9) | collective-permute-done | bytes 276512 | tf_op jit(solution)/shard_map/ppermute | solution.py:375
  148.9 2.7 %mix.2 = (bf16[1080,128]{1,0:T(8,128)(2,1)S(1)}, bf16[1080,128]{1,0:T(8,128)(2,1)S(1)}, bf16[1080,128]{1,0:T(8,128)(2,1)S(1)}) custom-call(bf16[1080,128]{1,0:T(8,128)(2,1)S(1)} %collective-permute-done.7.refs_0_, bf16[1080,128]{1,0:T(8,128)(2,1)S(1)} %collective-permute-done.8.refs_1_, bf16[1080,128]{1,0:T(8,128)(2,1)S(1)} %collective-permute-done.9.refs_2_, ...), custom_call_target="tpu_custom_call" | custom-call | flops 566231040 | bytes 10000000 | tf_op jit(solution)/shard_map/mix/pallas_call | solution.py:337
  155.8 3.0 %mix.3 = (bf16[1080,128]{1,0:T(8,128)(2,1)S(1)}, bf16[1080,128]{1,0:T(8,128)(2,1)S(1)}, bf16[1080,128]{1,0:T(8,128)(2,1)S(1)}, bf16[1080,128]{1,0:T(8,128)(2,1)S(1)}, bf16[1080,128]{1,0:T(8,128)(2,1)S(1)}) custom-call(bf16[1080,128]{1,0:T(8,128)(2,1)S(1)} %collective-permute-done.13.refs_0_, bf16[1080,128]{1,0:T(8,128)(2,1)S(1)} %collective-permute-done.14.refs_1_, ...), custom_call_target="tpu_custom_call" | custom-call | flops 566231040 | bytes 10000000 | tf_op jit(solution)/shard_map/mix/pallas_call | solution.py:337
  158.8 2.5 collective-permute-start.17
  163.4 3.1 %collective-permute-done.11.refs_1_ = bf16[1080,128]{1,0:T(8,128)(2,1)S(1)} collective-permute-done((bf16[1080,128]{1,0:T(8,128)(2,1)S(1)}, bf16[1080,128]{1,0:T(8,128)(2,1)S(1)}, u32[]{:S(2)}, u32[]{:S(2)}) %collective-permute-start.11) | collective-permute-done | bytes 276512 | tf_op jit(solution)/shard_map/ppermute | solution.py:375
  168.4 2.7 %collective-permute-done.12.refs_2_ = bf16[1080,128]{1,0:T(8,128)(2,1)S(1)} collective-permute-done((bf16[1080,128]{1,0:T(8,128)(2,1)S(1)}, bf16[1080,128]{1,0:T(8,128)(2,1)S(1)}, u32[]{:S(2)}, u32[]{:S(2)}) %collective-permute-start.12) | collective-permute-done | bytes 276512 | tf_op jit(solution)/shard_map/ppermute | solution.py:375
  171.2 3.3 %collective-permute-done.17.refs_3_ = bf16[1080,128]{1,0:T(8,128)(2,1)S(1)} collective-permute-done((bf16[1080,128]{1,0:T(8,128)(2,1)S(1)}, bf16[1080,128]{1,0:T(8,128)(2,1)S(1)}, u32[]{:S(2)}, u32[]{:S(2)}) %collective-permute-start.17) | collective-permute-done | bytes 276512 | tf_op jit(solution)/shard_map/ppermute | solution.py:375
  174.5 5.6 %collective-permute-done.18.refs_4_ = bf16[1080,128]{1,0:T(8,128)(2,1)S(1)} collective-permute-done((bf16[1080,128]{1,0:T(8,128)(2,1)S(1)}, bf16[1080,128]{1,0:T(8,128)(2,1)S(1)}, u32[]{:S(2)}, u32[]{:S(2)}) %collective-permute-start.18) | collective-permute-done | bytes 276512 | tf_op jit(solution)/shard_map/ppermute | solution.py:375
  180.2 6.6 %inverse_legendre.1 = bf16[9216,128]{1,0:T(8,128)(2,1)S(1)} custom-call(s32[8]{0:T(128)S(1)} %compare_select_fusion.2.src_ref, s32[8]{0:T(128)S(1)} %in_order.3.dest_ref, bf16[1080,128]{1,0:T(8,128)(2,1)S(1)} %collective-permute-done.10.refs_0_, bf16[1080,128]{1,0:T(8,128)(2,1)S(1)} %collective-permute-done.11.refs_1_, ...), custom_call_target="tpu_custom_call" | custom-call | flops 1811939328 | bytes 12000000 | tf_op jit(solution)/shard_map/inverse_legendre/pallas_call | solution.py:314
  186.8 36.7 %all_to_all.32 = bf16[128,72,128]{2,1,0:T(8,128)(2,1)S(1)} all-to-all(bf16[128,72,128]{2,1,0:T(8,128)(2,1)S(1)} %bitcast.11), channel_id=1, replica_groups=mesh['lat'=8,'lon'=16] {'lat','lon'}, dimensions={0} | all-to-all | bytes 4718592 | tf_op jit(solution)/shard_map/all_to_all | solution.py:369
  223.5 4.8 %inverse_dft.1 = bf16[16,6,96,128]{3,2,1,0:T(8,128)(2,1)S(1)} custom-call(bf16[9216,128]{1,0:T(8,128)(2,1)S(1)} %bitcast.13, bf16[1536,1536]{1,0:T(8,128)(2,1)S(1)} %bitcast.16), custom_call_target="tpu_custom_call" | custom-call | flops 3623878656 | bytes 10000000 | tf_op jit(solution)/shard_map/inverse_dft/pallas_call | solution.py:353
  228.3 34.6 %all_to_all.33 = bf16[96,96,128]{2,1,0:T(8,128)(2,1)S(1)} all-to-all(bf16[96,96,128]{2,1,0:T(8,128)(2,1)S(1)} %bitcast.14), channel_id=1, replica_groups=mesh['lat'=8,'lon'=16] {'lon'}, dimensions={0} | all-to-all | bytes 4718592 | tf_op jit(solution)/shard_map/all_to_all | solution.py:369
  (60 shorter events, 26.2 us)
Async XLA Ops:
  2.5 25.6 %collective-permute-start = (bf16[6,96,768]{2,1,0:T(8,128)(2,1)}, bf16[6,96,768]{2,1,0:T(8,128)(2,1)S(1)}, u32[]{:S(2)}, u32[]{:S(2)}) collective-permute-start(bf16[6,96,768]{2,1,0:T(8,128)(2,1)} %get-tuple-element.65), channel_id=1, source_target_pairs={{0,16},{16,32},{32,48},{48,64},{64,80},{80,96},{96,112},{112,0},{1... | collective-permute-start | bytes 2654216 | tf_op jit(solution)/shard_map/ppermute | solution.py:375
  2.5 34.2 %collective-permute-start.1 = (bf16[6,96,768]{2,1,0:T(8,128)(2,1)}, bf16[6,96,768]{2,1,0:T(8,128)(2,1)}, u32[]{:S(2)}, u32[]{:S(2)}) collective-permute-start(bf16[6,96,768]{2,1,0:T(8,128)(2,1)} %get-tuple-element.66), channel_id=1, source_target_pairs={{0,112},{16,0},{32,16},{48,32},{64,48},{80,64},{96,80},{112,96},{1... | collective-permute-start | bytes 2654216 | tf_op jit(solution)/shard_map/ppermute | solution.py:375
  8.0 7.3 %copy-start.6 = (bf16[90,90,128]{2,1,0:T(8,128)(2,1)S(1)}, bf16[90,90,128]{2,1,0:T(8,128)(2,1)}, u32[]{:S(2)}) copy-start(bf16[90,90,128]{2,1,0:T(8,128)(2,1)} %param.9) | copy-start | bytes 6220804
  10.2 26.5 %collective-permute-start.4 = (bf16[6,96,768]{2,1,0:T(8,128)(2,1)}, bf16[6,96,768]{2,1,0:T(8,128)(2,1)}, u32[]{:S(2)}, u32[]{:S(2)}) collective-permute-start(bf16[6,96,768]{2,1,0:T(8,128)(2,1)} %cut.6), channel_id=1, source_target_pairs={{0,64},{16,80},{32,96},{48,112},{64,0},{80,16},{96,32},{112,48},{1... | collective-permute-start | bytes 2654216 | tf_op jit(solution)/shard_map/ppermute | solution.py:375
  12.0 42.3 %collective-permute-start.2 = (bf16[6,96,768]{2,1,0:T(8,128)(2,1)}, bf16[6,96,768]{2,1,0:T(8,128)(2,1)}, u32[]{:S(2)}, u32[]{:S(2)}) collective-permute-start(bf16[6,96,768]{2,1,0:T(8,128)(2,1)} %get-tuple-element.67), channel_id=1, source_target_pairs={{0,32},{16,48},{32,64},{48,80},{64,96},{80,112},{96,0},{112,16},{1... | collective-permute-start | bytes 2654216 | tf_op jit(solution)/shard_map/ppermute | solution.py:375
  12.6 42.5 %collective-permute-start.3 = (bf16[6,96,768]{2,1,0:T(8,128)(2,1)}, bf16[6,96,768]{2,1,0:T(8,128)(2,1)}, u32[]{:S(2)}, u32[]{:S(2)}) collective-permute-start(bf16[6,96,768]{2,1,0:T(8,128)(2,1)} %get-tuple-element.68), channel_id=1, source_target_pairs={{0,96},{16,112},{32,0},{48,16},{64,32},{80,48},{96,64},{112,80},{1... | collective-permute-start | bytes 2654216 | tf_op jit(solution)/shard_map/ppermute | solution.py:375
  16.9 42.6 %all-to-all-start = ((bf16[96,96,128]{2,1,0:T(8,128)(2,1)}), bf16[96,96,128]{2,1,0:T(8,128)(2,1)S(1)}, u32[]{:S(2)}, u32[]{:S(2)}) async-start(bf16[96,96,128]{2,1,0:T(8,128)(2,1)} %pad.8), calls=%async_computation | async-start | bytes 4718592 | tf_op jit(solution)/shard_map/all_to_all | solution.py:369
  25.0 3.1 %copy-start.10 = (s32[8]{0:T(128)S(1)}, s32[8]{0:T(128)}, u32[]{:S(2)}) copy-start(s32[8]{0:T(128)} %constant.47) | copy-start | bytes 100
  25.0 3.1 %copy-start.9 = (s32[8]{0:T(128)S(1)}, s32[8]{0:T(128)}, u32[]{:S(2)}) copy-start(s32[8]{0:T(128)} %constant.35.clone) | copy-start | bytes 100
  55.2 24.3 %collective-permute-start.5 = (bf16[6,96,768]{2,1,0:T(8,128)(2,1)}, bf16[6,96,768]{2,1,0:T(8,128)(2,1)}, u32[]{:S(2)}, u32[]{:S(2)}) collective-permute-start(bf16[6,96,768]{2,1,0:T(8,128)(2,1)} %get-tuple-element.73), channel_id=1, source_target_pairs={{0,48},{16,64},{32,80},{48,96},{64,112},{80,0},{96,16},{112,32},{1... | collective-permute-start | bytes 2654216 | tf_op jit(solution)/shard_map/ppermute | solution.py:375
  55.2 40.5 %collective-permute-start.6 = (bf16[6,96,768]{2,1,0:T(8,128)(2,1)}, bf16[6,96,768]{2,1,0:T(8,128)(2,1)}, u32[]{:S(2)}, u32[]{:S(2)}) collective-permute-start(bf16[6,96,768]{2,1,0:T(8,128)(2,1)} %get-tuple-element.74), channel_id=1, source_target_pairs={{0,80},{16,96},{32,112},{48,0},{64,16},{80,32},{96,48},{112,64},{1... | collective-permute-start | bytes 2654216 | tf_op jit(solution)/shard_map/ppermute | solution.py:375
  68.5 50.4 %all-to-all-start.1 = ((bf16[128,72,128]{2,1,0:T(8,128)(2,1)}), bf16[128,72,128]{2,1,0:T(8,128)(2,1)S(1)}, u32[]{:S(2)}, u32[]{:S(2)}) async-start(bf16[128,72,128]{2,1,0:T(8,128)(2,1)} %bitcast.12), calls=%async_computation.1 | async-start | bytes 4718592 | tf_op jit(solution)/shard_map/all_to_all | solution.py:369
  120.1 28.8 %copy-start = (bf16[90,128,128]{2,1,0:T(8,128)(2,1)S(1)}, bf16[90,128,128]{2,1,0:T(8,128)(2,1)}, u32[]{:S(2)}) copy-start(bf16[90,128,128]{2,1,0:T(8,128)(2,1)} %refs_5_.1) | copy-start | bytes 8847364
  120.1 28.8 %copy-start.1 = (bf16[90,128,128]{2,1,0:T(8,128)(2,1)S(1)}, bf16[90,128,128]{2,1,0:T(8,128)(2,1)}, u32[]{:S(2)}) copy-start(bf16[90,128,128]{2,1,0:T(8,128)(2,1)} %refs_6_.1) | copy-start | bytes 8847364
  126.8 11.2 %collective-permute-start.7 = (bf16[1080,128]{1,0:T(8,128)(2,1)S(1)}, bf16[1080,128]{1,0:T(8,128)(2,1)S(1)}, u32[]{:S(2)}, u32[]{:S(2)}) collective-permute-start(bf16[1080,128]{1,0:T(8,128)(2,1)S(1)} %get-tuple-element.85), channel_id=1, source_target_pairs={{0,64},{16,80},{32,96},{48,112},{64,0},{80,16},{96,32},{112,48},{1... | collective-permute-start | bytes 829448 | tf_op jit(solution)/shard_map/ppermute | solution.py:375
  128.5 12.3 %collective-permute-start.8 = (bf16[1080,128]{1,0:T(8,128)(2,1)S(1)}, bf16[1080,128]{1,0:T(8,128)(2,1)S(1)}, u32[]{:S(2)}, u32[]{:S(2)}) collective-permute-start(bf16[1080,128]{1,0:T(8,128)(2,1)S(1)} %get-tuple-element.86), channel_id=1, source_target_pairs={{0,48},{16,64},{32,80},{48,96},{64,112},{80,0},{96,16},{112,32},{1... | collective-permute-start | bytes 829448 | tf_op jit(solution)/shard_map/ppermute | solution.py:375
  129.9 19.0 %collective-permute-start.9 = (bf16[1080,128]{1,0:T(8,128)(2,1)S(1)}, bf16[1080,128]{1,0:T(8,128)(2,1)S(1)}, u32[]{:S(2)}, u32[]{:S(2)}) collective-permute-start(bf16[1080,128]{1,0:T(8,128)(2,1)S(1)} %get-tuple-element.87), channel_id=1, source_target_pairs={{0,80},{16,96},{32,112},{48,0},{64,16},{80,32},{96,48},{112,64},{1... | collective-permute-start | bytes 829448 | tf_op jit(solution)/shard_map/ppermute | solution.py:375
  131.7 22.3 %collective-permute-start.13 = (bf16[1080,128]{1,0:T(8,128)(2,1)S(1)}, bf16[1080,128]{1,0:T(8,128)(2,1)S(1)}, u32[]{:S(2)}, u32[]{:S(2)}) collective-permute-start(bf16[1080,128]{1,0:T(8,128)(2,1)S(1)} %get-tuple-element.91), channel_id=1, source_target_pairs={{0,32},{16,48},{32,64},{48,80},{64,96},{80,112},{96,0},{112,16},{1... | collective-permute-start | bytes 829448 | tf_op jit(solution)/shard_map/ppermute | solution.py:375
  132.9 22.4 %collective-permute-start.14 = (bf16[1080,128]{1,0:T(8,128)(2,1)S(1)}, bf16[1080,128]{1,0:T(8,128)(2,1)S(1)}, u32[]{:S(2)}, u32[]{:S(2)}) collective-permute-start(bf16[1080,128]{1,0:T(8,128)(2,1)S(1)} %get-tuple-element.92), channel_id=1, source_target_pairs={{0,96},{16,112},{32,0},{48,16},{64,32},{80,48},{96,64},{112,80},{1... | collective-permute-start | bytes 829448 | tf_op jit(solution)/shard_map/ppermute | solution.py:375
  138.1 17.7 %collective-permute-start.15 = (bf16[1080,128]{1,0:T(8,128)(2,1)S(1)}, bf16[1080,128]{1,0:T(8,128)(2,1)S(1)}, u32[]{:S(2)}, u32[]{:S(2)}) collective-permute-start(bf16[1080,128]{1,0:T(8,128)(2,1)S(1)} %get-tuple-element.93), channel_id=1, source_target_pairs={{0,16},{16,32},{32,48},{48,64},{64,80},{80,96},{96,112},{112,0},{1... | collective-permute-start | bytes 829448 | tf_op jit(solution)/shard_map/ppermute | solution.py:375
  140.8 15.0 %collective-permute-start.16 = (bf16[1080,128]{1,0:T(8,128)(2,1)S(1)}, bf16[1080,128]{1,0:T(8,128)(2,1)S(1)}, u32[]{:S(2)}, u32[]{:S(2)}) collective-permute-start(bf16[1080,128]{1,0:T(8,128)(2,1)S(1)} %get-tuple-element.94), channel_id=1, source_target_pairs={{0,112},{16,0},{32,16},{48,32},{64,48},{80,64},{96,80},{112,96},{1... | collective-permute-start | bytes 829448 | tf_op jit(solution)/shard_map/ppermute | solution.py:375
  151.6 11.2 %collective-permute-start.10 = (bf16[1080,128]{1,0:T(8,128)(2,1)S(1)}, bf16[1080,128]{1,0:T(8,128)(2,1)S(1)}, u32[]{:S(2)}, u32[]{:S(2)}) collective-permute-start(bf16[1080,128]{1,0:T(8,128)(2,1)S(1)} %get-tuple-element.88), channel_id=1, source_target_pairs={{0,64},{16,80},{32,96},{48,112},{64,0},{80,16},{96,32},{112,48},{1... | collective-permute-start | bytes 829448 | tf_op jit(solution)/shard_map/ppermute | solution.py:375
  154.0 12.5 %collective-permute-start.11 = (bf16[1080,128]{1,0:T(8,128)(2,1)S(1)}, bf16[1080,128]{1,0:T(8,128)(2,1)S(1)}, u32[]{:S(2)}, u32[]{:S(2)}) collective-permute-start(bf16[1080,128]{1,0:T(8,128)(2,1)S(1)} %get-tuple-element.89), channel_id=1, source_target_pairs={{0,80},{16,96},{32,112},{48,0},{64,16},{80,32},{96,48},{112,64},{1... | collective-permute-start | bytes 829448 | tf_op jit(solution)/shard_map/ppermute | solution.py:375
  155.3 15.9 %collective-permute-start.12 = (bf16[1080,128]{1,0:T(8,128)(2,1)S(1)}, bf16[1080,128]{1,0:T(8,128)(2,1)S(1)}, u32[]{:S(2)}, u32[]{:S(2)}) collective-permute-start(bf16[1080,128]{1,0:T(8,128)(2,1)S(1)} %get-tuple-element.90), channel_id=1, source_target_pairs={{0,48},{16,64},{32,80},{48,96},{64,112},{80,0},{96,16},{112,32},{1... | collective-permute-start | bytes 829448 | tf_op jit(solution)/shard_map/ppermute | solution.py:375
  155.7 24.5 %copy-start.5 = (bf16[6,96,768]{2,1,0:T(8,128)(2,1)S(1)}, bf16[6,96,768]{2,1,0:T(8,128)(2,1)}, u32[]{:S(2)}) copy-start(bf16[6,96,768]{2,1,0:T(8,128)(2,1)} %get-tuple-element.77.refs_0_.refs_8_) | copy-start | bytes 2654212
  155.7 67.7 %slice-start = ((s8[4718592]{0:T(1024)(128)(4,1)}), s8[524288]{0:T(1024)(128)(4,1)S(1)}, s32[]{:S(2)}) async-start(s8[4718592]{0:T(1024)(128)(4,1)} %bitcast.15), calls=%async_computation.4 | async-start | bytes 1048576
  158.8 15.7 %collective-permute-start.17 = (bf16[1080,128]{1,0:T(8,128)(2,1)S(1)}, bf16[1080,128]{1,0:T(8,128)(2,1)S(1)}, u32[]{:S(2)}, u32[]{:S(2)}) collective-permute-start(bf16[1080,128]{1,0:T(8,128)(2,1)S(1)} %get-tuple-element.96), channel_id=1, source_target_pairs={{0,96},{16,112},{32,0},{48,16},{64,32},{80,48},{96,64},{112,80},{1... | collective-permute-start | bytes 829448 | tf_op jit(solution)/shard_map/ppermute | solution.py:375
  161.3 18.8 %collective-permute-start.18 = (bf16[1080,128]{1,0:T(8,128)(2,1)S(1)}, bf16[1080,128]{1,0:T(8,128)(2,1)S(1)}, u32[]{:S(2)}, u32[]{:S(2)}) collective-permute-start(bf16[1080,128]{1,0:T(8,128)(2,1)S(1)} %get-tuple-element.97), channel_id=1, source_target_pairs={{0,32},{16,48},{32,64},{48,80},{64,96},{80,112},{96,0},{112,16},{1... | collective-permute-start | bytes 829448 | tf_op jit(solution)/shard_map/ppermute | solution.py:375
  162.8 17.4 %collective-permute-start.19 = (bf16[1080,128]{1,0:T(8,128)(2,1)S(1)}, bf16[1080,128]{1,0:T(8,128)(2,1)S(1)}, u32[]{:S(2)}, u32[]{:S(2)}) collective-permute-start(bf16[1080,128]{1,0:T(8,128)(2,1)S(1)} %get-tuple-element.98), channel_id=1, source_target_pairs={{0,112},{16,0},{32,16},{48,32},{64,48},{80,64},{96,80},{112,96},{1... | collective-permute-start | bytes 829448 | tf_op jit(solution)/shard_map/ppermute | solution.py:375
  166.5 13.7 %collective-permute-start.20 = (bf16[1080,128]{1,0:T(8,128)(2,1)S(1)}, bf16[1080,128]{1,0:T(8,128)(2,1)S(1)}, u32[]{:S(2)}, u32[]{:S(2)}) collective-permute-start(bf16[1080,128]{1,0:T(8,128)(2,1)S(1)} %get-tuple-element.99), channel_id=1, source_target_pairs={{0,16},{16,32},{32,48},{48,64},{64,80},{80,96},{96,112},{112,0},{1... | collective-permute-start | bytes 829448 | tf_op jit(solution)/shard_map/ppermute | solution.py:375
  180.2 43.2 %slice-start.1 = ((s8[4718592]{0:T(1024)(128)(4,1)}), s8[4194304]{0:T(1024)(128)(4,1)S(1)}, s32[]{:S(2)}) async-start(s8[4718592]{0:T(1024)(128)(4,1)} %bitcast.15), calls=%async_computation.5 | async-start | bytes 8388608
  228.3 34.6 %copy-start.7 = (bf16[90,90,128]{2,1,0:T(8,128)(2,1)S(1)}, bf16[90,90,128]{2,1,0:T(8,128)(2,1)}, u32[]{:S(2)}) copy-start(bf16[90,90,128]{2,1,0:T(8,128)(2,1)} %param.9) | copy-start | bytes 6220804
  (4 other events, 8.0 us)
